TPU v7x, 32 devices: a whole 2x2x4 slice. The times are simulated.
32 devices in a mesh: seq: 8 (over y, x, core), fsdp: 4 (over z).
Axes of the slice: x: 2, y: 2, z: 4, core: 2. Of those that a mesh axis runs over, the one named last changes fastest.
Arguments:
- tokens: bfloat16 [8192, 1024], P(('seq', 'fsdp')), may hold values from -6 to 6
- lengths: int32 [8], replicated, may hold values from 1 to 1370, 8192 in all
- adapter_choice: int32 [8], replicated, may hold values from 0 to 7
- gain_rows: bfloat16 [4, 1024], P(None, ('seq', 'fsdp')), may hold values from 0.099609375 to 1.8984375
- bias_rows: bfloat16 [5, 1024], P(None, ('seq', 'fsdp')), may hold values from -1.796875 to 1.796875
- query_key_value: bfloat16 [1024, 3072], P(('seq', 'fsdp')), may hold values from -0.1875 to 0.1875
- output_weight: bfloat16 [1024, 1024], P(('seq', 'fsdp')), may hold values from -1 to 1
- expand_weight: bfloat16 [1024, 4096], P(('seq', 'fsdp')), may hold values from -0.1875 to 0.1875
- expand_bias: bfloat16 [4096], P(('seq', 'fsdp')), may hold values from -1.796875 to 1.796875
- contract_weight: bfloat16 [4096, 1024], P(('seq', 'fsdp')), may hold values from -0.09375 to 0.09375
- adapter_in_attention: bfloat16 [4, 1024, 128], P(None, ('seq', 'fsdp')), may hold values from -0.1875 to 0.1875
- adapter_out_attention: bfloat16 [4, 128, 1024], P(None, None, ('seq', 'fsdp')), may hold values from -1.5 to 1.5
- adapter_in_expand: bfloat16 [1024, 128], P(('seq', 'fsdp')), may hold values from -0.1875 to 0.1875
- adapter_out_expand: bfloat16 [128, 4096], P(None, ('seq', 'fsdp')), may hold values from -1.5 to 1.5
- adapter_in_contract: bfloat16 [4096, 128], P(('seq', 'fsdp')), may hold values from -0.09375 to 0.09375
- adapter_out_contract: bfloat16 [128, 1024], P(None, ('seq', 'fsdp')), may hold values from -1.5 to 1.5
- cotangent: bfloat16 [8192, 1024], P(('seq', 'fsdp')), may hold values from -6 to 6
Outputs:
- output: bfloat16 [8192, 1024], P(('seq', 'fsdp'))
- input_gradient: float32 [8192, 1024], P(('seq', 'fsdp'))
- adapter_in_attention_gradient: float32 [4, 1024, 128], P(None, ('seq', 'fsdp'))
- adapter_out_attention_gradient: float32 [4, 128, 1024], P(None, None, ('seq', 'fsdp'))
- adapter_in_expand_gradient: float32 [1024, 128], P(('seq', 'fsdp'))
- adapter_out_expand_gradient: float32 [128, 4096], P(None, ('seq', 'fsdp'))
- adapter_in_contract_gradient: float32 [4096, 128], P(('seq', 'fsdp'))
- adapter_out_contract_gradient: float32 [128, 1024], P(None, ('seq', 'fsdp'))
Inputs may be any that keep to these rules, and one draw needn't show every extreme that they name: Image lengths in the order of the tokens, summing to 8192; the longest is exactly 1370.
All inputs are finite; a program needn't handle non-finite values.
Results may differ from a plain program's by a relative error of at most 0.015.
The roundings to bfloat16 on the way count: a program that leaves them out, or rounds other values in their place, can miss the bound.
Values may be sent and summed in bfloat16 or wider, within the bound.
A program may use at most 256 MiB of HBM per device.

v0:
```python
import jax
import jax.numpy as jnp
from jax import lax
from jax.sharding import PartitionSpec as P

HEADS = 16
RANK = 16
HOPS = 6
EDGE = 1408


epsilon = 1e-06
float_type = jnp.float32
narrow_type = jnp.bfloat16


def passed_along(block, axis, distance):
    devices = range(lax.axis_size(axis))
    route = [(i - distance, i) for i in devices if i - distance in devices]
    return lax.ppermute(block, axis, route)


def layer_norm(inputs_row, gain_row, bias_row):
    center = inputs_row - jnp.mean(inputs_row, axis=-1, keepdims=True)
    scaling = lax.rsqrt(jnp.mean(center * center, axis=-1, keepdims=True) + epsilon)
    normal = center * scaling
    return (normal * gain_row + bias_row, normal, scaling)


def norm_backward(gradient, gain_row, normal, scaling):
    weighted = gradient * gain_row
    return scaling * (
        weighted
        - jnp.mean(weighted, axis=-1, keepdims=True)
        - normal * jnp.mean(weighted * normal, axis=-1, keepdims=True)
    )


def matmul(first_operand, second_operand):
    return jnp.dot(first_operand, second_operand, preferred_element_type=float_type)


def transposed_left(first_operand, second_operand):
    return lax.dot_general(
        first_operand, second_operand, (((0,), (0,)), ((), ())), preferred_element_type=float_type
    )


def transposed_right(first_operand, second_operand):
    return lax.dot_general(
        first_operand, second_operand, (((1,), (1,)), ((), ())), preferred_element_type=float_type
    )


def gelu_slope(hidden_pre):
    cumulative = 0.5 * (1.0 + lax.erf(hidden_pre * 0.7071067811865476))
    density = jnp.exp(-0.5 * hidden_pre * hidden_pre) * 0.3989422804014327
    return cumulative + hidden_pre * density


def per_device(
    tokens,
    lengths,
    adapter_choice,
    gain_rows,
    bias_rows,
    query_key_value,
    output_weight,
    expand_weight,
    expand_bias,
    contract_weight,
    adapter_in_attention,
    adapter_out_attention,
    adapter_in_expand,
    adapter_out_expand,
    adapter_in_contract,
    adapter_out_contract,
    cotangent,
):
    gathered = (
        lax.all_gather(gain_rows, ("seq", "fsdp"), axis=1, tiled=True),
        lax.all_gather(bias_rows, ("seq", "fsdp"), axis=1, tiled=True),
        lax.all_gather(query_key_value, ("seq", "fsdp"), axis=0, tiled=True),
        lax.all_gather(output_weight, ("seq", "fsdp"), axis=0, tiled=True),
        lax.all_gather(expand_weight, ("seq", "fsdp"), axis=0, tiled=True),
        lax.all_gather(expand_bias, ("seq", "fsdp"), axis=0, tiled=True),
        lax.all_gather(contract_weight, ("seq", "fsdp"), axis=0, tiled=True),
        lax.all_gather(adapter_in_attention, ("seq", "fsdp"), axis=1, tiled=True),
        lax.all_gather(adapter_out_attention, ("seq", "fsdp"), axis=2, tiled=True),
        lax.all_gather(adapter_in_expand, ("seq", "fsdp"), axis=0, tiled=True),
        lax.all_gather(adapter_out_expand, ("seq", "fsdp"), axis=1, tiled=True),
        lax.all_gather(adapter_in_contract, ("seq", "fsdp"), axis=0, tiled=True),
        lax.all_gather(adapter_out_contract, ("seq", "fsdp"), axis=1, tiled=True),
    )
    (
        gains_full,
        biases_full,
        qkv_full,
        output_full,
        expand_full,
        expand_bias_full,
        contract_full,
        attention_down,
        attention_up,
        expand_down,
        expand_up,
        contract_down,
        contract_up,
    ) = gathered
    gains_wide = gains_full.astype(float_type)
    biases_wide = biases_full.astype(float_type)
    row_count, features = tokens.shape
    device_count = lax.axis_size(("seq", "fsdp"))
    position = lax.axis_index(("seq", "fsdp"))
    head_width = features // HEADS
    pair_width = 2 * head_width
    pair_count = HEADS // 2
    scaling_score = head_width ** (-0.5)
    rank_width = attention_down.shape[2]
    window_start = HOPS * row_count - EDGE
    window_rows = row_count + 2 * EDGE
    image_ends = jnp.cumsum(lengths)
    places = (
        position * row_count
        - HOPS * row_count
        + jnp.arange((2 * HOPS + 1) * row_count, dtype=jnp.int32)
    )
    image_of = jnp.sum((places[:, None] >= image_ends[None, :]).astype(jnp.int32), axis=1)
    image_of = jnp.where((places >= 0) & (places < device_count * row_count), image_of, -1)
    own_image = image_of[HOPS * row_count : (HOPS + 1) * row_count]
    key_image = image_of[window_start : window_start + window_rows]
    allowed = own_image[:, None] == key_image[None, :]
    matches = own_image[:, None] == jnp.arange(lengths.shape[0], dtype=jnp.int32)[None, :]
    chosen = jnp.sum(jnp.where(matches, adapter_choice[None, :], 0), axis=1)
    select = (jnp.arange(rank_width, dtype=jnp.int32)[None, :] // RANK == chosen[:, None]).astype(
        float_type
    )
    residual = tokens.astype(float_type)
    normed_first, normal_first, scaling_first = layer_norm(residual, gains_wide[0], biases_wide[0])
    normed_first = normed_first.astype(narrow_type)
    rank_qkv = (
        jnp.einsum(
            "td,pdr->tpr", normed_first, attention_down[:3], preferred_element_type=float_type
        )
        * select[:, None, :]
    ).astype(narrow_type)
    adapted_qkv = jnp.einsum(
        "tpr,prd->tpd", rank_qkv, attention_up[:3], preferred_element_type=float_type
    ).reshape(row_count, 3 * features)
    query_bias = jnp.concatenate([biases_wide[1], jnp.zeros((2 * features,), float_type)])
    projected = (matmul(normed_first, qkv_full) + adapted_qkv + query_bias).astype(narrow_type)
    queries = projected[:, :features]
    key_values = projected[:, features:]
    from_lower = []
    from_higher = []
    for distance in range(1, HOPS + 1):
        from_lower.append(passed_along(key_values, ("seq", "fsdp"), distance))
        from_higher.append(passed_along(key_values, ("seq", "fsdp"), -distance))
    beside_all = jnp.concatenate(from_lower[::-1] + [key_values] + from_higher, axis=0)
    window = beside_all[window_start : window_start + window_rows]

    def pair_slices(pair_index):
        offset = pair_index * pair_width
        query_part = lax.dynamic_slice_in_dim(queries, offset, pair_width, 1).reshape(
            row_count, 2, head_width
        )
        key_part = lax.dynamic_slice_in_dim(window, offset, pair_width, 1).reshape(
            window_rows, 2, head_width
        )
        value_part = lax.dynamic_slice_in_dim(window, features + offset, pair_width, 1).reshape(
            window_rows, 2, head_width
        )
        scores = (
            jnp.einsum("qhd,khd->hqk", query_part, key_part, preferred_element_type=float_type)
            * scaling_score
        )
        scores = jnp.where(allowed[None], scores, -1e30)
        return (query_part, key_part, value_part, scores)

    def pair_forward(pair_index):
        query_part, key_part, value_part, scores = pair_slices(pair_index)
        highest = jnp.max(scores, axis=2, keepdims=True)
        weights = jnp.exp(scores - highest)
        denominator = jnp.sum(weights, axis=2, keepdims=True)
        soft = (weights / denominator).astype(narrow_type)
        mixed_part = jnp.einsum("hqk,khd->qhd", soft, value_part, preferred_element_type=float_type)
        return (
            mixed_part.reshape(row_count, pair_width),
            (highest + jnp.log(denominator))[:, :, 0],
        )

    attended_pairs, log_totals = lax.map(pair_forward, jnp.arange(pair_count))
    attended = attended_pairs.transpose(1, 0, 2).reshape(row_count, features).astype(narrow_type)
    rank_out = (matmul(attended, attention_down[3]) * select).astype(narrow_type)
    mixed = matmul(attended, output_full) + biases_wide[2] + matmul(rank_out, attention_up[3])
    middle = residual + gains_wide[1] * mixed
    normed_second, normal_second, scaling_second = layer_norm(middle, gains_wide[2], biases_wide[3])
    normed_second = normed_second.astype(narrow_type)
    rank_expand = (matmul(normed_second, expand_down) * select).astype(narrow_type)
    hidden_pre = (
        matmul(normed_second, expand_full)
        + expand_bias_full.astype(float_type)
        + matmul(rank_expand, expand_up)
    )
    active = jax.nn.gelu(hidden_pre, approximate=False).astype(narrow_type)
    rank_contract = (matmul(active, contract_down) * select).astype(narrow_type)
    branch = matmul(active, contract_full) + biases_wide[4] + matmul(rank_contract, contract_up)
    result = (middle + gains_wide[3] * branch).astype(narrow_type)
    renewed = lax.optimization_barrier(
        (
            gain_rows,
            bias_rows,
            query_key_value,
            output_weight,
            expand_weight,
            expand_bias,
            contract_weight,
            adapter_in_attention,
            adapter_out_attention,
            adapter_in_expand,
            adapter_out_expand,
            adapter_in_contract,
            adapter_out_contract,
            cotangent,
        )
    )
    gathered = (
        lax.all_gather(renewed[0], ("seq", "fsdp"), axis=1, tiled=True),
        lax.all_gather(renewed[1], ("seq", "fsdp"), axis=1, tiled=True),
        lax.all_gather(renewed[2], ("seq", "fsdp"), axis=0, tiled=True),
        lax.all_gather(renewed[3], ("seq", "fsdp"), axis=0, tiled=True),
        lax.all_gather(renewed[4], ("seq", "fsdp"), axis=0, tiled=True),
        lax.all_gather(renewed[5], ("seq", "fsdp"), axis=0, tiled=True),
        lax.all_gather(renewed[6], ("seq", "fsdp"), axis=0, tiled=True),
        lax.all_gather(renewed[7], ("seq", "fsdp"), axis=1, tiled=True),
        lax.all_gather(renewed[8], ("seq", "fsdp"), axis=2, tiled=True),
        lax.all_gather(renewed[9], ("seq", "fsdp"), axis=0, tiled=True),
        lax.all_gather(renewed[10], ("seq", "fsdp"), axis=1, tiled=True),
        lax.all_gather(renewed[11], ("seq", "fsdp"), axis=0, tiled=True),
        lax.all_gather(renewed[12], ("seq", "fsdp"), axis=1, tiled=True),
    )
    (
        gains_full,
        biases_full,
        qkv_full,
        output_full,
        expand_full,
        expand_bias_full,
        contract_full,
        attention_down,
        attention_up,
        expand_down,
        expand_up,
        contract_down,
        contract_up,
    ) = gathered
    gains_wide = gains_full.astype(float_type)
    gradient_out = cotangent.astype(float_type)
    grad_branch = (gains_wide[3] * gradient_out).astype(narrow_type)
    grad_rank_contract = (transposed_right(grad_branch, contract_up) * select).astype(narrow_type)
    grad_contract_down = transposed_left(active, grad_rank_contract)
    grad_contract_up = transposed_left(rank_contract, grad_branch)
    grad_active = transposed_right(grad_branch, contract_full) + transposed_right(
        grad_rank_contract, contract_down
    )
    grad_hidden = (grad_active * gelu_slope(hidden_pre)).astype(narrow_type)
    grad_rank_expand = (transposed_right(grad_hidden, expand_up) * select).astype(narrow_type)
    grad_expand_down = transposed_left(normed_second, grad_rank_expand)
    grad_expand_up = transposed_left(rank_expand, grad_hidden)
    grad_normed_second = transposed_right(grad_hidden, expand_full) + transposed_right(
        grad_rank_expand, expand_down
    )
    grad_middle = gradient_out + norm_backward(
        grad_normed_second, gains_wide[2], normal_second, scaling_second
    )
    grad_mixed = (gains_wide[1] * grad_middle).astype(narrow_type)
    grad_rank_out = (transposed_right(grad_mixed, attention_up[3]) * select).astype(narrow_type)
    grad_out_down = transposed_left(attended, grad_rank_out)
    grad_out_up = transposed_left(rank_out, grad_mixed)
    grad_attended = (
        transposed_right(grad_mixed, output_full)
        + transposed_right(grad_rank_out, attention_down[3])
    ).astype(narrow_type)

    def pair_backward(pair_index):
        query_part, key_part, value_part, scores = pair_slices(pair_index)
        grad_part = lax.dynamic_slice_in_dim(
            grad_attended, pair_index * pair_width, pair_width, 1
        ).reshape(row_count, 2, head_width)
        log_pair = log_totals[pair_index]
        probable = jnp.exp(scores - log_pair[:, :, None])
        grad_probable = jnp.einsum(
            "qhd,khd->hqk", grad_part, value_part, preferred_element_type=float_type
        )
        grad_scores = probable * (
            grad_probable - jnp.sum(grad_probable * probable, axis=2, keepdims=True)
        )
        grad_scores = grad_scores.astype(narrow_type)
        grad_query = (
            jnp.einsum("hqk,khd->qhd", grad_scores, key_part, preferred_element_type=float_type)
            * scaling_score
        )
        grad_key = (
            jnp.einsum("hqk,qhd->khd", grad_scores, query_part, preferred_element_type=float_type)
            * scaling_score
        )
        grad_value = jnp.einsum(
            "hqk,qhd->khd",
            probable.astype(narrow_type),
            grad_part,
            preferred_element_type=float_type,
        )
        return (
            grad_query.reshape(row_count, pair_width),
            grad_key.reshape(window_rows, pair_width),
            grad_value.reshape(window_rows, pair_width),
        )

    grad_query_pairs, grad_key_pairs, grad_value_pairs = lax.map(
        pair_backward, jnp.arange(pair_count)
    )
    grad_queries = grad_query_pairs.transpose(1, 0, 2).reshape(row_count, features)
    grad_keys = grad_key_pairs.transpose(1, 0, 2).reshape(window_rows, features)
    grad_values = grad_value_pairs.transpose(1, 0, 2).reshape(window_rows, features)
    grad_window = jnp.concatenate([grad_keys, grad_values], axis=1)
    padded_grads = jnp.pad(grad_window, ((window_start, window_start), (0, 0)))
    grad_pairs = padded_grads[HOPS * row_count : (HOPS + 1) * row_count]
    for distance in range(1, HOPS + 1):
        lower_piece = padded_grads[
            (HOPS - distance) * row_count : (HOPS - distance + 1) * row_count
        ]
        higher_piece = padded_grads[
            (HOPS + distance) * row_count : (HOPS + distance + 1) * row_count
        ]
        grad_pairs = grad_pairs + passed_along(
            lower_piece.astype(jnp.bfloat16), ("seq", "fsdp"), -distance
        ).astype(lower_piece.dtype)
        grad_pairs = grad_pairs + passed_along(
            higher_piece.astype(jnp.bfloat16), ("seq", "fsdp"), distance
        ).astype(higher_piece.dtype)
    grad_projected = jnp.concatenate([grad_queries, grad_pairs], axis=1).astype(narrow_type)
    grad_blocks = grad_projected.reshape(row_count, 3, features)
    grad_rank_qkv = (
        jnp.einsum("tpd,prd->tpr", grad_blocks, attention_up[:3], preferred_element_type=float_type)
        * select[:, None, :]
    ).astype(narrow_type)
    grad_qkv_down = jnp.einsum(
        "td,tpr->pdr", normed_first, grad_rank_qkv, preferred_element_type=float_type
    )
    grad_qkv_up = jnp.einsum(
        "tpr,tpd->prd", rank_qkv, grad_blocks, preferred_element_type=float_type
    )
    grad_normed_first = transposed_right(grad_projected, qkv_full) + jnp.einsum(
        "tpr,pdr->td", grad_rank_qkv, attention_down[:3], preferred_element_type=float_type
    )
    input_gradient = grad_middle + norm_backward(
        grad_normed_first, gains_wide[0], normal_first, scaling_first
    )
    grad_attention_down = jnp.concatenate([grad_qkv_down, grad_out_down[None]], axis=0)
    grad_attention_up = jnp.concatenate([grad_qkv_up, grad_out_up[None]], axis=0)
    summed = (
        lax.psum_scatter(grad_attention_down, ("seq", "fsdp"), scatter_dimension=1, tiled=True),
        lax.psum_scatter(grad_attention_up, ("seq", "fsdp"), scatter_dimension=2, tiled=True),
        lax.psum_scatter(grad_expand_down, ("seq", "fsdp"), scatter_dimension=0, tiled=True),
        lax.psum_scatter(grad_expand_up, ("seq", "fsdp"), scatter_dimension=1, tiled=True),
        lax.psum_scatter(grad_contract_down, ("seq", "fsdp"), scatter_dimension=0, tiled=True),
        lax.psum_scatter(grad_contract_up, ("seq", "fsdp"), scatter_dimension=1, tiled=True),
    )
    return (
        result,
        input_gradient,
        summed[0],
        summed[1],
        summed[2],
        summed[3],
        summed[4],
        summed[5],
    )


def solution(mesh):
    placed = (
        P(("seq", "fsdp"), None),
        P(),
        P(),
        P(None, ("seq", "fsdp")),
        P(None, ("seq", "fsdp")),
        P(("seq", "fsdp"), None),
        P(("seq", "fsdp"), None),
        P(("seq", "fsdp"), None),
        P(("seq", "fsdp")),
        P(("seq", "fsdp"), None),
        P(None, ("seq", "fsdp"), None),
        P(None, None, ("seq", "fsdp")),
        P(("seq", "fsdp"), None),
        P(None, ("seq", "fsdp")),
        P(("seq", "fsdp"), None),
        P(None, ("seq", "fsdp")),
        P(("seq", "fsdp"), None),
    )
    return jax.shard_map(
        per_device,
        mesh=mesh,
        in_specs=placed,
        out_specs=(
            P(("seq", "fsdp"), None),
            P(("seq", "fsdp"), None),
            P(None, ("seq", "fsdp"), None),
            P(None, None, ("seq", "fsdp")),
            P(("seq", "fsdp"), None),
            P(None, ("seq", "fsdp")),
            P(("seq", "fsdp"), None),
            P(None, ("seq", "fsdp")),
        ),
        check_vma=False,
    )
```

profile of v0, /device:TPU:0, one launch (start us, length us, event | category | flops | bytes accessed | tf_op | source)
XLA Modules:
  0.0 2266.3 jit_solution(13788401422368956888)
XLA Ops:
  20.4 70.4 %all-gather.1 = bf16[32,32,5]{1,2,0:T(8,128)(2,1)S(1)} all-gather(bf16[1,32,5]{1,2,0:T(8,128)(2,1)} %bitcast.283), channel_id=1, replica_groups=mesh['seq'=8,'fsdp'=4] {'seq','fsdp'}, dimensions={0}, use_global_device_ids=true | all-gather | bytes 10560 | tf_op jit(solution)/shard_map/all_gather | solution.py:82
  91.5 63.9 %all-gather = bf16[32,32,4]{1,2,0:T(4,128)(2,1)S(1)} all-gather(bf16[1,32,4]{1,2,0:T(4,128)(2,1)} %bitcast.280), channel_id=1, replica_groups=mesh['seq'=8,'fsdp'=4] {'seq','fsdp'}, dimensions={0}, use_global_device_ids=true | all-gather | bytes 8448 | tf_op jit(solution)/shard_map/all_gather | solution.py:81
  158.7 65.9 %all-gather.3 = bf16[32,32,4]{1,2,0:T(4,128)(2,1)S(1)} all-gather(bf16[1,32,4]{1,2,0:T(4,128)(2,1)} %bitcast.281), channel_id=1, replica_groups=mesh['seq'=8,'fsdp'=4] {'seq','fsdp'}, dimensions={0}, use_global_device_ids=true | all-gather | bytes 8448 | tf_op jit(solution)/shard_map/all_gather | solution.py:228
  231.6 3.7 copy.140
  235.4 5.8 fusion.28
  249.9 121.4 %all_gather.87 = bf16[128,1024]{0,1:T(8,128)(2,1)S(1)} all-gather(bf16[128,32]{0,1:T(8,128)(2,1)S(1)} %copy-done.31), channel_id=1, replica_groups=mesh['seq'=8,'fsdp'=4] {'seq','fsdp'}, dimensions={1}, use_global_device_ids=true | all-gather | bytes 270336 | tf_op jit(solution)/shard_map/all_gather | solution.py:240
  373.9 89.1 %all_gather.80 = bf16[1024,128]{1,0:T(8,128)(2,1)} all-gather(bf16[32,128]{1,0:T(8,128)(2,1)S(1)} %copy-done.30), channel_id=1, replica_groups=mesh['seq'=8,'fsdp'=4] {'seq','fsdp'}, dimensions={0}, use_global_device_ids=true | all-gather | bytes 270336 | tf_op jit(solution)/shard_map/all_gather | solution.py:90
  465.3 113.4 %all_gather.91 = bf16[1024,128]{1,0:T(8,128)(2,1)} all-gather(bf16[32,128]{1,0:T(8,128)(2,1)S(1)} %copy-done.30), channel_id=1, replica_groups=mesh['seq'=8,'fsdp'=4] {'seq','fsdp'}, dimensions={0}, use_global_device_ids=true | all-gather | bytes 270336 | tf_op jit(solution)/shard_map/all_gather | solution.py:237
  578.7 63.1 %all-gather.2 = bf16[32,1,128]{2,1,0:T(2,128)(2,1)S(1)} all-gather(bf16[1,1,128]{2,1,0:T(2,128)(2,1)S(1)} %bitcast.285), channel_id=1, replica_groups=mesh['seq'=8,'fsdp'=4] {'seq','fsdp'}, dimensions={0}, use_global_device_ids=true | all-gather | bytes 8448 | tf_op jit(solution)/shard_map/all_gather | solution.py:86
  648.5 4.2 collective-permute-start.5
  664.4 14.2 collective-permute-done.5
  680.1 14.7 collective-permute-done.6
  696.6 82.3 %collective-permute-done.7 = bf16[256,2048]{1,0:T(8,128)(2,1)S(1)} collective-permute-done((bf16[256,2048]{1,0:T(8,128)(2,1)}, bf16[256,2048]{1,0:T(8,128)(2,1)S(1)}, u32[]{:S(2)}, u32[]{:S(2)}) %collective-permute-start.7) | collective-permute-done | bytes 1048608 | tf_op jit(solution)/shard_map/ppermute | solution.py:20
  779.3 33.3 %collective-permute-done.11 = bf16[256,2048]{1,0:T(8,128)(2,1)S(1)} collective-permute-done((bf16[256,2048]{1,0:T(8,128)(2,1)}, bf16[256,2048]{1,0:T(8,128)(2,1)S(1)}, u32[]{:S(2)}, u32[]{:S(2)}) %collective-permute-start.11) | collective-permute-done | bytes 1048608 | tf_op jit(solution)/shard_map/ppermute | solution.py:20
  812.6 5.1 slice.187
  817.7 15.6 copy.141
  834.1 82.5 %while.32 = (s32[]{:T(128)}, bf16[8,256,128]{1,2,0:T(8,128)(2,1)}, f32[8,2,256]{2,1,0:T(2,128)S(1)}, s32[8]{0:T(128)S(1)}, bf16[3072,2048]{0,1:T(8,128)(2,1)}, /...) while((s32[]{:T(128)}, bf16[8,256,128]{1,2,0:T(8,128)(2,1)}, ...), condition=%wide.region_8.9_spmd.clone, body=%wide.region_5.8_spmd.clone.sunk | while | flops 422313472 | bytes 27161876 | solution.py:192
  922.1 7.7 fusion.80
  929.8 7.8 convolution_add_fusion.2
  937.6 12.6 fusion.15
  950.2 5.8 fusion.12
  956.1 7.4 fusion.95
  969.6 8.7 all-gather.45.cloned.1.call-done
  980.7 51.2 %all-gather.49.cloned.1.call-done = bf16[4,1024,128]{2,1,0:T(8,128)(2,1)} async-done(((bf16[4,32,128]{2,1,0:T(8,128)(2,1)}), bf16[4,1024,128]{2,1,0:T(8,128)(2,1)}) %all-gather.49.cloned.1.call-update) | async-done | bytes 1048592 | tf_op jit(solution)/shard_map/all_gather | solution.py:235
  1034.7 180.7 %while.33 = (s32[]{:T(128)}, bf16[8,256,128]{1,2,0:T(8,128)(2,1)}, f32[8,3072,128]{1,2,0:T(8,128)}, f32[8,3072,128]{1,2,0:T(8,128)}, s32[8]{0:T(128)S(1)}, /*ind...) while((s32[]{:T(128)}, bf16[8,256,128]{1,2,0:T(8,128)(2,1)}, ...), condition=%wide.region_15.16_spmd.clone, body=%wide.region_13.15_spmd.clone.sunk | while | flops 1022033408 | bytes 83451272 | solution.py:319
  1040.6 4.4 subtract_exponential_fusion.3
  1046.0 4.0 multiply_reduce_fusion.4
  1062.9 4.4 subtract_exponential_fusion.3
  1068.3 4.0 multiply_reduce_fusion.4
  1085.3 4.4 subtract_exponential_fusion.3
  1090.6 4.0 multiply_reduce_fusion.4
  1107.7 4.4 subtract_exponential_fusion.3
  1113.1 4.0 multiply_reduce_fusion.4
  1130.3 4.4 subtract_exponential_fusion.3
  1135.7 4.9 multiply_reduce_fusion.4
  1153.8 4.4 subtract_exponential_fusion.3
  1159.1 4.0 multiply_reduce_fusion.4
  1176.4 4.4 subtract_exponential_fusion.3
  1181.7 4.1 multiply_reduce_fusion.4
  1198.7 4.4 subtract_exponential_fusion.3
  1204.1 4.0 multiply_reduce_fusion.4
  1215.5 9.3 fusion.87
  1225.1 4.3 collective-permute-start.23
  1231.0 5.2 fusion.90
  1236.3 3.2 collective-permute-start.21
  1240.8 4.4 collective-permute-start.19
  1245.2 11.0 collective-permute-done.23
  1257.5 76.4 %collective-permute-done.22 = bf16[256,2048]{0,1:T(8,128)(2,1)S(1)} collective-permute-done((bf16[256,2048]{0,1:T(8,128)(2,1)S(1)}, bf16[256,2048]{0,1:T(8,128)(2,1)S(1)}, u32[]{:S(2)}, u32[]{:S(2)}) %collective-permute-start.22) | collective-permute-done | bytes 1048608 | tf_op jit(solution)/shard_map/ppermute | solution.py:20
  1333.9 19.4 collective-permute-start.17
  1357.4 7.6 collective-permute-start.13
  1365.0 12.2 collective-permute-done.17
  1379.9 19.7 collective-permute-done.16
  1399.7 90.3 %collective-permute-done.14 = bf16[256,2048]{0,1:T(8,128)(2,1)S(1)} collective-permute-done((bf16[256,2048]{0,1:T(8,128)(2,1)}, bf16[256,2048]{0,1:T(8,128)(2,1)S(1)}, u32[]{:S(2)}, u32[]{:S(2)}) %collective-permute-start.14) | collective-permute-done | bytes 1048608 | tf_op jit(solution)/shard_map/ppermute | solution.py:20
  1490.0 3.4 fusion.41
  1511.5 3.4 fusion.99
  1515.0 3.7 fusion.100
  1518.7 119.6 %all_gather.84 = bf16[128,1024]{0,1:T(8,128)(2,1)S(1)} all-gather(bf16[128,32]{0,1:T(8,128)(2,1)S(1)} %copy-done.32), channel_id=1, replica_groups=mesh['seq'=8,'fsdp'=4] {'seq','fsdp'}, dimensions={1}, use_global_device_ids=true | all-gather | bytes 270336 | tf_op jit(solution)/shard_map/all_gather | solution.py:93
  1638.3 6.5 convolution_add_fusion.10
  1647.3 5.4 fusion.88
  1654.1 59.5 %all-reduce.7.cloned.1.call-done = (f32[4,1024,128]{2,0,1:T(4,128)}, f32[4,128,1024]{1,0,2:T(4,128)}) async-done(((f32[4,1024,128]{2,0,1:T(4,128)}, f32[4,128,1024]{1,0,2:T(4,128)}), (f32[4,1024,128]{2,0,1:T(4,128)}, f32[4,128,1024]{1,0,2:T(4,128)})) %all-reduce.7.cloned.1.call-update) | async-done | bytes 4194320
  1716.6 133.1 %reduce-scatter.5.cloned.1.call-done = f32[32,128]{1,0:T(8,128)} async-done(((f32[1024,128]{1,0:T(8,128)}), f32[32,128]{1,0:T(8,128)}) %reduce-scatter.5.cloned.1.call-update) | async-done | bytes 16400 | tf_op jit(solution)/shard_map/reduce_scatter | solution.py:364
  1849.7 133.4 %reduce-scatter.11.cloned.1.call-done = f32[128,32]{0,1:T(8,128)} async-done(((f32[128,1024]{0,1:T(8,128)}), f32[128,32]{0,1:T(8,128)}) %reduce-scatter.11.cloned.1.call-update) | async-done | bytes 16400 | tf_op jit(solution)/shard_map/reduce_scatter | solution.py:367
  1983.1 136.8 %reduce-scatter.7.cloned.1.call-done = f32[128,128]{1,0:T(8,128)} async-done(((f32[128,4096]{1,0:T(8,128)}), f32[128,128]{1,0:T(8,128)}) %reduce-scatter.7.cloned.1.call-update) | async-done | bytes 65552 | tf_op jit(solution)/shard_map/reduce_scatter | solution.py:365
  2119.9 139.1 %reduce-scatter.9.cloned.1.call-done = f32[128,128]{1,0:T(8,128)} async-done(((f32[4096,128]{1,0:T(8,128)}), f32[128,128]{1,0:T(8,128)}) %reduce-scatter.9.cloned.1.call-update) | async-done | bytes 65552 | tf_op jit(solution)/shard_map/reduce_scatter | solution.py:366
  (501 shorter events, 283.5 us)
Async XLA Ops:
  7.2 218.3 %all-gather.23.cloned.1.call-start = ((), (), s32[]{:S(2)}) async-start(), calls=%async_computation.5 | async-start | bytes 1081344 | tf_op jit(solution)/shard_map/all_gather | solution.py:88
  7.9 219.4 %all-gather.25.cloned.1.call-start = ((), (), s32[]{:S(2)}) async-start(), calls=%async_computation.6 | async-start | bytes 1081344 | tf_op jit(solution)/shard_map/all_gather | solution.py:89
  9.4 226.0 %all-gather.21.cloned.1.call-start = ((), (), s32[]{:S(2)}) async-start(), calls=%async_computation.4 | async-start | bytes 6488064 | tf_op jit(solution)/shard_map/all_gather | solution.py:83
  10.1 634.5 %all-gather.47.cloned.1.call-start = ((), (), s32[]{:S(2)}) async-start(), calls=%async_computation.17 | async-start | bytes 1081344 | tf_op jit(solution)/shard_map/all_gather | solution.py:236
  11.6 906.6 %all-gather.27.cloned.1.call-start = ((), (), s32[]{:S(2)}) async-start(), calls=%async_computation.7 | async-start | bytes 2162688 | tf_op jit(solution)/shard_map/all_gather | solution.py:84
  12.2 909.9 %all-gather.37.cloned.1.call-start = ((), (), s32[]{:S(2)}) async-start(), calls=%async_computation.12 | async-start | bytes 8650752 | tf_op jit(solution)/shard_map/all_gather | solution.py:234
  12.7 917.1 %all-gather.29.cloned.1.call-start = ((), (), s32[]{:S(2)}) async-start(), calls=%async_computation.8 | async-start | bytes 8650752 | tf_op jit(solution)/shard_map/all_gather | solution.py:85
  13.5 924.2 %all-gather.31.cloned.1.call-start = ((), (), s32[]{:S(2)}) async-start(), calls=%async_computation.9 | async-start | bytes 1081344 | tf_op jit(solution)/shard_map/all_gather | solution.py:91
  14.2 936.0 %all-gather.39.cloned.1.call-start = ((), (), s32[]{:S(2)}) async-start(), calls=%async_computation.13 | async-start | bytes 1081344 | tf_op jit(solution)/shard_map/all_gather | solution.py:239
  15.0 941.1 %all-gather.41.cloned.1.call-start = ((), (), s32[]{:S(2)}) async-start(), calls=%async_computation.14 | async-start | bytes 8650752 | tf_op jit(solution)/shard_map/all_gather | solution.py:232
  15.6 947.9 %all-gather.43.cloned.1.call-start = ((), (), s32[]{:S(2)}) async-start(), calls=%async_computation.15 | async-start | bytes 1081344 | tf_op jit(solution)/shard_map/all_gather | solution.py:238
  16.3 962.0 %all-gather.45.cloned.1.call-start = ((), (), s32[]{:S(2)}) async-start(), calls=%async_computation.16 | async-start | bytes 2162688 | tf_op jit(solution)/shard_map/all_gather | solution.py:231
  16.9 1015.0 %all-gather.49.cloned.1.call-start = ((), (), s32[]{:S(2)}) async-start(), calls=%async_computation.18 | async-start | bytes 1081344 | tf_op jit(solution)/shard_map/all_gather | solution.py:235
  17.6 1490.0 %all-gather.35.cloned.1.call-start = ((), (), s32[]{:S(2)}) async-start(), calls=%async_computation.11 | async-start | bytes 1081344 | tf_op jit(solution)/shard_map/all_gather | solution.py:92
  18.2 1620.1 %all-gather.33.cloned.1.call-start = ((), (), s32[]{:S(2)}) async-start(), calls=%async_computation.10 | async-start | bytes 8650752 | tf_op jit(solution)/shard_map/all_gather | solution.py:87
  18.8 1628.5 %all-gather.51.cloned.1.call-start = ((), (), s32[]{:S(2)}) async-start(), calls=%async_computation.19 | async-start | bytes 6488064 | tf_op jit(solution)/shard_map/all_gather | solution.py:230
  19.4 1694.3 %all-reduce.7.cloned.1.call-start = ((), (), s32[]{:S(2)}) async-start(), calls=%async_computation.24 | async-start | bytes 8388608
  91.5 143.8 %copy-start.35 = (f32[1,1024]{1,0:T(1,128)}, f32[1,1024]{1,0:T(1,128)S(1)}, u32[]{:S(2)}) copy-start(f32[1,1024]{1,0:T(1,128)S(1)} %get-tuple-element.534) | copy-start | bytes 12292
  156.1 79.2 %copy-start.38 = (f32[1,1024]{1,0:T(1,128)}, f32[1,1024]{1,0:T(1,128)S(1)}, u32[]{:S(2)}) copy-start(f32[1,1024]{1,0:T(1,128)S(1)} %get-tuple-element.541) | copy-start | bytes 12292
  157.3 78.0 %copy-start.33 = (f32[256]{0:T(256)}, f32[256]{0:T(256)S(1)}, u32[]{:S(2)}) copy-start(f32[256]{0:T(256)S(1)} %broadcast_multiply_fusion.5) | copy-start | bytes 3076
  158.7 76.7 %copy-start.42 = (f32[256]{0:T(256)}, f32[256]{0:T(256)S(1)}, u32[]{:S(2)}) copy-start(f32[256]{0:T(256)S(1)} %add_rsqrt_fusion.1) | copy-start | bytes 3076
  235.3 138.2 %copy-start.9 = (bf16[256,1024]{1,0:T(8,128)(2,1)S(1)}, bf16[256,1024]{1,0:T(8,128)(2,1)}, u32[]{:S(2)}) copy-start(bf16[256,1024]{1,0:T(8,128)(2,1)} %param.37) | copy-start | bytes 1572868
  235.3 138.5 %copy-start.30 = (bf16[32,128]{1,0:T(8,128)(2,1)S(1)}, bf16[32,128]{1,0:T(8,128)(2,1)}, u32[]{:S(2)}) copy-start(bf16[32,128]{1,0:T(8,128)(2,1)} %param.33) | copy-start | bytes 24580
  241.2 337.5 %copy-start.46 = (bf16[128]{0:T(256)(128)(2,1)S(1)}, bf16[128]{0:T(256)(128)(2,1)}, u32[]{:S(2)}) copy-start(bf16[128]{0:T(256)(128)(2,1)} %param.29) | copy-start | bytes 772
  242.3 406.2 %collective-permute-start = (bf16[256,2048]{1,0:T(8,128)(2,1)}, bf16[256,2048]{1,0:T(8,128)(2,1)}, u32[]{:S(2)}, u32[]{:S(2)}) collective-permute-start(bf16[256,2048]{1,0:T(8,128)(2,1)} %slice.186), channel_id=1, source_target_pairs={{0,6},{1,7},{2,8},{3,9},{4,10},{5,11},{6,12},{7,13},{8,14},{9,15},... | collective-permute-start | bytes 3145736 | tf_op jit(solution)/shard_map/ppermute | solution.py:20
  244.7 409.3 %collective-permute-start.1 = (bf16[256,2048]{1,0:T(8,128)(2,1)}, bf16[256,2048]{1,0:T(8,128)(2,1)}, u32[]{:S(2)}, u32[]{:S(2)}) collective-permute-start(bf16[256,2048]{1,0:T(8,128)(2,1)} %slice.186), channel_id=1, source_target_pairs={{0,5},{1,6},{2,7},{3,8},{4,9},{5,10},{6,11},{7,12},{8,13},{9,14},{... | collective-permute-start | bytes 3145736 | tf_op jit(solution)/shard_map/ppermute | solution.py:20
  247.6 674.5 %copy-start.40 = (f32[1,1024]{1,0:T(1,128)}, f32[1,1024]{1,0:T(1,128)S(1)}, u32[]{:S(2)}) copy-start(f32[1,1024]{1,0:T(1,128)S(1)} %get-tuple-element.538) | copy-start | bytes 12292
  247.6 409.0 %collective-permute-start.2 = (bf16[256,2048]{1,0:T(8,128)(2,1)}, bf16[256,2048]{1,0:T(8,128)(2,1)}, u32[]{:S(2)}, u32[]{:S(2)}) collective-permute-start(bf16[256,2048]{1,0:T(8,128)(2,1)} %slice.186), channel_id=1, source_target_pairs={{0,4},{1,5},{2,6},{3,7},{4,8},{5,9},{6,10},{7,11},{8,12},{9,13},{1... | collective-permute-start | bytes 3145736 | tf_op jit(solution)/shard_map/ppermute | solution.py:20
  371.3 287.9 %collective-permute-start.3 = (bf16[256,2048]{1,0:T(8,128)(2,1)}, bf16[256,2048]{1,0:T(8,128)(2,1)}, u32[]{:S(2)}, u32[]{:S(2)}) collective-permute-start(bf16[256,2048]{1,0:T(8,128)(2,1)} %slice.186), channel_id=1, source_target_pairs={{0,3},{1,4},{2,5},{3,6},{4,7},{5,8},{6,9},{7,10},{8,11},{9,12},{10... | collective-permute-start | bytes 3145736 | tf_op jit(solution)/shard_map/ppermute | solution.py:20
  373.9 576.4 %copy-start.28 = (bf16[256,128]{1,0:T(8,128)(2,1)}, bf16[256,128]{1,0:T(8,128)(2,1)S(1)}, u32[]{:S(2)}) copy-start(bf16[256,128]{1,0:T(8,128)(2,1)S(1)} %fusion.61) | copy-start | bytes 196612
  463.0 198.8 %collective-permute-start.4 = (bf16[256,2048]{1,0:T(8,128)(2,1)}, bf16[256,2048]{1,0:T(8,128)(2,1)}, u32[]{:S(2)}, u32[]{:S(2)}) collective-permute-start(bf16[256,2048]{1,0:T(8,128)(2,1)} %slice.186), channel_id=1, source_target_pairs={{0,2},{1,3},{2,4},{3,5},{4,6},{5,7},{6,8},{7,9},{8,10},{9,11},{10,... | collective-permute-start | bytes 3145736 | tf_op jit(solution)/shard_map/ppermute | solution.py:20
  648.5 30.1 %collective-permute-start.5 = (bf16[256,2048]{1,0:T(8,128)(2,1)}, bf16[256,2048]{1,0:T(8,128)(2,1)S(1)}, u32[]{:S(2)}, u32[]{:S(2)}) collective-permute-start(bf16[256,2048]{1,0:T(8,128)(2,1)} %slice.186), channel_id=1, source_target_pairs={{0,1},{1,2},{2,3},{3,4},{4,5},{5,6},{6,7},{7,8},{8,9},{9,10},{10,1... | collective-permute-start | bytes 3145736 | tf_op jit(solution)/shard_map/ppermute | solution.py:20
  653.9 40.8 %collective-permute-start.6 = (bf16[256,2048]{1,0:T(8,128)(2,1)}, bf16[256,2048]{1,0:T(8,128)(2,1)S(1)}, u32[]{:S(2)}, u32[]{:S(2)}) collective-permute-start(bf16[256,2048]{1,0:T(8,128)(2,1)} %slice.186), channel_id=1, source_target_pairs={{1,0},{2,1},{3,2},{4,3},{5,4},{6,5},{7,6},{8,7},{9,8},{10,9},{11,1... | collective-permute-start | bytes 3145736 | tf_op jit(solution)/shard_map/ppermute | solution.py:20
  656.6 122.4 %collective-permute-start.7 = (bf16[256,2048]{1,0:T(8,128)(2,1)}, bf16[256,2048]{1,0:T(8,128)(2,1)S(1)}, u32[]{:S(2)}, u32[]{:S(2)}) collective-permute-start(bf16[256,2048]{1,0:T(8,128)(2,1)} %slice.186), channel_id=1, source_target_pairs={{2,0},{3,1},{4,2},{5,3},{6,4},{7,5},{8,6},{9,7},{10,8},{11,9},{12,... | collective-permute-start | bytes 3145736 | tf_op jit(solution)/shard_map/ppermute | solution.py:20
  659.2 119.9 %collective-permute-start.8 = (bf16[256,2048]{1,0:T(8,128)(2,1)}, bf16[256,2048]{1,0:T(8,128)(2,1)S(1)}, u32[]{:S(2)}, u32[]{:S(2)}) collective-permute-start(bf16[256,2048]{1,0:T(8,128)(2,1)} %slice.186), channel_id=1, source_target_pairs={{3,0},{4,1},{5,2},{6,3},{7,4},{8,5},{9,6},{10,7},{11,8},{12,9},{13... | collective-permute-start | bytes 3145736 | tf_op jit(solution)/shard_map/ppermute | solution.py:20
  661.8 117.3 %collective-permute-start.9 = (bf16[256,2048]{1,0:T(8,128)(2,1)}, bf16[256,2048]{1,0:T(8,128)(2,1)S(1)}, u32[]{:S(2)}, u32[]{:S(2)}) collective-permute-start(bf16[256,2048]{1,0:T(8,128)(2,1)} %slice.186), channel_id=1, source_target_pairs={{4,0},{5,1},{6,2},{7,3},{8,4},{9,5},{10,6},{11,7},{12,8},{13,9},{1... | collective-permute-start | bytes 3145736 | tf_op jit(solution)/shard_map/ppermute | solution.py:20
  678.6 100.6 %collective-permute-start.10 = (bf16[256,2048]{1,0:T(8,128)(2,1)}, bf16[256,2048]{1,0:T(8,128)(2,1)S(1)}, u32[]{:S(2)}, u32[]{:S(2)}) collective-permute-start(bf16[256,2048]{1,0:T(8,128)(2,1)} %slice.186), channel_id=1, source_target_pairs={{5,0},{6,1},{7,2},{8,3},{9,4},{10,5},{11,6},{12,7},{13,8},{14,9},{... | collective-permute-start | bytes 3145736 | tf_op jit(solution)/shard_map/ppermute | solution.py:20
  694.8 117.8 %collective-permute-start.11 = (bf16[256,2048]{1,0:T(8,128)(2,1)}, bf16[256,2048]{1,0:T(8,128)(2,1)S(1)}, u32[]{:S(2)}, u32[]{:S(2)}) collective-permute-start(bf16[256,2048]{1,0:T(8,128)(2,1)} %slice.186), channel_id=1, source_target_pairs={{6,0},{7,1},{8,2},{9,3},{10,4},{11,5},{12,6},{13,7},{14,8},{15,9},... | collective-permute-start | bytes 3145736 | tf_op jit(solution)/shard_map/ppermute | solution.py:20
  922.0 15.6 copy-start.24
  1225.1 31.1 %collective-permute-start.23 = (bf16[256,2048]{0,1:T(8,128)(2,1)S(1)}, bf16[256,2048]{0,1:T(8,128)(2,1)S(1)}, u32[]{:S(2)}, u32[]{:S(2)}) collective-permute-start(bf16[256,2048]{0,1:T(8,128)(2,1)S(1)} %get-tuple-element.529), channel_id=1, source_target_pairs={{0,6},{1,7},{2,8},{3,9},{4,10},{5,11},{6,12},{7,13},{8,14},{9,15},... | collective-permute-start | bytes 3145736 | tf_op jit(solution)/shard_map/ppermute | solution.py:20
  1229.4 260.6 %slice-start.2 = ((s8[12582912]{0:T(1024)(128)(4,1)}), s8[4194304]{0:T(1024)(128)(4,1)S(1)}, s32[]{:S(2)}) async-start(s8[12582912]{0:T(1024)(128)(4,1)} %bitcast.235), calls=%async_computation.27 | async-start | bytes 8388608
  1229.4 149.0 %copy-start.2 = (bf16[8,256,128]{1,2,0:T(8,128)(2,1)S(1)}, bf16[8,256,128]{1,2,0:T(8,128)(2,1)}, u32[]{:S(2)}) copy-start(bf16[8,256,128]{1,2,0:T(8,128)(2,1)} %get-tuple-element.236) | copy-start | bytes 1572868
  1229.4 149.4 %copy-start.27 = (bf16[256,128]{1,0:T(8,128)(2,1)S(1)}, bf16[256,128]{1,0:T(8,128)(2,1)}, u32[]{:S(2)}) copy-start(bf16[256,128]{1,0:T(8,128)(2,1)} %copy-done.26) | copy-start | bytes 196612
  1229.4 260.5 %slice-start.3 = ((s8[12582912]{0:T(1024)(128)(4,1)}), s8[4194304]{0:T(1024)(128)(4,1)S(1)}, s32[]{:S(2)}) async-start(s8[12582912]{0:T(1024)(128)(4,1)} %bitcast.235), calls=%async_computation.28 | async-start | bytes 8388608
  1229.5 260.5 %slice-start.4 = ((s8[12582912]{0:T(1024)(128)(4,1)}), s8[4194304]{0:T(1024)(128)(4,1)S(1)}, s32[]{:S(2)}) async-start(s8[12582912]{0:T(1024)(128)(4,1)} %bitcast.235), calls=%async_computation.29 | async-start | bytes 8388608
  1229.5 104.5 %collective-permute-start.22 = (bf16[256,2048]{0,1:T(8,128)(2,1)S(1)}, bf16[256,2048]{0,1:T(8,128)(2,1)S(1)}, u32[]{:S(2)}, u32[]{:S(2)}) collective-permute-start(bf16[256,2048]{0,1:T(8,128)(2,1)S(1)} %get-tuple-element.528), channel_id=1, source_target_pairs={{6,0},{7,1},{8,2},{9,3},{10,4},{11,5},{12,6},{13,7},{14,8},{15,9},... | collective-permute-start | bytes 3145736 | tf_op jit(solution)/shard_map/ppermute | solution.py:20
  1236.3 117.1 %collective-permute-start.21 = (bf16[256,2048]{0,1:T(8,128)(2,1)}, bf16[256,2048]{0,1:T(8,128)(2,1)S(1)}, u32[]{:S(2)}, u32[]{:S(2)}) collective-permute-start(bf16[256,2048]{0,1:T(8,128)(2,1)} %get-tuple-element.519), channel_id=1, source_target_pairs={{0,5},{1,6},{2,7},{3,8},{4,9},{5,10},{6,11},{7,12},{8,13},{9,14},{... | collective-permute-start | bytes 3145736 | tf_op jit(solution)/shard_map/ppermute | solution.py:20
  1239.5 115.2 %collective-permute-start.20 = (bf16[256,2048]{0,1:T(8,128)(2,1)}, bf16[256,2048]{0,1:T(8,128)(2,1)S(1)}, u32[]{:S(2)}, u32[]{:S(2)}) collective-permute-start(bf16[256,2048]{0,1:T(8,128)(2,1)} %get-tuple-element.520), channel_id=1, source_target_pairs={{5,0},{6,1},{7,2},{8,3},{9,4},{10,5},{11,6},{12,7},{13,8},{14,9},{... | collective-permute-start | bytes 3145736 | tf_op jit(solution)/shard_map/ppermute | solution.py:20
  1240.8 115.3 %collective-permute-start.19 = (bf16[256,2048]{0,1:T(8,128)(2,1)}, bf16[256,2048]{0,1:T(8,128)(2,1)S(1)}, u32[]{:S(2)}, u32[]{:S(2)}) collective-permute-start(bf16[256,2048]{0,1:T(8,128)(2,1)} %get-tuple-element.521), channel_id=1, source_target_pairs={{0,4},{1,5},{2,6},{3,7},{4,8},{5,9},{6,10},{7,11},{8,12},{9,13},{1... | collective-permute-start | bytes 3145736 | tf_op jit(solution)/shard_map/ppermute | solution.py:20
  1256.2 101.1 %collective-permute-start.18 = (bf16[256,2048]{0,1:T(8,128)(2,1)}, bf16[256,2048]{0,1:T(8,128)(2,1)S(1)}, u32[]{:S(2)}, u32[]{:S(2)}) collective-permute-start(bf16[256,2048]{0,1:T(8,128)(2,1)} %get-tuple-element.522), channel_id=1, source_target_pairs={{4,0},{5,1},{6,2},{7,3},{8,4},{9,5},{10,6},{11,7},{12,8},{13,9},{1... | collective-permute-start | bytes 3145736 | tf_op jit(solution)/shard_map/ppermute | solution.py:20
  1333.9 43.2 %collective-permute-start.17 = (bf16[256,2048]{0,1:T(8,128)(2,1)}, bf16[256,2048]{0,1:T(8,128)(2,1)S(1)}, u32[]{:S(2)}, u32[]{:S(2)}) collective-permute-start(bf16[256,2048]{0,1:T(8,128)(2,1)} %get-tuple-element.523), channel_id=1, source_target_pairs={{0,3},{1,4},{2,5},{3,6},{4,7},{5,8},{6,9},{7,10},{8,11},{9,12},{10... | collective-permute-start | bytes 3145736 | tf_op jit(solution)/shard_map/ppermute | solution.py:20
  1353.4 46.1 %collective-permute-start.16 = (bf16[256,2048]{0,1:T(8,128)(2,1)}, bf16[256,2048]{0,1:T(8,128)(2,1)S(1)}, u32[]{:S(2)}, u32[]{:S(2)}) collective-permute-start(bf16[256,2048]{0,1:T(8,128)(2,1)} %get-tuple-element.524), channel_id=1, source_target_pairs={{3,0},{4,1},{5,2},{6,3},{7,4},{8,5},{9,6},{10,7},{11,8},{12,9},{13... | collective-permute-start | bytes 3145736 | tf_op jit(solution)/shard_map/ppermute | solution.py:20
  1354.7 45.0 %collective-permute-start.15 = (bf16[256,2048]{0,1:T(8,128)(2,1)}, bf16[256,2048]{0,1:T(8,128)(2,1)S(1)}, u32[]{:S(2)}, u32[]{:S(2)}) collective-permute-start(bf16[256,2048]{0,1:T(8,128)(2,1)} %get-tuple-element.525), channel_id=1, source_target_pairs={{0,2},{1,3},{2,4},{3,5},{4,6},{5,7},{6,8},{7,9},{8,10},{9,11},{10,... | collective-permute-start | bytes 3145736 | tf_op jit(solution)/shard_map/ppermute | solution.py:20
  1356.1 133.9 %collective-permute-start.14 = (bf16[256,2048]{0,1:T(8,128)(2,1)}, bf16[256,2048]{0,1:T(8,128)(2,1)S(1)}, u32[]{:S(2)}, u32[]{:S(2)}) collective-permute-start(bf16[256,2048]{0,1:T(8,128)(2,1)} %get-tuple-element.526), channel_id=1, source_target_pairs={{2,0},{3,1},{4,2},{5,3},{6,4},{7,5},{8,6},{9,7},{10,8},{11,9},{12,... | collective-permute-start | bytes 3145736 | tf_op jit(solution)/shard_map/ppermute | solution.py:20
  1357.4 132.6 %collective-permute-start.13 = (bf16[256,2048]{0,1:T(8,128)(2,1)}, bf16[256,2048]{0,1:T(8,128)(2,1)S(1)}, u32[]{:S(2)}, u32[]{:S(2)}) collective-permute-start(bf16[256,2048]{0,1:T(8,128)(2,1)} %get-tuple-element.527), channel_id=1, source_target_pairs={{0,1},{1,2},{2,3},{3,4},{4,5},{5,6},{6,7},{7,8},{8,9},{9,10},{10,1... | collective-permute-start | bytes 3145736 | tf_op jit(solution)/shard_map/ppermute | solution.py:20
  1377.2 112.8 %collective-permute-start.12 = (bf16[256,2048]{0,1:T(8,128)(2,1)}, bf16[256,2048]{0,1:T(8,128)(2,1)S(1)}, u32[]{:S(2)}, u32[]{:S(2)}) collective-permute-start(bf16[256,2048]{0,1:T(8,128)(2,1)} %get-tuple-element.518), channel_id=1, source_target_pairs={{1,0},{2,1},{3,2},{4,3},{5,4},{6,5},{7,6},{8,7},{9,8},{10,9},{11,1... | collective-permute-start | bytes 3145736 | tf_op jit(solution)/shard_map/ppermute | solution.py:20
  1379.9 113.6 %copy-start.8 = (bf16[8,256,128]{1,2,0:T(8,128)(2,1)S(1)}, bf16[8,256,128]{1,2,0:T(8,128)(2,1)}, u32[]{:S(2)}) copy-start(bf16[8,256,128]{1,2,0:T(8,128)(2,1)} %get-tuple-element.248) | copy-start | bytes 1572868
  1379.9 114.6 %copy-start.12 = (bf16[4,128,1024]{1,0,2:T(4,128)(2,1)S(1)}, bf16[4,128,1024]{1,0,2:T(4,128)(2,1)}, u32[]{:S(2)}) copy-start(bf16[4,128,1024]{1,0,2:T(4,128)(2,1)} %all-gather.47.cloned.1.call-done) | copy-start | bytes 3145732
  1379.9 114.6 %copy-start.23 = (f32[256,128]{1,0:T(8,128)S(1)}, f32[256,128]{1,0:T(8,128)}, u32[]{:S(2)}) copy-start(f32[256,128]{1,0:T(8,128)} %copy-done.22) | copy-start | bytes 393220
  1506.3 343.4 %reduce-scatter.5.cloned.1.call-start = ((), (), s32[]{:S(2)}) async-start(), calls=%async_computation.20 | async-start | bytes 540672 | tf_op jit(solution)/shard_map/reduce_scatter | solution.py:364
  1507.6 475.5 %reduce-scatter.11.cloned.1.call-start = ((), (), s32[]{:S(2)}) async-start(), calls=%async_computation.23 | async-start | bytes 540672 | tf_op jit(solution)/shard_map/reduce_scatter | solution.py:367
  1511.4 608.5 %reduce-scatter.7.cloned.1.call-start = ((), (), s32[]{:S(2)}) async-start(), calls=%async_computation.21 | async-start | bytes 2162688 | tf_op jit(solution)/shard_map/reduce_scatter | solution.py:365
  1514.9 123.3 %copy-start.44 = (f32[1,1024]{1,0:T(1,128)S(1)}, f32[1,1024]{1,0:T(1,128)}, u32[]{:S(2)}) copy-start(f32[1,1024]{1,0:T(1,128)} %get-tuple-element.530) | copy-start | bytes 12292
  1514.9 744.1 %reduce-scatter.9.cloned.1.call-start = ((), (), s32[]{:S(2)}) async-start(), calls=%async_computation.22 | async-start | bytes 2162688 | tf_op jit(solution)/shard_map/reduce_scatter | solution.py:366
  (47 other events, 204.1 us)
Sparse Core Ops, SparseCore 0:
  10.9 54.5 all-gather.22
  69.0 53.4 all-gather.24
  125.4 68.4 all-gather.20
  197.3 93.7 all-gather.46
  293.8 56.0 all-gather.26
  352.7 98.3 all-gather.36
  454.0 112.8 all-gather.28
  569.8 47.7 all-gather.30
  620.5 66.8 all-gather.38
  690.2 158.3 all-gather.40
  851.4 67.9 all-gather.42
  922.2 56.0 all-gather.44
  981.2 50.5 all-gather.48
  1034.7 53.4 all-gather.34
  1091.0 76.3 all-gather.32
  1170.2 127.4 all-gather.50
  1506.4 207.1 all-reduce.6
  1716.3 133.3 reduce-scatter.4
  1852.6 130.4 reduce-scatter.10
  1985.8 134.0 reduce-scatter.6
  2122.8 136.1 reduce-scatter.8
where the time goes:
time: 2280 us; the launch traced here: 2270 us
  waiting for transfers between devices  1020 us (45%)
  blocking collectives  707 us (31%)
  matrix products  212 us (9%)
  local copies, waits for them, and re-layouts  149 us (7%)
  starting transfers between devices  72.9 us (3%)
  other arithmetic  60.9 us (3%)
  loops' own time  24.4 us (1%)
    ppermute x24, waiting for transfers between devices, passed_along(): return lax.ppermute(block, axis, route)  354 us
    reduce_scatter x1, waiting for transfers between devices, per_device(): lax.psum_scatter(grad_contract_down, ('seq', 'fsdp'), scatter_dimension=0...  139 us
    reduce_scatter x1, waiting for transfers between devices, per_device(): lax.psum_scatter(grad_expand_up, ('seq', 'fsdp'), scatter_dimension=1, ti...  137 us
    reduce_scatter x1, waiting for transfers between devices, per_device(): lax.psum_scatter(grad_contract_up, ('seq', 'fsdp'), scatter_dimension=1,...  133 us
    reduce_scatter x1, waiting for transfers between devices, per_device(): lax.psum_scatter(grad_expand_down, ('seq', 'fsdp'), scatter_dimension=0,...  133 us
    all_gather x1, blocking collectives, per_device(): lax.all_gather(renewed[12], ('seq', 'fsdp'), axis=1, tiled=True)  121 us
    all_gather x1, blocking collectives, per_device(): lax.all_gather(adapter_out_contract, ('seq', 'fsdp'), axis=1, tiled=True)  120 us
    all_gather x1, blocking collectives, per_device(): lax.all_gather(renewed[9], ('seq', 'fsdp'), axis=0, tiled=True)  113 us
  transfers between devices with their start and end apart: 45, of which 17 were waited for; matrix products, arithmetic and copies ran while one was open for 18% of the time, Pallas kernels for 0%

commit v1 on v0

--- a/solution.py
+++ b/solution.py
@@ -1,12 +1,16 @@
+import functools
 import jax
 import jax.numpy as jnp
 from jax import lax
+from jax.experimental import pallas as pl
+from jax.experimental.pallas import tpu as pltpu
 from jax.sharding import PartitionSpec as P
 
 HEADS = 16
 RANK = 16
 HOPS = 6
 EDGE = 1408
+LONGEST = 1370
 
 
 epsilon = 1e-06
@@ -58,7 +62,7 @@
     return cumulative + hidden_pre * density
 
 
-def per_device(
+def general_layer(
     tokens,
     lengths,
     adapter_choice,
@@ -378,7 +382,850 @@
     )
 
 
+MESH_ID = pl.DeviceIdType.MESH
+CORES, SIDE_X, SIDE_Y = 1, 2, 4
+ANYWHERE = pl.BlockSpec(memory_space=pl.ANY)
+IN_VMEM = pl.BlockSpec(memory_space=pltpu.VMEM)
+IN_SMEM = pl.BlockSpec(memory_space=pltpu.SMEM)
+
+
+def place_here():
+    return lax.axis_index("seq"), lax.axis_index("fsdp")
+
+
+def remote(source, target, send, receive, seq, fsdp):
+    return pltpu.make_async_remote_copy(
+        src_ref=source,
+        dst_ref=target,
+        send_sem=send,
+        recv_sem=receive,
+        device_id=(seq, fsdp),
+        device_id_type=MESH_ID,
+    )
+
+
+def greet(barrier, seq, fsdp):
+    pl.semaphore_signal(barrier, 1, device_id=(seq, fsdp), device_id_type=MESH_ID)
+
+
+def greet_neighbours(barrier, seq, fsdp, depth):
+    for bit in (CORES, SIDE_X, SIDE_Y):
+        greet(barrier, seq ^ bit, fsdp)
+    for step in range(1, depth):
+        greet(barrier, seq, lax.rem(fsdp + step, depth))
+
+
+def gather_kernel(count, chunks, depth, *refs):
+    shards, fulls, sems = refs[:count], refs[count : 2 * count], refs[2 * count :]
+    send, receive, local = sems
+    seq, fsdp = place_here()
+    me = seq * depth + fsdp
+    barrier = pltpu.get_barrier_semaphore()
+    greet_neighbours(barrier, seq, fsdp, depth)
+    own = [
+        pltpu.make_async_copy(shard, full.at[me], local.at[i])
+        for i, (shard, full) in enumerate(zip(shards, fulls))
+    ]
+    for copy in own:
+        copy.start()
+    pl.semaphore_wait(barrier, 3 + depth - 1)
+    issued = []
+
+    def go(source, target, index, seq_to, fsdp_to):
+        copy = remote(source, target, send.at[index], receive.at[index], seq_to, fsdp_to)
+        copy.start()
+        issued.append(copy)
+        return copy
+
+    def group(chunk, at_seq):
+        array, rows, columns, _ = chunk
+        return fulls[array].at[pl.ds(at_seq * depth, depth), rows, columns]
+
+    tick = [0]
+
+    def fresh():
+        tick[0] += 1
+        return tick[0] - 1
+
+    along_z = []
+    for array, rows, columns, _ in chunks:
+        waits = []
+        for step in range(1, depth):
+            waits.append(
+                go(
+                    shards[array].at[rows, columns],
+                    fulls[array].at[me, rows, columns],
+                    fresh(),
+                    seq,
+                    lax.rem(fsdp + step, depth),
+                )
+            )
+        along_z.append(waits)
+    for copy in own:
+        copy.wait()
+    second, third, last = [], [], []
+
+    def to_core(chunk, at_seq):
+        piece = group(chunk, at_seq)
+        last.append(go(piece, piece, fresh(), seq ^ CORES, fsdp))
+
+    for turn in range(len(chunks) + 2):
+        if turn < len(chunks):
+            chunk = chunks[turn]
+            first_side = SIDE_X if chunk[3] else SIDE_Y
+            for copy in along_z[turn]:
+                copy.wait_recv()
+            piece = group(chunk, seq)
+            second.append(go(piece, piece, fresh(), seq ^ first_side, fsdp))
+            to_core(chunk, seq)
+        if 0 <= turn - 1 < len(chunks):
+            chunk = chunks[turn - 1]
+            first_side, other = (SIDE_X, SIDE_Y) if chunk[3] else (SIDE_Y, SIDE_X)
+            mine = group(chunk, seq)
+            third.append([go(mine, mine, fresh(), seq ^ other, fsdp)])
+            second[turn - 1].wait_recv()
+            piece = group(chunk, seq ^ first_side)
+            third[-1].append(go(piece, piece, fresh(), seq ^ other, fsdp))
+            to_core(chunk, seq ^ first_side)
+        if 0 <= turn - 2 < len(chunks):
+            chunk = chunks[turn - 2]
+            first_side, other = (SIDE_X, SIDE_Y) if chunk[3] else (SIDE_Y, SIDE_X)
+            for copy, at_seq in zip(third[turn - 2], (seq ^ other, seq ^ other ^ first_side)):
+                copy.wait_recv()
+                to_core(chunk, at_seq)
+    for copy in last:
+        copy.wait_recv()
+    for copy in issued:
+        copy.wait_send()
+
+
+def gather_everything(shards, chunks, devices, depth, collective):
+    copies = len(chunks) * ((depth - 1) + 1 + 2 + 4)
+    return pl.pallas_call(
+        functools.partial(gather_kernel, len(shards), chunks, depth),
+        out_shape=tuple(jax.ShapeDtypeStruct((devices,) + a.shape, a.dtype) for a in shards),
+        in_specs=[ANYWHERE] * len(shards),
+        out_specs=tuple([ANYWHERE] * len(shards)),
+        scratch_shapes=[
+            pltpu.SemaphoreType.DMA((copies,)),
+            pltpu.SemaphoreType.DMA((copies,)),
+            pltpu.SemaphoreType.DMA((len(shards),)),
+        ],
+        compiler_params=pltpu.CompilerParams(collective_id=collective, has_side_effects=True),
+    )(*shards)
+
+
+def holder_of(head, core, depth):
+    return lax.div(head, depth) * 2 + core, lax.rem(head, depth)
+
+
+def to_heads_kernel(heads, depth, halo, x_ref, y_ref, send, receive, local):
+    seq, fsdp = place_here()
+    me = seq * depth + fsdp
+    core, half = lax.rem(seq, 2), lax.div(seq, 4)
+    head = lax.div(seq, 2) * depth + fsdp
+    own = heads
+    base = core * (own - halo)
+    barrier = pltpu.get_barrier_semaphore()
+
+    @pl.loop(0, heads)
+    def _(k):
+        source = core * own + k
+
+        @pl.when(source != me)
+        def _():
+            greet(barrier, lax.div(source, depth), lax.rem(source, depth))
+
+    if halo:
+        greet(barrier, seq ^ CORES, fsdp)
+
+    @pl.when(half == core)
+    def _():
+        pltpu.make_async_copy(x_ref.at[:, head], y_ref.at[me - base], local).start()
+
+    pl.semaphore_wait(barrier, heads - (half == core).astype(jnp.int32) + (1 if halo else 0))
+    target_slot = me - half * (own - halo)
+
+    def piece(k):
+        seq_to, fsdp_to = holder_of(k, half, depth)
+        return remote(
+            x_ref.at[:, k], y_ref.at[target_slot], send.at[k], receive.at[lax.rem(me, own)], seq_to, fsdp_to
+        )
+
+    @pl.loop(0, heads)
+    def _(step):
+        k = lax.rem(step + head, heads)
+
+        @pl.when((k != head) | (half != core))
+        def _():
+            piece(k).start()
+
+    @pl.loop(0, heads)
+    def _(k):
+        source = core * own + k
+
+        @pl.when(source != me)
+        def _():
+            remote(
+                x_ref.at[:, k], y_ref.at[source - base], send.at[k], receive.at[k], seq ^ CORES, fsdp
+            ).wait_recv()
+
+    @pl.when(half == core)
+    def _():
+        pltpu.make_async_copy(x_ref.at[:, head], y_ref.at[me - base], local).wait()
+
+    if halo:
+        here = (own - halo) - base
+        there = (own - halo) + halo - base - (own - halo)
+        first = jnp.where(core == 0, own - halo, own)
+        source_slot = first - base
+        other_slot = first - (own - halo) * (1 - core)
+        over = remote(
+            y_ref.at[pl.ds(source_slot, halo), 1:3],
+            y_ref.at[pl.ds(other_slot, halo), 1:3],
+            send.at[heads],
+            receive.at[heads],
+            seq ^ CORES,
+            fsdp,
+        )
+        over.start()
+        over.wait()
+
+    @pl.loop(0, heads)
+    def _(k):
+        @pl.when((k != head) | (half != core))
+        def _():
+            piece(k).wait_send()
+
+
+def to_heads(x, halo, depth, collective):
+    parts, heads, width, rows = x.shape
+    return pl.pallas_call(
+        functools.partial(to_heads_kernel, heads, depth, halo),
+        out_shape=jax.ShapeDtypeStruct((heads + halo, parts, width, rows), x.dtype),
+        in_specs=[ANYWHERE],
+        out_specs=ANYWHERE,
+        scratch_shapes=[
+            pltpu.SemaphoreType.DMA((heads + 1,)),
+            pltpu.SemaphoreType.DMA((heads + 1,)),
+            pltpu.SemaphoreType.DMA,
+        ],
+        compiler_params=pltpu.CompilerParams(collective_id=collective, has_side_effects=True),
+    )(x)
+
+
+def to_rows_kernel(heads, depth, x_ref, y_ref, send, receive, local):
+    seq, fsdp = place_here()
+    me = seq * depth + fsdp
+    core, half = lax.rem(seq, 2), lax.div(seq, 4)
+    head = lax.div(seq, 2) * depth + fsdp
+    own = heads
+    barrier = pltpu.get_barrier_semaphore()
+
+    @pl.loop(0, heads)
+    def _(k):
+        seq_to, fsdp_to = holder_of(k, half, depth)
+
+        @pl.when((k != head) | (half != core))
+        def _():
+            greet(barrier, seq_to, fsdp_to)
+
+    @pl.when(half == core)
+    def _():
+        pltpu.make_async_copy(x_ref.at[me - core * own], y_ref.at[:, head], local).start()
+
+    pl.semaphore_wait(barrier, heads - (half == core).astype(jnp.int32))
+
+    def piece(k):
+        target = core * own + k
+        return remote(
+            x_ref.at[k],
+            y_ref.at[:, head],
+            send.at[k],
+            receive.at[head],
+            lax.div(target, depth),
+            lax.rem(target, depth),
+        )
+
+    @pl.loop(0, heads)
+    def _(step):
+        k = lax.rem(step + me, heads)
+
+        @pl.when(core * own + k != me)
+        def _():
+            piece(k).start()
+
+    @pl.loop(0, heads)
+    def _(k):
+        @pl.when((k != head) | (half != core))
+        def _():
+            remote(x_ref.at[0], y_ref.at[:, k], send.at[k], receive.at[k], seq ^ CORES, fsdp).wait_recv()
+
+    @pl.when(half == core)
+    def _():
+        pltpu.make_async_copy(x_ref.at[me - core * own], y_ref.at[:, head], local).wait()
+
+    @pl.loop(0, heads)
+    def _(k):
+        @pl.when(core * own + k != me)
+        def _():
+            piece(k).wait_send()
+
+
+def to_rows(x, depth, collective):
+    heads, parts, width, rows = x.shape
+    return pl.pallas_call(
+        functools.partial(to_rows_kernel, heads, depth),
+        out_shape=jax.ShapeDtypeStruct((parts, heads, width, rows), x.dtype),
+        in_specs=[ANYWHERE],
+        out_specs=ANYWHERE,
+        scratch_shapes=[
+            pltpu.SemaphoreType.DMA((heads,)),
+            pltpu.SemaphoreType.DMA((heads,)),
+            pltpu.SemaphoreType.DMA,
+        ],
+        compiler_params=pltpu.CompilerParams(collective_id=collective, has_side_effects=True),
+    )(x)
+
+
+def to_rows_merged_kernel(heads, depth, halo, x_ref, h_ref, y_ref, merged, other, send, receive, local):
+    seq, fsdp = place_here()
+    me = seq * depth + fsdp
+    core, half = lax.rem(seq, 2), lax.div(seq, 4)
+    head = lax.div(seq, 2) * depth + fsdp
+    own = heads
+    barrier = pltpu.get_barrier_semaphore()
+    greet(barrier, seq ^ CORES, fsdp)
+
+    @pl.loop(0, heads)
+    def _(k):
+        seq_to, fsdp_to = holder_of(k, half, depth)
+
+        @pl.when((k != head) | (half != core))
+        def _():
+            greet(barrier, seq_to, fsdp_to)
+
+    pl.semaphore_wait(barrier, heads + 1 - (half == core).astype(jnp.int32))
+    over = remote(h_ref, other, send.at[heads], receive.at[heads], seq ^ CORES, fsdp)
+    over.start()
+
+    def piece(k):
+        target = core * own + k
+        return remote(
+            merged.at[k],
+            y_ref.at[:, head],
+            send.at[k],
+            receive.at[head],
+            lax.div(target, depth),
+            lax.rem(target, depth),
+        )
+
+    def launch(k):
+        @pl.when(core * own + k != me)
+        def _():
+            piece(k).start()
+
+        @pl.when(core * own + k == me)
+        def _():
+            pltpu.make_async_copy(merged.at[k], y_ref.at[:, head], local).start()
+
+    shared = jnp.where(core == 0, own - halo, 0)
+    alone = jnp.where(core == 0, 0, halo)
+
+    @pl.loop(0, own - halo)
+    def _(step):
+        k = alone + lax.rem(step + me, own - halo)
+        merged[k] = x_ref[k]
+        launch(k)
+
+    over.wait_recv()
+
+    @pl.loop(0, halo)
+    def _(step):
+        k = shared + step
+        merged[k, 0] = x_ref[k, 0]
+        for part in range(2):
+            merged[k, 1 + part] = (
+                x_ref[k, 1 + part].astype(float_type) + other[step, part].astype(float_type)
+            ).astype(narrow_type)
+        launch(k)
+
+    @pl.loop(0, heads)
+    def _(k):
+        @pl.when((k != head) | (half != core))
+        def _():
+            remote(merged.at[0], y_ref.at[:, k], send.at[k], receive.at[k], seq ^ CORES, fsdp).wait_recv()
+
+    @pl.when(half == core)
+    def _():
+        pltpu.make_async_copy(merged.at[0], y_ref.at[:, head], local).wait()
+
+    @pl.loop(0, heads)
+    def _(k):
+        @pl.when(core * own + k != me)
+        def _():
+            piece(k).wait_send()
+
+    over.wait_send()
+
+
+def to_rows_merged(x, h, depth, collective):
+    heads, parts, width, rows = x.shape
+    return pl.pallas_call(
+        functools.partial(to_rows_merged_kernel, heads, depth, h.shape[0]),
+        out_shape=jax.ShapeDtypeStruct((parts, heads, width, rows), x.dtype),
+        in_specs=[IN_VMEM, IN_VMEM],
+        out_specs=ANYWHERE,
+        scratch_shapes=[
+            pltpu.VMEM(x.shape, x.dtype),
+            pltpu.VMEM(h.shape, h.dtype),
+            pltpu.SemaphoreType.DMA((heads + 1,)),
+            pltpu.SemaphoreType.DMA((heads + 1,)),
+            pltpu.SemaphoreType.DMA,
+        ],
+        compiler_params=pltpu.CompilerParams(
+            collective_id=collective, has_side_effects=True, vmem_limit_bytes=24 << 20
+        ),
+    )(x, h)
+
+
+def reduce_kernel(depth, g_ref, out_ref, first, second, third, fourth, send, receive):
+    seq, fsdp = place_here()
+    core, x, y = lax.rem(seq, 2), lax.rem(lax.div(seq, 2), 2), lax.div(seq, 4)
+    barrier = pltpu.get_barrier_semaphore()
+    greet_neighbours(barrier, seq, fsdp, depth)
+    pl.semaphore_wait(barrier, 3 + depth - 1)
+    rows = g_ref.shape[2]
+    half = rows // 2
+    halves = (pl.ds(0, half), pl.ds(half, half))
+    tick = [0]
+    issued = []
+
+    def go(source, target, seq_to, fsdp_to):
+        index = tick[0]
+        tick[0] += 1
+        copy = remote(source, target, send.at[index], receive.at[index], seq_to, fsdp_to)
+        copy.start()
+        issued.append(copy)
+        return copy
+
+    def add_into(target, other):
+        @pl.loop(0, depth)
+        def _(i):
+            target[i] = (target[i].astype(float_type) + other[i].astype(float_type)).astype(narrow_type)
+
+    copies = [go(g_ref.at[2 * t + 1 - core], first.at[t], seq ^ CORES, fsdp) for t in range(4)]
+    for t in range(4):
+        copies[t].wait_recv()
+        add_into(first.at[t], g_ref.at[2 * t + core])
+    over = [
+        [go(first.at[2 * j + 1 - x, :, halves[0]], second.at[0, j], seq ^ SIDE_X, fsdp) for j in range(2)],
+        [go(first.at[2 * (1 - y) + j, :, halves[1]], second.at[1, j], seq ^ SIDE_Y, fsdp) for j in range(2)],
+    ]
+    for j in range(2):
+        over[0][j].wait_recv()
+        add_into(second.at[0, j], first.at[2 * j + x, :, halves[0]])
+        over[1][j].wait_recv()
+        add_into(second.at[1, j], first.at[2 * y + j, :, halves[1]])
+    last = [
+        go(second.at[0, 1 - y], third.at[0], seq ^ SIDE_Y, fsdp),
+        go(second.at[1, 1 - x], third.at[1], seq ^ SIDE_X, fsdp),
+    ]
+    last[0].wait_recv()
+    add_into(third.at[0], second.at[0, y])
+    last[1].wait_recv()
+    add_into(third.at[1], second.at[1, x])
+    finals = []
+    for step in range(1, depth):
+        to = lax.rem(fsdp + step, depth)
+        for j in range(2):
+            finals.append(go(third.at[j, to], fourth.at[j, step], seq, to))
+    for copy in finals:
+        copy.wait_recv()
+    for j in range(2):
+        total = third[j, fsdp].astype(float_type)
+        for step in range(1, depth):
+            total = total + fourth[j, step].astype(float_type)
+        out_ref[halves[j]] = total
+    for copy in issued:
+        copy.wait_send()
+
+
+def reduce_shards(g, depth, collective):
+    seqs, _, rows, lanes = g.shape
+    half = rows // 2
+    copies = 4 + 4 + 2 + 2 * (depth - 1)
+    return pl.pallas_call(
+        functools.partial(reduce_kernel, depth),
+        out_shape=jax.ShapeDtypeStruct((rows, lanes), float_type),
+        in_specs=[IN_VMEM],
+        out_specs=IN_VMEM,
+        scratch_shapes=[
+            pltpu.VMEM((4, depth, rows, lanes), g.dtype),
+            pltpu.VMEM((2, 2, depth, half, lanes), g.dtype),
+            pltpu.VMEM((2, depth, half, lanes), g.dtype),
+            pltpu.VMEM((2, depth, half, lanes), g.dtype),
+            pltpu.SemaphoreType.DMA((copies,)),
+            pltpu.SemaphoreType.DMA((copies,)),
+        ],
+        compiler_params=pltpu.CompilerParams(
+            collective_id=collective, has_side_effects=True, vmem_limit_bytes=32 << 20
+        ),
+    )(g)
+
+
+BIG = 32768.0
+
+
+def bounds(lens_ref, n, base_block, rows, i):
+    first=(base_block+i)*rows; last=first+rows-1
+    lo=jnp.int32(0); hi=jnp.int32(0); start=jnp.int32(0)
+    for m in range(n):
+        end=start+lens_ref[m]
+        lo=jnp.where((start<=first)&(first<end),start,lo)
+        hi=jnp.where((start<=last)&(last<end),end-1,hi)
+        start=end
+    return lax.div(lo,rows), lax.div(hi,rows)
+
+def image_marks(lens_ref, n, marks, rows):
+    r=lax.broadcasted_iota(jnp.int32,(marks,rows),0)
+    st=jnp.full((marks,rows),1<<30,jnp.int32); en=jnp.zeros((marks,rows),jnp.int32)
+    start=jnp.int32(0)
+    for m in range(n):
+        end=start+lens_ref[m]
+        st=jnp.where(r==m,start,st); en=jnp.where(r==m,end,en)
+        start=end
+    return st,en
+
+def fwd_kernel(n,own,slots,halo,rows,width,marks, lens_ref,x_ref,att_ref,lse_ref,o_ref,qa,ka):
+    core=lax.rem(lax.axis_index("seq"),2)
+    base=core*(own-halo)
+    shift=core*halo
+    st,en=image_marks(lens_ref,n,marks,rows)
+    pos=lax.broadcasted_iota(jnp.int32,(marks,rows),1)
+    def prep(s,_):
+        p=pos+(base+s)*rows
+        inside=(p>=st)&(p<en)
+        oh=jnp.where(inside,1.0,0.0).astype(float_type)
+        kt=jnp.concatenate([x_ref[s,1].astype(float_type),(oh-1.0)*BIG],axis=0)
+        ka[s]=kt.T.astype(narrow_type)
+        return 0
+    lax.fori_loop(0,slots,prep,0)
+    def one_q(i,_):
+        s_q=i+shift
+        p=pos+(base+s_q)*rows
+        oh=jnp.where((p>=st)&(p<en),1.0,0.0).astype(narrow_type)
+        q=jnp.concatenate([(x_ref[s_q,0].astype(float_type)*(width**-0.5)).astype(narrow_type),oh],axis=0)
+        lo,hi=bounds(lens_ref,n,base+shift,rows,i)
+        lo=lo-base; hi=hi-base
+        def tile(m,l,o,s):
+            sc=matmul(ka[s],q)
+            m2=jnp.maximum(m,jnp.max(sc,axis=0,keepdims=True))
+            pr=jnp.exp(sc-m2)
+            al=jnp.exp(m-m2)
+            return m2, l*al+jnp.sum(pr,axis=0,keepdims=True), o*al+matmul(x_ref[s,2],pr.astype(narrow_type))
+        def tile2(m,l,o,s):
+            sa=matmul(ka[s],q); sb=matmul(ka[s+1],q)
+            m2=jnp.maximum(m,jnp.maximum(jnp.max(sa,axis=0,keepdims=True),jnp.max(sb,axis=0,keepdims=True)))
+            pa=jnp.exp(sa-m2); pb=jnp.exp(sb-m2)
+            al=jnp.exp(m-m2)
+            l=l*al+jnp.sum(pa,axis=0,keepdims=True)+jnp.sum(pb,axis=0,keepdims=True)
+            return m2,l,o*al+matmul(x_ref[s,2],pa.astype(narrow_type))+matmul(x_ref[s+1,2],pb.astype(narrow_type))
+        m=jnp.full((1,rows),-1e30,float_type); l=jnp.zeros((1,rows),float_type); o=jnp.zeros((width,rows),float_type)
+        cnt=hi-lo+1
+        m,l,o=lax.fori_loop(0,cnt//2,lambda t,c: tile2(*c,lo+2*t),(m,l,o))
+        m,l,o=lax.fori_loop(0,cnt%2,lambda t,c: tile(*c,hi),(m,l,o))
+        o=o/l
+        att_ref[i]=o.astype(narrow_type)
+        o_ref[i]=o
+        lse_ref[i]=jnp.broadcast_to(m+jnp.log(l),(8,rows))
+        return 0
+    lax.fori_loop(0,own,one_q,0)
+
+def attention_forward(lengths,x,own,halo):
+    slots,_,width,rows=x.shape
+    n=lengths.shape[0]; marks=-(-n//16)*16
+    V=pl.BlockSpec(memory_space=pltpu.VMEM)
+    return pl.pallas_call(functools.partial(fwd_kernel,n,own,slots,halo,rows,width,marks),
+        out_shape=(jax.ShapeDtypeStruct((own,width,rows),narrow_type),jax.ShapeDtypeStruct((own,8,rows),float_type),jax.ShapeDtypeStruct((own,width,rows),float_type)),
+        in_specs=[pl.BlockSpec(memory_space=pltpu.SMEM),V],out_specs=(V,V,V),
+        scratch_shapes=[pltpu.VMEM((width+marks,rows),narrow_type),pltpu.VMEM((slots,rows,width+marks),narrow_type)],
+        compiler_params=pltpu.CompilerParams(vmem_limit_bytes=40<<20))(lengths,x)
+
+def bwd_kernel(n,own,slots,halo,rows,width,marks, lens_ref,x_ref,g_ref,lse_ref,o_ref,dx_ref,dh_ref,ka,vv,qa,qn,gn,dd,dq):
+    core=lax.rem(lax.axis_index("seq"),2)
+    base=core*(own-halo); shift=core*halo
+    st,en=image_marks(lens_ref,n,marks,rows)
+    pos=lax.broadcasted_iota(jnp.int32,(marks,rows),1)
+    def prep(s,_):
+        p=pos+(base+s)*rows
+        oh=jnp.where((p>=st)&(p<en),1.0,0.0).astype(float_type)
+        kt=jnp.concatenate([x_ref[s,1].astype(float_type),(oh-1.0)*BIG],axis=0)
+        ka[s]=kt.T.astype(narrow_type)
+        vv[s]=x_ref[s,2].astype(float_type).T.astype(narrow_type)
+        return 0
+    lax.fori_loop(0,slots,prep,0)
+    def prepq(i,_):
+        s=i+shift
+        p=pos+(base+s)*rows
+        oh=jnp.where((p>=st)&(p<en),1.0,0.0).astype(narrow_type)
+        qs=x_ref[s,0].astype(float_type)*(width**-0.5)
+        qa[i]=jnp.concatenate([qs.astype(narrow_type),oh],axis=0)
+        qn[i]=qs.T.astype(narrow_type)
+        g=g_ref[i].astype(float_type)
+        gn[i]=g.T.astype(narrow_type)
+        dd[i]=jnp.broadcast_to(jnp.sum(g*o_ref[i],axis=0,keepdims=True),(8,rows))
+        dq[i]=jnp.zeros((width,rows),float_type)
+        return 0
+    lax.fori_loop(0,own,prepq,0)
+    def one_k(s,_):
+        lo,hi=bounds(lens_ref,n,base,rows,s)
+        lo=jnp.maximum(lo-base-shift,0); hi=jnp.minimum(hi-base-shift,own-1)
+        kt=x_ref[s,1]
+        def tile(i,dk,dv):
+            sc=matmul(ka[s],qa[i])
+            pr=jnp.exp(sc-lse_ref[i][0:1])
+            dp=matmul(vv[s],g_ref[i])
+            ds=(pr*(dp-dd[i][0:1])).astype(narrow_type)
+            dq[i]+=matmul(kt,ds)
+            return dk+matmul(ds,qn[i]), dv+matmul(pr.astype(narrow_type),gn[i])
+        z=jnp.zeros((rows,width),float_type)
+        cnt=jnp.maximum(hi-lo+1,0)
+        def two(t,c):
+            c=tile(lo+2*t,*c)
+            return tile(lo+2*t+1,*c)
+        dk,dv=lax.fori_loop(0,cnt//2,two,(z,z))
+        dk,dv=lax.fori_loop(0,cnt%2,lambda t,c: tile(hi,*c),(dk,dv))
+        i=s-shift
+        @pl.when((i>=0)&(i<own))
+        def _():
+            dx_ref[i,1]=dk.T.astype(narrow_type)
+            dx_ref[i,2]=dv.T.astype(narrow_type)
+        @pl.when((i<0)|(i>=own))
+        def _():
+            j=jnp.where(i<0,s,i-own)
+            dh_ref[j,0]=dk.T.astype(narrow_type)
+            dh_ref[j,1]=dv.T.astype(narrow_type)
+        return 0
+    lax.fori_loop(0,slots,one_k,0)
+    def fin(i,_):
+        dx_ref[i,0]=(dq[i]*(width**-0.5)).astype(narrow_type)
+        return 0
+    lax.fori_loop(0,own,fin,0)
+
+def attention_backward(lengths,x,g,lse,o,own,halo):
+    slots,_,width,rows=x.shape
+    n=lengths.shape[0]; marks=-(-n//16)*16
+    V=pl.BlockSpec(memory_space=pltpu.VMEM)
+    return pl.pallas_call(functools.partial(bwd_kernel,n,own,slots,halo,rows,width,marks),
+        out_shape=(jax.ShapeDtypeStruct((own,3,width,rows),narrow_type),jax.ShapeDtypeStruct((halo,2,width,rows),narrow_type)),
+        in_specs=[pl.BlockSpec(memory_space=pltpu.SMEM),V,V,V,V],out_specs=(V,V),
+        scratch_shapes=[pltpu.VMEM((slots,rows,width+marks),narrow_type),pltpu.VMEM((slots,rows,width),narrow_type),
+          pltpu.VMEM((own,width+marks,rows),narrow_type),pltpu.VMEM((own,rows,width),narrow_type),pltpu.VMEM((own,rows,width),narrow_type),
+          pltpu.VMEM((own,8,rows),float_type),pltpu.VMEM((own,width,rows),float_type)],
+        compiler_params=pltpu.CompilerParams(vmem_limit_bytes=48<<20))(lengths,x,g,lse,o)
+
+
+def layer_on_slice(
+    tokens,
+    lengths,
+    adapter_choice,
+    gain_rows,
+    bias_rows,
+    query_key_value,
+    output_weight,
+    expand_weight,
+    expand_bias,
+    contract_weight,
+    adapter_in_attention,
+    adapter_out_attention,
+    adapter_in_expand,
+    adapter_out_expand,
+    adapter_in_contract,
+    adapter_out_contract,
+    cotangent,
+):
+    row_count, features = tokens.shape
+    depth = lax.axis_size("fsdp")
+    devices = lax.axis_size(("seq", "fsdp"))
+    position = lax.axis_index(("seq", "fsdp"))
+    own = devices // 2
+    head_width = features // HEADS
+    rank_width = adapter_in_attention.shape[2]
+    share = features // devices
+    hidden_share = contract_weight.shape[0]
+    halo = -(-(LONGEST - 1) // row_count)
+
+    vectors = jnp.concatenate([gain_rows.T, bias_rows.T, expand_bias.reshape(share, -1)], axis=1)
+    vectors = jnp.pad(vectors, ((0, 0), (0, rank_width - vectors.shape[1])))
+    pieces = (
+        adapter_in_attention.reshape(4 * share, rank_width),
+        adapter_out_attention.transpose(0, 2, 1).reshape(4 * share, rank_width),
+        adapter_in_expand,
+        adapter_out_expand.T,
+        adapter_in_contract,
+        adapter_out_contract.T,
+        vectors,
+    )
+    offsets = [0]
+    for piece in pieces:
+        offsets.append(offsets[-1] + piece.shape[0])
+    packed = jnp.concatenate(pieces, axis=0)
+    shards = (packed, query_key_value, output_weight, expand_weight, contract_weight)
+    chunks = []
+    for array in (0, 1, 2, 3, 4):
+        rows, columns = shards[array].shape
+        for which in range(2):
+            if columns > rank_width:
+                half = columns // 2
+                chunks.append((array, slice(0, rows), slice(which * half, (which + 1) * half), which))
+            else:
+                half = rows // 2
+                chunks.append((array, slice(which * half, (which + 1) * half), slice(0, columns), which))
+    packed_full, qkv_full, output_full, expand_full, contract_full = gather_everything(
+        shards, chunks, devices, depth, 1
+    )
+    qkv_full = qkv_full.reshape(features, 3 * features)
+    output_full = output_full.reshape(features, features)
+    expand_full = expand_full.reshape(features, -1)
+    contract_full = contract_full.reshape(-1, features)
+    parts = [packed_full[:, a:b] for a, b in zip(offsets[:-1], offsets[1:])]
+
+    def four(part):
+        return (
+            part.reshape(devices, 4, share, rank_width).transpose(1, 0, 2, 3).reshape(4, features, rank_width)
+        )
+
+    attention_down, attention_up = four(parts[0]), four(parts[1])
+    expand_down, expand_up, contract_down, contract_up = (
+        part.reshape(-1, rank_width) for part in parts[2:6]
+    )
+    vectors = parts[6].reshape(features, rank_width).astype(float_type)
+    gains_wide = vectors[:, :4].T
+    biases_wide = vectors[:, 4:9].T
+    expand_bias_wide = vectors[:, 9 : 9 + hidden_share // share].reshape(-1)
+
+    image_ends = jnp.cumsum(lengths)
+    places = position * row_count + jnp.arange(row_count, dtype=jnp.int32)
+    own_image = jnp.sum((places[:, None] >= image_ends[None, :]).astype(jnp.int32), axis=1)
+    matches = own_image[:, None] == jnp.arange(lengths.shape[0], dtype=jnp.int32)[None, :]
+    chosen = jnp.sum(jnp.where(matches, adapter_choice[None, :], 0), axis=1)
+    select = (jnp.arange(rank_width, dtype=jnp.int32)[None, :] // RANK == chosen[:, None]).astype(float_type)
+
+    residual = tokens.astype(float_type)
+    normed_first, normal_first, scaling_first = layer_norm(residual, gains_wide[0], biases_wide[0])
+    normed_first = normed_first.astype(narrow_type)
+    rank_qkv = [
+        (matmul(normed_first, attention_down[p]) * select).astype(narrow_type) for p in range(3)
+    ]
+    adapted = jnp.concatenate([transposed_right(attention_up[p], rank_qkv[p]) for p in range(3)], axis=0)
+    query_bias = jnp.concatenate([biases_wide[1], jnp.zeros((2 * features,), float_type)])
+    projected = lax.dot_general(
+        qkv_full, normed_first, (((0,), (1,)), ((), ())), preferred_element_type=float_type
+    )
+    projected = (projected + adapted + query_bias[:, None]).astype(narrow_type)
+    on_heads = to_heads(projected.reshape(3, HEADS, head_width, row_count), halo, depth, 2)
+    attended_blocks, log_totals, attended_wide = attention_forward(lengths, on_heads, own, halo)
+    attended = to_rows(attended_blocks[:, None], depth, 3).reshape(features, row_count)
+
+    rank_out = (transposed_left(attended, attention_down[3]) * select).astype(narrow_type)
+    mixed = (
+        transposed_left(attended, output_full)
+        + biases_wide[2]
+        + transposed_right(rank_out, attention_up[3])
+    )
+    middle = residual + gains_wide[1] * mixed
+    normed_second, normal_second, scaling_second = layer_norm(middle, gains_wide[2], biases_wide[3])
+    normed_second = normed_second.astype(narrow_type)
+    rank_expand = (matmul(normed_second, expand_down) * select).astype(narrow_type)
+    hidden_pre = (
+        matmul(normed_second, expand_full)
+        + expand_bias_wide
+        + transposed_right(rank_expand, expand_up)
+    )
+    active = jax.nn.gelu(hidden_pre, approximate=False).astype(narrow_type)
+    rank_contract = (matmul(active, contract_down) * select).astype(narrow_type)
+    branch = (
+        matmul(active, contract_full) + biases_wide[4] + transposed_right(rank_contract, contract_up)
+    )
+    result = (middle + gains_wide[3] * branch).astype(narrow_type)
+
+    gradient_out = cotangent.astype(float_type)
+    grad_branch = (gains_wide[3] * gradient_out).astype(narrow_type)
+    grad_rank_contract = (matmul(grad_branch, contract_up) * select).astype(narrow_type)
+    grad_contract_down = transposed_left(active, grad_rank_contract)
+    grad_contract_up = transposed_left(grad_branch, rank_contract)
+    grad_active = transposed_right(grad_branch, contract_full) + transposed_right(
+        grad_rank_contract, contract_down
+    )
+    grad_hidden = (grad_active * gelu_slope(hidden_pre)).astype(narrow_type)
+    grad_rank_expand = (matmul(grad_hidden, expand_up) * select).astype(narrow_type)
+    grad_expand_down = transposed_left(normed_second, grad_rank_expand)
+    grad_expand_up = transposed_left(grad_hidden, rank_expand)
+    grad_normed_second = transposed_right(grad_hidden, expand_full) + transposed_right(
+        grad_rank_expand, expand_down
+    )
+    grad_middle = gradient_out + norm_backward(
+        grad_normed_second, gains_wide[2], normal_second, scaling_second
+    )
+    grad_mixed = (gains_wide[1] * grad_middle).astype(narrow_type)
+    grad_rank_out = (matmul(grad_mixed, attention_up[3]) * select).astype(narrow_type)
+    grad_out_down = matmul(attended, grad_rank_out)
+    grad_out_up = transposed_left(grad_mixed, rank_out)
+    grad_attended = (
+        transposed_right(output_full, grad_mixed) + transposed_right(attention_down[3], grad_rank_out)
+    ).astype(narrow_type)
+    grad_on_heads = to_heads(
+        grad_attended.reshape(1, HEADS, head_width, row_count), 0, depth, 4
+    ).reshape(own, head_width, row_count)
+    grad_blocks, grad_halo = attention_backward(
+        lengths, on_heads, grad_on_heads, log_totals, attended_wide, own, halo
+    )
+    grad_projected = to_rows_merged(grad_blocks, grad_halo, depth, 5).reshape(3, features, row_count)
+
+    grad_rank_qkv = [
+        (transposed_left(grad_projected[p], attention_up[p]) * select).astype(narrow_type)
+        for p in range(3)
+    ]
+    grad_down = [transposed_left(normed_first, grad_rank_qkv[p]) for p in range(3)] + [grad_out_down]
+    grad_up = [matmul(grad_projected[p], rank_qkv[p]) for p in range(3)] + [grad_out_up]
+    grad_normed_first = lax.dot_general(
+        grad_projected.reshape(3 * features, row_count),
+        qkv_full,
+        (((0,), (1,)), ((), ())),
+        preferred_element_type=float_type,
+    )
+    for p in range(3):
+        grad_normed_first = grad_normed_first + transposed_right(grad_rank_qkv[p], attention_down[p])
+    input_gradient = grad_middle + norm_backward(
+        grad_normed_first, gains_wide[0], normal_first, scaling_first
+    )
+
+    terms = jnp.concatenate(
+        [
+            grad.astype(narrow_type).reshape(devices, -1, rank_width)
+            for grad in grad_down
+            + grad_up
+            + [grad_expand_down, grad_expand_up, grad_contract_down, grad_contract_up]
+        ],
+        axis=1,
+    )
+    total = reduce_shards(terms.reshape(devices // depth, depth, -1, rank_width), depth, 6)
+    shares = [total[a:b] for a, b in zip(offsets[:-1], offsets[1:-1])]
+    return (
+        result,
+        input_gradient,
+        shares[0].reshape(4, share, rank_width),
+        shares[1].reshape(4, share, rank_width).transpose(0, 2, 1),
+        shares[2],
+        shares[3].T,
+        shares[4],
+        shares[5].T,
+    )
+
+
 def solution(mesh):
+    per_device = layer_on_slice if dict(mesh.shape) == {"seq": 8, "fsdp": 4} else general_layer
     placed = (
         P(("seq", "fsdp"), None),
         P(),

time: 2280 us -> 496 us (0.22)
  waiting for transfers between devices: 1020 us -> 0 us
  blocking collectives: 707 us -> 0 us
  Pallas kernels: 0 us -> 393 us
  matrix products: 212 us -> 61.8 us
  local copies, waits for them, and re-layouts: 149 us -> 24.8 us
  starting transfers between devices: 72.9 us -> 0 us
  other arithmetic: 60.9 us -> 4.49 us
  loops' own time: 24.4 us -> 0 us
    all_gather x8 -> x0, blocking collectives: 707 us -> none  [the longest x1 121 us: per_device(): lax.all_gather(renewed[12], ('seq', 'fsdp'), axis=1, tiled=True)]
    reduce_scatter x4 -> x0, waiting for transfers between devices: 542 us -> none  [the longest x1 139 us: per_device(): lax.psum_scatter(grad_contract_down, ('seq', 'fsdp'), scatter_dimension=0...]
    pallas_call x0 -> x8, Pallas kernels: none -> 393 us  [the longest x1 163 us: gather_everything(): pl.pallas_call(functools.partial(gather_kernel, len(shards), chunks, dept...]
    ppermute x24 -> x0, waiting for transfers between devices: 354 us -> none  [passed_along(): return lax.ppermute(block, axis, route)]
    dot_general x62 -> x2, matrix products: 124 us -> 11.1 us  [the longest x1 6.38 us: layer_on_slice(): lax.dot_general(qkv_full, normed_first, (((0,), (1,)), ((), ())), preferr...]
    ppermute x24 -> x0, starting transfers between devices: 72 us -> none  [passed_along(): return lax.ppermute(block, axis, route)]
    unnamed x22 -> x0, waiting for transfers between devices: 68.1 us -> none
    all_gather x16 -> x0, waiting for transfers between devices: 60 us -> none  [the longest x1 51.2 us: per_device(): lax.all_gather(renewed[7], ('seq', 'fsdp'), axis=1, tiled=True)]
  transfers between devices with their start and end apart: 45 -> 0, of which waited for: 17 -> 0; matrix products, arithmetic and copies ran while one was open for 18% -> 0% of each run, Pallas kernels for 0% -> 0%
where the time goes in v1:
time: 496 us; the launch traced here: 487 us
  Pallas kernels  393 us (79%)
  matrix products  61.8 us (12%)
  local copies, waits for them, and re-layouts  24.8 us (5%)
    pallas_call x1, Pallas kernels, gather_everything(): pl.pallas_call(functools.partial(gather_kernel, len(shards), chunks, dept...  163 us
    pallas_call x2, Pallas kernels, to_heads(): pl.pallas_call(functools.partial(to_heads_kernel, heads, depth, halo), ou...  57.4 us
    pallas_call x1, Pallas kernels, reduce_shards(): pl.pallas_call(functools.partial(reduce_kernel, depth), out_shape=jax.Sha...  45.7 us
    pallas_call x1, Pallas kernels, attention_backward(): pl.pallas_call(functools.partial(bwd_kernel, n, own, slots, halo, rows, w...  43.9 us
    pallas_call x1, Pallas kernels, to_rows_merged(): pl.pallas_call(functools.partial(to_rows_merged_kernel, heads, depth, h.s...  35 us
    dot_general x15, matrix products, transposed_right(): lax.dot_general(first_operand, second_operand, (((1,), (1,)), ((), ())),...  29.5 us
    pallas_call x1, Pallas kernels, attention_forward(): pl.pallas_call(functools.partial(fwd_kernel, n, own, slots, halo, rows, w...  27.1 us
    pallas_call x1, Pallas kernels, to_rows(): pl.pallas_call(functools.partial(to_rows_kernel, heads, depth), out_shape...  21.1 us

profile of v1, /device:TPU:0, one launch (start us, length us, event | category | flops | bytes accessed | tf_op | source)
XLA Modules:
  0.0 486.8 jit_solution(4058282230747255488)
XLA Ops:
  0.6 0.8 constant_dynamic-update-slice_fusion.6
  1.4 0.8 constant_dynamic-update-slice_fusion.5
  2.2 0.7 constant_dynamic-update-slice_fusion.4
  2.9 0.9 copy.34
  3.7 0.8 constant_dynamic-update-slice_fusion.2
  4.5 0.7 constant_dynamic-update-slice_fusion.1
  5.2 0.8 reshape.250
  6.0 0.8 copy.36
  6.8 0.8 copy.35
  7.6 0.7 copy-done.52
  8.3 163.1 %shard_map.224 = (bf16[32,608,128]{2,1,0:T(8,128)(2,1)}, bf16[32,32,3072]{2,1,0:T(8,128)(2,1)}, bf16[32,32,1024]{2,1,0:T(8,128)(2,1)}, bf16[32,32,4096]{2,1,0:T(8,128)(2,1)}, bf16[32,128,1024]{2,1,0:T(8,128)(2,1)}) custom-call(bf16[608,128]{1,0:T(8,128)(2,1)} %copy-done.52, bf16[32,3072]{1,0:T(8,128)(2,1)} %refs_1_.1, bf16[32,1024]{1,0:T(8,128)(2,1)} %refs_2_.1, ...), custom_call_target="tpu_custom_call" | custom-call | tf_op jit(solution)/shard_map/pallas_call | solution.py:504
  171.4 2.1 fusion.61
  173.9 1.0 fusion.66
  174.9 1.0 slice_reduce_fusion.1
  176.8 2.1 fusion.62
  178.9 1.0 fusion.64
  179.8 0.8 fusion.65
  181.9 1.3 fusion.71
  183.8 6.4 %fusion.17 = bf16[3072,256]{1,0:T(8,128)(2,1)} fusion(bf16[1024,3072]{1,0:T(8,128)(2,1)} %bitcast.235, bf16[256,1024]{1,0:T(8,128)(2,1)S(1)} %fusion.43, f32[1024,256]{1,0:T(8,128)S(1)} %fusion.72, f32[1024,256]{1,0:T(8,128)S(1)} %fusion.71, f32[1024,256]{1,0:T(8,128)S(1)} %fusion.70, f32[3072]{0:T(1024)S(1)} %concatenate.43), kind=kOutput, calls=%fused_computation.33 | convolution fusion | flops 1614544896 | bytes 11546624 | tf_op jit(solution)/shard_map/dot_general | solution.py:1123
  190.3 40.5 %shard_map.225.x_ref = bf16[22,3,64,256]{3,2,1,0:T(8,128)(2,1)} custom-call(bf16[3,16,64,256]{3,2,1,0:T(8,128)(2,1)} %bitcast.201), custom_call_target="tpu_custom_call" | custom-call | tf_op jit(solution)/shard_map/pallas_call | solution.py:603
  230.8 1.6 copy-done
  232.4 27.1 %shard_map.226 = (bf16[16,64,256]{2,1,0:T(8,128)(2,1)S(1)}, f32[16,8,256]{2,1,0:T(8,128)S(1)}, f32[16,64,256]{2,1,0:T(8,128)S(1)}) custom-call(s32[8]{0:T(128)S(1)} %copy-done.4, bf16[22,3,64,256]{3,2,1,0:T(8,128)(2,1)S(1)} %copy-done), custom_call_target="tpu_custom_call" | custom-call | tf_op jit(solution)/shard_map/pallas_call | solution.py:949
  259.5 0.8 copy-done.3
  260.3 21.1 %shard_map.227 = bf16[1,16,64,256]{3,2,1,0:T(8,128)(2,1)} custom-call(bf16[16,1,64,256]{3,2,1,0:T(8,128)(2,1)} %bitcast.161), custom_call_target="tpu_custom_call" | custom-call | tf_op jit(solution)/shard_map/pallas_call | solution.py:677
  281.4 2.5 convolution_add_fusion.11
  283.9 1.4 fusion.35
  285.3 0.4 fusion.69
  286.6 1.3 add.164
  287.9 5.9 %convolution_add_fusion.2 = f32[256,4096]{1,0:T(8,128)S(1)} fusion(bf16[256,1024]{1,0:T(8,128)(2,1)S(1)} %add_convert_fusion, bf16[1024,4096]{1,0:T(8,128)(2,1)} %bitcast.227, f32[4096]{0:T(1024)S(1)} %add.164), kind=kOutput, calls=%fused_computation.5 | convolution fusion | flops 2148532224 | bytes 13123584 | tf_op jit(solution)/shard_map/dot_general | solution.py:44
  294.2 10.9 %fusion.4 = (bf16[256,4096]{1,0:T(8,128)(2,1)S(1)}, f32[256,4096]{1,0:T(8,128)}) fusion(f32[256,4096]{1,0:T(8,128)S(1)} %convolution_add_fusion.2, bf16[256,128]{1,0:T(8,128)(2,1)S(1)} %fusion.36, bf16[4096,128]{1,0:T(8,128)(2,1)S(1)} %bitcast.174), kind=kOutput, calls=%fused_computation.11 | convolution fusion | flops 337641472 | bytes 11599872 | tf_op jit(solution)/shard_map/dot_general | solution.py:54
  305.1 2.4 convolution_add_fusion.12
  307.6 0.7 fusion.30
  308.3 1.1 fusion.23
  309.4 4.5 fusion.52
  314.2 4.7 fusion.1
  319.0 2.6 fusion.73
  321.6 0.7 fusion.31
  322.3 0.5 fusion.60
  322.9 1.4 multiply_convert_fusion
  324.3 0.7 fusion.74
  325.4 1.1 fusion.24
  326.5 17.0 %shard_map.228 = bf16[16,1,64,256]{3,2,1,0:T(8,128)(2,1)} custom-call(bf16[1,16,64,256]{3,2,1,0:T(8,128)(2,1)} %bitcast.200), custom_call_target="tpu_custom_call" | custom-call | tf_op jit(solution)/shard_map/pallas_call | solution.py:603
  343.5 1.0 copy-done.2
  344.6 43.9 %shard_map.229 = (bf16[16,3,64,256]{3,2,1,0:T(8,128)(2,1)S(1)}, bf16[6,2,64,256]{3,2,1,0:T(8,128)(2,1)S(1)}) custom-call(s32[8]{0:T(128)S(1)} %copy-done.4, bf16[22,3,64,256]{3,2,1,0:T(8,128)(2,1)S(1)} %copy-done.1, bf16[16,64,256]{2,1,0:T(8,128)(2,1)S(1)} %bitcast.160, f32[16,8,256]{2,1,0:T(8,128)S(1)} %get-tuple-element.24.lse_ref, ...), custom_call_target="tpu_custom_call" | custom-call | tf_op jit(solution)/shard_map/pallas_call | solution.py:1020
  388.5 35.0 %shard_map.230 = bf16[3,16,64,256]{3,2,1,0:T(8,128)(2,1)S(1)} custom-call(bf16[16,3,64,256]{3,2,1,0:T(8,128)(2,1)S(1)} %get-tuple-element.26.x_ref, bf16[6,2,64,256]{3,2,1,0:T(8,128)(2,1)S(1)} %get-tuple-element.27.h_ref), custom_call_target="tpu_custom_call" | custom-call | tf_op jit(solution)/shard_map/pallas_call | solution.py:774
  423.5 4.7 fusion.75
  428.5 0.3 fusion.39
  429.2 0.3 fusion.40
  429.9 0.3 fusion.41
  430.3 0.5 fusion.59
  430.9 1.3 fusion.47
  432.2 0.4 convolution_convert_fusion.11
  432.6 0.4 convolution_convert_fusion.10
  433.0 0.4 convolution_convert_fusion.9
  434.9 0.4 convolution_convert_fusion.4
  435.3 0.4 convolution_convert_fusion.3
  435.7 0.8 convolution_convert_fusion.1
  436.6 0.6 copy-done.10
  437.2 0.8 convolution_convert_fusion
  438.3 0.3 convolution_convert_fusion.2
  438.7 45.7 %shard_map.231 = f32[576,128]{1,0:T(8,128)S(1)} custom-call(bf16[8,4,576,128]{3,2,1,0:T(8,128)(2,1)S(1)} %constant_dynamic-update-slice_fusion.7.g_ref), custom_call_target="tpu_custom_call" | custom-call | tf_op jit(solution)/shard_map/pallas_call | solution.py:858
  484.4 0.7 fusion.67
  485.1 0.6 slice_bitcast_fusion.2
  485.7 0.7 copy.38
  (196 shorter events, 7.8 us)
Async XLA Ops:
  171.4 4.6 copy-start.7
  173.9 2.9 copy-start.14
  176.0 2.9 copy-start.55
  176.0 109.3 %copy-start.59 = (f32[1024]{0:T(1024)}, f32[1024]{0:T(1024)S(1)}, u32[]{:S(2)}) copy-start(f32[1024]{0:T(1024)S(1)} %get-tuple-element.59) | copy-start | bytes 12292
  176.0 110.0 %copy-start.57 = (f32[1024]{0:T(1024)}, f32[1024]{0:T(1024)S(1)}, u32[]{:S(2)}) copy-start(f32[1024]{0:T(1024)S(1)} %get-tuple-element.57) | copy-start | bytes 12292
  176.2 2.7 copy-start.61
  176.5 2.4 copy-start.65
  176.8 7.1 %copy-start.5 = (bf16[256,1024]{1,0:T(8,128)(2,1)}, bf16[256,1024]{1,0:T(8,128)(2,1)S(1)}, u32[]{:S(2)}) copy-start(bf16[256,1024]{1,0:T(8,128)(2,1)S(1)} %fusion.43) | copy-start | bytes 1572868
  178.8 1.8 copy-start.4
  178.9 2.1 copy-start.69
  179.8 4.0 copy-start.28
  180.6 9.6 %copy-start.22 = (bf16[1,32,32,128]{3,2,0,1:T(8,128)(2,1)}, bf16[1,32,32,128]{3,2,0,1:T(8,128)(2,1)S(1)}, u32[]{:S(2)}) copy-start(bf16[1,32,32,128]{3,2,0,1:T(8,128)(2,1)S(1)} %get-tuple-element.77) | copy-start | bytes 786436
  180.6 9.6 %copy-start.24 = (bf16[1,32,32,128]{3,2,0,1:T(8,128)(2,1)}, bf16[1,32,32,128]{3,2,0,1:T(8,128)(2,1)S(1)}, u32[]{:S(2)}) copy-start(bf16[1,32,32,128]{3,2,0,1:T(8,128)(2,1)S(1)} %get-tuple-element.78) | copy-start | bytes 786436
  180.6 9.6 %copy-start.26 = (bf16[1,32,32,128]{3,2,0,1:T(8,128)(2,1)}, bf16[1,32,32,128]{3,2,0,1:T(8,128)(2,1)S(1)}, u32[]{:S(2)}) copy-start(bf16[1,32,32,128]{3,2,0,1:T(8,128)(2,1)S(1)} %get-tuple-element.79) | copy-start | bytes 786436
  180.6 2.9 copy-start.31
  181.3 8.9 %copy-start.42 = (bf16[256,128]{1,0:T(8,128)(2,1)}, bf16[256,128]{1,0:T(8,128)(2,1)S(1)}, u32[]{:S(2)}) copy-start(bf16[256,128]{1,0:T(8,128)(2,1)S(1)} %fusion.34) | copy-start | bytes 196612
  181.9 8.3 %copy-start.44 = (bf16[256,128]{1,0:T(8,128)(2,1)}, bf16[256,128]{1,0:T(8,128)(2,1)S(1)}, u32[]{:S(2)}) copy-start(bf16[256,128]{1,0:T(8,128)(2,1)S(1)} %fusion.33) | copy-start | bytes 196612
  183.5 6.8 %copy-start.46 = (bf16[256,128]{1,0:T(8,128)(2,1)}, bf16[256,128]{1,0:T(8,128)(2,1)S(1)}, u32[]{:S(2)}) copy-start(bf16[256,128]{1,0:T(8,128)(2,1)S(1)} %fusion.32) | copy-start | bytes 196612
  230.7 1.6 copy-start
  232.4 51.5 %copy-start.36 = (bf16[1,32,32,128]{3,2,0,1:T(8,128)(2,1)S(1)}, bf16[1,32,32,128]{3,2,0,1:T(8,128)(2,1)}, u32[]{:S(2)}) copy-start(bf16[1,32,32,128]{3,2,0,1:T(8,128)(2,1)} %get-tuple-element.76) | copy-start | bytes 786436
  232.4 53.0 %copy-start.34 = (bf16[1,32,32,128]{3,2,0,1:T(8,128)(2,1)S(1)}, bf16[1,32,32,128]{3,2,0,1:T(8,128)(2,1)}, u32[]{:S(2)}) copy-start(bf16[1,32,32,128]{3,2,0,1:T(8,128)(2,1)} %get-tuple-element.72) | copy-start | bytes 786436
  285.7 8.1 %copy-start.63 = (f32[256]{0:T(256)}, f32[256]{0:T(256)S(1)}, u32[]{:S(2)}) copy-start(f32[256]{0:T(256)S(1)} %broadcast_multiply_fusion.4) | copy-start | bytes 3076
  286.3 7.5 %copy-start.15 = (bf16[256,1024]{1,0:T(8,128)(2,1)}, bf16[256,1024]{1,0:T(8,128)(2,1)S(1)}, u32[]{:S(2)}) copy-start(bf16[256,1024]{1,0:T(8,128)(2,1)S(1)} %add_convert_fusion) | copy-start | bytes 1572868
  287.9 5.9 %copy-start.33 = (bf16[32,32,128]{2,1,0:T(8,128)(2,1)S(1)}, bf16[32,32,128]{2,1,0:T(8,128)(2,1)}, u32[]{:S(2)}) copy-start(bf16[32,32,128]{2,1,0:T(8,128)(2,1)} %get-tuple-element.63) | copy-start | bytes 786436
  287.9 6.2 %copy-start.19 = (bf16[32,128,128]{2,1,0:T(8,128)(2,1)S(1)}, bf16[32,128,128]{2,1,0:T(8,128)(2,1)}, u32[]{:S(2)}) copy-start(bf16[32,128,128]{2,1,0:T(8,128)(2,1)} %get-tuple-element.66) | copy-start | bytes 3145732
  287.9 17.1 %slice-start.2 = ((s8[8388608]{0:T(1024)(128)(4,1)}), s8[4194304]{0:T(1024)(128)(4,1)S(1)}, s32[]{:S(2)}) async-start(s8[8388608]{0:T(1024)(128)(4,1)} %bitcast.231), calls=%async_computation.2 | async-start | bytes 8388608
  294.1 10.9 %copy-start.50 = (bf16[256,128]{1,0:T(8,128)(2,1)}, bf16[256,128]{1,0:T(8,128)(2,1)S(1)}, u32[]{:S(2)}) copy-start(bf16[256,128]{1,0:T(8,128)(2,1)S(1)} %fusion.36) | copy-start | bytes 196612
  294.2 10.9 %slice-start.3 = ((s8[8388608]{0:T(1024)(128)(4,1)}), s8[4194304]{0:T(1024)(128)(4,1)S(1)}, s32[]{:S(2)}) async-start(s8[8388608]{0:T(1024)(128)(4,1)} %bitcast.231), calls=%async_computation.3 | async-start | bytes 8388608
  305.0 2.5 copy-start.9
  305.1 2.5 copy-start.20
  305.1 3.2 copy-start.41
  307.5 1.9 copy-start.39
  309.4 9.5 %slice-start = ((s8[8388608]{0:T(1024)(128)(4,1)}), s8[4194304]{0:T(1024)(128)(4,1)S(1)}, s32[]{:S(2)}) async-start(s8[8388608]{0:T(1024)(128)(4,1)} %bitcast.228), calls=%async_computation | async-start | bytes 8388608
  313.9 5.0 %slice-start.1 = ((s8[8388608]{0:T(1024)(128)(4,1)}), s8[4194304]{0:T(1024)(128)(4,1)S(1)}, s32[]{:S(2)}) async-start(s8[8388608]{0:T(1024)(128)(4,1)} %bitcast.228), calls=%async_computation.1 | async-start | bytes 8388608
  314.2 4.7 copy-start.53
  318.9 2.7 copy-start.11
  318.9 3.4 copy-start.58
  318.9 3.4 copy-start.64
  319.0 3.4 copy-start.68
  322.3 2.0 copy-start.38
  322.9 2.2 copy-start.35
  324.3 2.2 copy-start.17
  324.3 19.2 %copy-start.1 = (bf16[22,3,64,256]{3,2,1,0:T(8,128)(2,1)S(1)}, bf16[22,3,64,256]{3,2,1,0:T(8,128)(2,1)}, u32[]{:S(2)}) copy-start(bf16[22,3,64,256]{3,2,1,0:T(8,128)(2,1)} %shard_map.225.x_ref) | copy-start | bytes 6488068
  423.5 5.0 %copy-start.32 = (bf16[1,32,32,128]{3,2,0,1:T(8,128)(2,1)S(1)}, bf16[1,32,32,128]{3,2,0,1:T(8,128)(2,1)}, u32[]{:S(2)}) copy-start(bf16[1,32,32,128]{3,2,0,1:T(8,128)(2,1)} %get-tuple-element.75) | copy-start | bytes 786436
  423.5 5.4 %copy-start.27 = (bf16[1,32,32,128]{3,2,0,1:T(8,128)(2,1)S(1)}, bf16[1,32,32,128]{3,2,0,1:T(8,128)(2,1)}, u32[]{:S(2)}) copy-start(bf16[1,32,32,128]{3,2,0,1:T(8,128)(2,1)} %copy-done.26) | copy-start | bytes 786436
  428.3 1.6 copy-start.29
  428.4 1.8 copy-start.8
  428.5 1.8 copy-start.23
  428.5 1.8 copy-start.56
  428.5 1.8 copy-start.62
  428.5 1.8 copy-start.66
  428.9 2.0 copy-start.21
  429.9 2.4 copy-start.6
  430.8 2.6 copy-start.13
  430.8 2.6 copy-start.49
  430.9 3.0 copy-start.47
  432.2 1.9 copy-start.45
  432.2 2.3 copy-start.43
  432.6 2.2 copy-start.18
  433.0 2.2 copy-start.16
  433.5 2.2 copy-start.12
  433.5 2.2 copy-start.51
  435.6 1.6 copy-start.10
  435.6 1.6 copy-start.54
  (10 other events, 9.9 us)

commit v2 on v0

--- a/solution.py
+++ b/solution.py
@@ -1,12 +1,16 @@
+import functools
 import jax
 import jax.numpy as jnp
 from jax import lax
+from jax.experimental import pallas as pl
+from jax.experimental.pallas import tpu as pltpu
 from jax.sharding import PartitionSpec as P
 
 HEADS = 16
 RANK = 16
 HOPS = 6
 EDGE = 1408
+LONGEST = 1370
 
 
 epsilon = 1e-06
@@ -58,7 +62,7 @@
     return cumulative + hidden_pre * density
 
 
-def per_device(
+def general_layer(
     tokens,
     lengths,
     adapter_choice,
@@ -378,7 +382,1296 @@
     )
 
 
+MESH_ID = pl.DeviceIdType.MESH
+CORES, SIDE_X, SIDE_Y = 1, 2, 4
+ANYWHERE = pl.BlockSpec(memory_space=pl.ANY)
+IN_VMEM = pl.BlockSpec(memory_space=pltpu.VMEM)
+IN_SMEM = pl.BlockSpec(memory_space=pltpu.SMEM)
+
+
+def place_here():
+    return lax.axis_index("seq"), lax.axis_index("fsdp")
+
+
+def remote(source, target, send, receive, seq, fsdp):
+    return pltpu.make_async_remote_copy(
+        src_ref=source,
+        dst_ref=target,
+        send_sem=send,
+        recv_sem=receive,
+        device_id=(seq, fsdp),
+        device_id_type=MESH_ID,
+    )
+
+
+def greet(barrier, seq, fsdp):
+    pl.semaphore_signal(barrier, 1, device_id=(seq, fsdp), device_id_type=MESH_ID)
+
+
+def greet_neighbours(barrier, seq, fsdp, depth):
+    for bit in (CORES, SIDE_X, SIDE_Y):
+        greet(barrier, seq ^ bit, fsdp)
+    for step in range(1, depth):
+        greet(barrier, seq, lax.rem(fsdp + step, depth))
+
+
+class Gather:
+    STEPS = 10
+
+    def __init__(self, depth, send, receive):
+        self.depth, self.send, self.receive = depth, send, receive
+        self.seq, self.fsdp = place_here()
+        self.me = self.seq * depth + self.fsdp
+
+    def copy(self, index, step, source, target, seq, fsdp):
+        at = index * self.STEPS + step
+        return remote(source, target, self.send.at[at], self.receive.at[at], seq, fsdp)
+
+    def group(self, chunk, at_seq):
+        full, rows, columns, _ = chunk
+        return full.at[pl.ds(at_seq * self.depth, self.depth), rows, columns]
+
+    def sides(self, chunk):
+        flip = chunk[3]
+        if isinstance(flip, int):
+            return (SIDE_X, SIDE_Y) if flip else (SIDE_Y, SIDE_X)
+        return SIDE_Y - flip * (SIDE_Y - SIDE_X), SIDE_X + flip * (SIDE_Y - SIDE_X)
+
+    def line(self, index, chunk):
+        full, rows, columns, _ = chunk
+        piece = full.at[self.me, rows, columns]
+        return [
+            self.copy(index, step - 1, piece, piece, self.seq, lax.rem(self.fsdp + step, self.depth))
+            for step in range(1, self.depth)
+        ]
+
+    def over(self, index, chunk):
+        a, b = self.sides(chunk)
+        mine, theirs = self.group(chunk, self.seq), self.group(chunk, self.seq ^ a)
+        return [
+            self.copy(index, 3, mine, mine, self.seq ^ a, self.fsdp),
+            self.copy(index, 4, mine, mine, self.seq ^ b, self.fsdp),
+            self.copy(index, 5, theirs, theirs, self.seq ^ b, self.fsdp),
+        ]
+
+    def across(self, index, chunk):
+        a, b = self.sides(chunk)
+        copies = []
+        for i, at_seq in enumerate((self.seq, self.seq ^ a, self.seq ^ b, self.seq ^ a ^ b)):
+            piece = self.group(chunk, at_seq)
+            copies.append(self.copy(index, 6 + i, piece, piece, self.seq ^ CORES, self.fsdp))
+        return copies
+
+    def along(self, index, chunk):
+        for copy in self.line(index, chunk):
+            copy.start()
+
+    def first(self, index, chunk):
+        for copy in self.line(index, chunk):
+            copy.wait_recv()
+        over = self.over(index, chunk)
+        over[0].start()
+        over[1].start()
+        self.across(index, chunk)[0].start()
+
+    def second(self, index, chunk):
+        over = self.over(index, chunk)
+        over[0].wait_recv()
+        over[2].start()
+        self.across(index, chunk)[1].start()
+
+    def third(self, index, chunk):
+        over, across = self.over(index, chunk), self.across(index, chunk)
+        over[1].wait_recv()
+        across[2].start()
+        over[2].wait_recv()
+        across[3].start()
+
+    def finish(self, index, chunk):
+        for copy in self.across(index, chunk):
+            copy.wait_recv()
+
+    def drain(self, index, chunk):
+        for copy in self.line(index, chunk) + self.over(index, chunk) + self.across(index, chunk):
+            copy.wait_send()
+
+
+class Exchange:
+    def __init__(self, depth, heads):
+        self.depth, self.heads = depth, heads
+        self.seq, self.fsdp = place_here()
+        self.me = self.seq * depth + self.fsdp
+        self.core, self.half = lax.rem(self.seq, 2), lax.div(self.seq, 4)
+        self.head = lax.div(self.seq, 2) * depth + self.fsdp
+        self.same = (self.half == self.core).astype(jnp.int32)
+
+    def holder(self, k):
+        return lax.div(k, self.depth) * 2 + self.half, lax.rem(k, self.depth)
+
+    def owner(self, k):
+        block = self.core * self.heads + k
+        return lax.div(block, self.depth), lax.rem(block, self.depth)
+
+    def away_head(self, k):
+        return (k != self.head) | (self.half != self.core)
+
+    def away_block(self, k):
+        return self.core * self.heads + k != self.me
+
+    def greet_holders(self, barrier):
+        @pl.loop(0, self.heads)
+        def _(k):
+            @pl.when(self.away_head(k))
+            def _():
+                greet(barrier, *self.holder(k))
+
+        return self.heads - self.same
+
+    def greet_owners(self, barrier):
+        @pl.loop(0, self.heads)
+        def _(k):
+            @pl.when(self.away_block(k))
+            def _():
+                greet(barrier, *self.owner(k))
+
+        return self.heads - self.same
+
+
+def as_matrix(block):
+    return block.reshape(-1, block.shape[-1])
+
+
+def turned(block, tile=256):
+    return block.astype(float_type).T.astype(narrow_type)
+
+
+def rows_of_vectors(ve, target):
+    flat = as_matrix(ve[:, 0:32, :]).astype(float_type)
+    target[...] = flat.T[0:16]
+
+
+def attention_in_kernel(
+    depth,
+    halo,
+    heads,
+    chunks,
+    tok_ref,
+    sel_ref,
+    wqkv,
+    wout,
+    a_att,
+    b_att,
+    a_exp,
+    b_con,
+    w2,
+    a_con,
+    b_exp,
+    vec,
+    fa_out,
+    ve_out,
+    f2,
+    y_ref,
+    rank_ref,
+    fa,
+    ve,
+    proj,
+    normed,
+    vectors,
+    send,
+    receive,
+    local,
+    piece_send,
+    piece_receive,
+    piece_local,
+):
+    gather, swap = Gather(depth, send, receive), Exchange(depth, heads)
+    me, seq, fsdp = swap.me, swap.seq, swap.fsdp
+    core, half, head, own = swap.core, swap.half, swap.head, heads
+    features = normed.shape[1]
+    wide = features + 256
+    barrier = pltpu.get_barrier_semaphore()
+    greet_neighbours(barrier, seq, fsdp, depth)
+    waits = 3 + depth - 1 + swap.greet_owners(barrier)
+    places = [(vec, ve.at[me])]
+    for p in range(4):
+        source = wqkv.at[:, pl.ds(p * features, features)] if p < 3 else wout
+        places.append((source, fa.at[me, :, pl.ds(p * wide, features)]))
+        places.append((a_att.at[p], fa.at[me, :, pl.ds(p * wide + features, 128)]))
+        places.append((b_att.at[p], fa.at[me, :, pl.ds(p * wide + features + 128, 128)]))
+    places.append((a_exp, fa.at[me, :, pl.ds(4 * wide, 128)]))
+    places.append((b_con, fa.at[me, :, pl.ds(4 * wide + 128, 128)]))
+    places.append((w2, f2.at[me, :, pl.ds(0, features)]))
+    places.append((a_con, f2.at[me, :, pl.ds(features, 128)]))
+    places.append((b_exp, f2.at[me, :, pl.ds(features + 128, 128)]))
+    placed = [pltpu.make_async_copy(a, b, local.at[i]) for i, (a, b) in enumerate(places)]
+    for copy in placed:
+        copy.start()
+    for copy in placed:
+        copy.wait()
+    refs = {"ve": ve, "fa": fa, "f2": f2}
+    chunks = [(refs[name], rows, columns, flip) for name, rows, columns, flip in chunks]
+    pl.semaphore_wait(barrier, waits)
+    for index, chunk in enumerate(chunks):
+        gather.along(index, chunk)
+    base = core * (own - halo)
+    slot = me - half * (own - halo)
+
+    def piece(p, k):
+        return remote(
+            proj.at[p, k],
+            y_ref.at[slot, p],
+            piece_send.at[p, k],
+            piece_receive.at[p, lax.rem(me, own)],
+            *swap.holder(k),
+        )
+
+    def arrival(p, k):
+        return remote(
+            proj.at[p, 0],
+            y_ref.at[core * own + k - base, p],
+            piece_send.at[p, k],
+            piece_receive.at[p, k],
+            seq ^ CORES,
+            fsdp,
+        )
+
+    def kept(p):
+        return pltpu.make_async_copy(proj.at[p, head], y_ref.at[me - base, p], piece_local.at[p])
+
+    def norm():
+        rows_of_vectors(ve, vectors)
+        rows = tok_ref[...].astype(float_type)
+        normed[...] = layer_norm(rows, vectors[0:1], vectors[4:5])[0].astype(narrow_type)
+
+    def project(p):
+        down = as_matrix(fa[:, :, p * wide + features : p * wide + features + 128])
+        rank = (matmul(normed[...], down) * sel_ref[...]).astype(narrow_type)
+        rank_ref[p] = rank
+
+        @pl.loop(0, features // 256)
+        def _(j):
+            weight = as_matrix(fa[:, :, pl.ds(pl.multiple_of(p * wide + j * 256, 128), 256)])
+            up = as_matrix(fa[pl.ds(j * 8, 8), :, p * wide + features + 128 : (p + 1) * wide])
+            result = matmul(normed[...], weight) + transposed_right(rank, up)
+            if p == 0:
+                result = result + vectors[5:6, pl.ds(pl.multiple_of(j * 256, 128), 256)]
+            proj[p, pl.ds(j * 4, 4)] = result.T.astype(narrow_type).reshape(4, 64, 256)
+
+            @pl.loop(0, 4)
+            def _(i):
+                k = j * 4 + i
+
+                @pl.when(swap.away_head(k))
+                def _():
+                    piece(p, k).start()
+
+        @pl.when(half == core)
+        def _():
+            kept(p).start()
+
+    after = {0: norm, 2: lambda: project(0), 4: lambda: project(1), 6: lambda: project(2)}
+    after_attention = [i for i, chunk in enumerate(chunks) if chunk[0] is fa][-1]
+    outs = [
+        pltpu.make_async_copy(fa, fa_out, local.at[0]),
+        pltpu.make_async_copy(ve, ve_out, local.at[1]),
+    ]
+
+    def store():
+        for copy in outs:
+            copy.start()
+
+    for turn in range(len(chunks) + 3):
+        for delay, step in enumerate((gather.first, gather.second, gather.third, gather.finish)):
+            index = turn - delay
+            if 0 <= index < len(chunks):
+                step(index, chunks[index])
+                if delay == 3:
+                    after.get(index, lambda: None)()
+                    if index == after_attention:
+                        store()
+
+    @pl.loop(0, own)
+    def _(k):
+        @pl.when(swap.away_block(k))
+        def _():
+            for p in range(3):
+                arrival(p, k).wait_recv()
+
+    @pl.when(half == core)
+    def _():
+        for p in range(3):
+            kept(p).wait()
+
+    first = jnp.where(core == 0, own - halo, own)
+    over = remote(
+        y_ref.at[pl.ds(first - base, halo), 1:3],
+        y_ref.at[pl.ds(first - (own - halo) * (1 - core), halo), 1:3],
+        piece_send.at[3, 0],
+        piece_receive.at[3, 0],
+        seq ^ CORES,
+        fsdp,
+    )
+    over.start()
+    over.wait()
+
+    @pl.loop(0, heads)
+    def _(k):
+        @pl.when(swap.away_head(k))
+        def _():
+            for p in range(3):
+                piece(p, k).wait_send()
+
+    for index, chunk in enumerate(chunks):
+        gather.drain(index, chunk)
+    for copy in outs:
+        copy.wait()
+
+
+def attention_in(tokens, select, arrays, halo, depth, heads, devices, collective):
+    rows, features = tokens.shape
+    wide = features + 256
+    total = 4 * wide + 256
+    share, hidden_share = features // devices, arrays[6].shape[0]
+    chunks = [("ve", slice(0, 48), slice(0, 128), 0)]
+    for p in range(3):
+        chunks.append(("fa", slice(0, share), slice(p * wide, p * wide + wide // 2), 0))
+        chunks.append(("fa", slice(0, share), slice(p * wide + wide // 2, (p + 1) * wide), 1))
+    middle = 3 * wide + (total - 3 * wide) // 2
+    chunks.append(("fa", slice(0, share), slice(3 * wide, middle), 0))
+    chunks.append(("fa", slice(0, share), slice(middle, total), 1))
+    for part in range(0, hidden_share, 32):
+        chunks.append(("f2", slice(part, part + 32), slice(0, wide // 2), 0))
+        chunks.append(("f2", slice(part, part + 32), slice(wide // 2, wide), 1))
+    copies = Gather.STEPS * len(chunks)
+    return pl.pallas_call(
+        functools.partial(attention_in_kernel, depth, halo, heads, chunks),
+        out_shape=(
+            jax.ShapeDtypeStruct((devices, share, total), narrow_type),
+            jax.ShapeDtypeStruct((devices, 48, 128), narrow_type),
+            jax.ShapeDtypeStruct((devices, hidden_share, wide), narrow_type),
+            jax.ShapeDtypeStruct((heads + halo, 3, features // heads, rows), narrow_type),
+            jax.ShapeDtypeStruct((3, rows, 128), narrow_type),
+        ),
+        in_specs=[IN_VMEM, IN_VMEM] + [ANYWHERE] * len(arrays),
+        out_specs=(ANYWHERE, ANYWHERE, ANYWHERE, ANYWHERE, IN_VMEM),
+        scratch_shapes=[
+            pltpu.VMEM((devices, share, total), narrow_type),
+            pltpu.VMEM((devices, 48, 128), narrow_type),
+            pltpu.VMEM((3, heads, features // heads, rows), narrow_type),
+            pltpu.VMEM((rows, features), narrow_type),
+            pltpu.VMEM((16, features), float_type),
+            pltpu.SemaphoreType.DMA((copies,)),
+            pltpu.SemaphoreType.DMA((copies,)),
+            pltpu.SemaphoreType.DMA((20,)),
+            pltpu.SemaphoreType.DMA((4, heads)),
+            pltpu.SemaphoreType.DMA((4, heads)),
+            pltpu.SemaphoreType.DMA((3,)),
+        ],
+        compiler_params=pltpu.CompilerParams(
+            collective_id=collective, has_side_effects=True, vmem_limit_bytes=48 << 20
+        ),
+    )(tokens, select, *arrays)
+
+
+HIDDEN_TILE = 512
+
+
+def middle_kernel(
+    depth,
+    heads,
+    att_ref,
+    tok_ref,
+    cot_ref,
+    sel_ref,
+    fa_in,
+    ve,
+    f2_in,
+    w1,
+    result_ref,
+    gm_ref,
+    terms,
+    gy_ref,
+    fa,
+    f2,
+    f1,
+    att_t,
+    att,
+    gatt_t,
+    vectors,
+    hidden_bias,
+    middle,
+    normal,
+    normed,
+    branch,
+    grad_branch,
+    grad_normed,
+    ranks,
+    rank_sums,
+    send,
+    receive,
+    local,
+    a_send,
+    a_receive,
+    b_send,
+    b_receive,
+    own_local,
+):
+    gather, swap = Gather(depth, send, receive), Exchange(depth, heads)
+    me, seq, fsdp = swap.me, swap.seq, swap.fsdp
+    core, half, head, own = swap.core, swap.half, swap.head, heads
+    devices, share = f1.shape[0], f1.shape[1]
+    row_count, features = tok_ref.shape
+    wide = features + 256
+    tiles = f1.shape[2] // HIDDEN_TILE
+    in_tile = HIDDEN_TILE // f2.shape[1]
+    barrier = pltpu.get_barrier_semaphore()
+    greet_neighbours(barrier, seq, fsdp, depth)
+    waits = 3 + depth - 1 + swap.greet_owners(barrier) + swap.greet_holders(barrier)
+    loads = [
+        pltpu.make_async_copy(w1, f1.at[me], local.at[0]),
+        pltpu.make_async_copy(fa_in.at[:, :, pl.ds(3 * wide, wide + 256)], fa, local.at[1]),
+        pltpu.make_async_copy(f2_in, f2, local.at[2]),
+    ]
+    for copy in loads:
+        copy.start()
+    loads[0].wait()
+    pl.semaphore_wait(barrier, waits)
+
+    def attended_piece(k):
+        return remote(att_ref.at[k], att_t.at[head], a_send.at[k], a_receive.at[head], *swap.owner(k))
+
+    def attended_arrival(k):
+        return remote(att_ref.at[0], att_t.at[k], a_send.at[k], a_receive.at[k], seq ^ CORES, fsdp)
+
+    attended_kept = pltpu.make_async_copy(att_ref.at[me - core * own], att_t.at[head], own_local.at[0])
+
+    @pl.when(half == core)
+    def _():
+        attended_kept.start()
+
+    @pl.loop(0, own)
+    def _(step):
+        k = lax.rem(step + me, own)
+
+        @pl.when(swap.away_block(k))
+        def _():
+            attended_piece(k).start()
+
+    def chunk(c):
+        flip = c % 2 if isinstance(c, int) else lax.rem(c, 2)
+        start = c * HIDDEN_TILE if isinstance(c, int) else pl.multiple_of(c * HIDDEN_TILE, 128)
+        return (f1, slice(0, share), pl.ds(start, HIDDEN_TILE), flip)
+
+    @pl.loop(0, tiles)
+    def _(c):
+        gather.along(c, chunk(c))
+
+    rows_of_vectors(ve, vectors)
+    for d in range(devices):
+        hidden_bias[:, d * 128 : (d + 1) * 128] = ve[d, 32:48, :].astype(float_type)[0:8]
+    grad_branch[...] = (vectors[3:4] * cot_ref[...].astype(float_type)).astype(narrow_type)
+    loads[1].wait()
+    contract_up = as_matrix(fa[:, :, wide + 128 : wide + 256])
+    ranks[1] = (matmul(grad_branch[...], contract_up) * sel_ref[...]).astype(narrow_type)
+    branch[...] = jnp.zeros_like(branch)
+    grad_normed[...] = jnp.zeros_like(grad_normed)
+    rank_sums[...] = jnp.zeros_like(rank_sums)
+
+    gather.first(0, chunk(0))
+    gather.first(1, chunk(1))
+    gather.second(0, chunk(0))
+    gather.first(2, chunk(2))
+    gather.second(1, chunk(1))
+    gather.third(0, chunk(0))
+
+    @pl.loop(0, heads)
+    def _(k):
+        @pl.when(swap.away_head(k))
+        def _():
+            attended_arrival(k).wait_recv()
+
+    @pl.when(half == core)
+    def _():
+        attended_kept.wait()
+
+    for j in range(4):
+        att[:, j * 256 : (j + 1) * 256] = turned(as_matrix(att_t[4 * j : 4 * j + 4]))
+    out_down = as_matrix(fa[:, :, features : features + 128])
+    rank_out = (matmul(att[...], out_down) * sel_ref[...]).astype(narrow_type)
+    ranks[2] = rank_out
+
+    @pl.loop(0, 4)
+    def _(j):
+        at = pl.ds(pl.multiple_of(j * 256, 128), 256)
+        weight = as_matrix(fa[:, :, at])
+        up = as_matrix(fa[pl.ds(j * 8, 8), :, features + 128 : wide])
+        mixed = matmul(att[...], weight) + transposed_right(rank_out, up) + vectors[6:7, at]
+        middle[:, at] = tok_ref[:, at].astype(float_type) + vectors[1:2, at] * mixed
+
+    shifted, normal_rows, scaling = layer_norm(middle[...], vectors[2:3], vectors[7:8])
+    normal[...] = normal_rows
+    normed[...] = shifted.astype(narrow_type)
+    expand_down = as_matrix(fa[:, :, wide : wide + 128])
+    rank_expand = (matmul(normed[...], expand_down) * sel_ref[...]).astype(narrow_type)
+    ranks[0] = rank_expand
+    ranks[3, 0:128] = turned(rank_expand)[:, 0:128]
+    ranks[3, 128:256] = turned(rank_expand)[:, 128:256]
+    ranks[4, 0:128] = turned(ranks[1])[:, 0:128]
+    ranks[4, 128:256] = turned(ranks[1])[:, 128:256]
+    loads[2].wait()
+
+    def hidden(c):
+        at = pl.ds(pl.multiple_of(c * HIDDEN_TILE, 128), HIDDEN_TILE)
+        slots = pl.ds(c * in_tile, in_tile)
+        expand = as_matrix(f1[:, :, at])
+        contract = as_matrix(f2[slots, :, 0:features])
+        down = as_matrix(f2[slots, :, features : features + 128])
+        up = as_matrix(f2[slots, :, features + 128 : wide])
+        before = matmul(normed[...], expand) + transposed_right(ranks[0], up) + hidden_bias[0:1, at]
+        total = 0.5 * (1.0 + lax.erf(before * 0.7071067811865476))
+        density = jnp.exp(-0.5 * before * before) * 0.3989422804014327
+        active = (before * total).astype(narrow_type)
+        slope = total + before * density
+        branch[...] += matmul(active, contract)
+        rank_sums[0] += matmul(active, down)
+        grad_active = transposed_right(grad_branch[...], contract) + transposed_right(ranks[1], down)
+        grad_hidden = (grad_active * slope).astype(narrow_type)
+        rank_sums[1] += matmul(grad_hidden, up)
+        grad_normed[...] += transposed_right(grad_hidden, expand)
+        turned_expand = jnp.concatenate([ranks[3, 0:128], ranks[3, 128:256]], axis=1)
+        turned_contract = jnp.concatenate([ranks[4, 0:128], ranks[4, 128:256]], axis=1)
+        grad_up = matmul(turned_expand, grad_hidden).astype(narrow_type)
+        grad_down = matmul(turned_contract, active).astype(narrow_type)
+        for i in range(in_tile):
+            terms[c * in_tile + i, 96:224] = grad_up[:, i * 128 : (i + 1) * 128]
+            terms[c * in_tile + i, 224:352] = grad_down[:, i * 128 : (i + 1) * 128]
+
+    @pl.loop(3, tiles + 3)
+    def _(turn):
+        @pl.when(turn < tiles)
+        def _():
+            gather.first(turn, chunk(turn))
+
+        @pl.when(turn - 1 < tiles)
+        def _():
+            gather.second(turn - 1, chunk(turn - 1))
+
+        @pl.when(turn - 2 < tiles)
+        def _():
+            gather.third(turn - 2, chunk(turn - 2))
+
+        gather.finish(turn - 3, chunk(turn - 3))
+        hidden(turn - 3)
+
+    rank_contract = (rank_sums[0] * sel_ref[...]).astype(narrow_type)
+    grad_rank_expand = (rank_sums[1] * sel_ref[...]).astype(narrow_type)
+    gradient = grad_normed[...] + transposed_right(grad_rank_expand, expand_down)
+    gm_ref[...] = cot_ref[...].astype(float_type) + norm_backward(gradient, vectors[2:3], normal[...], scaling)
+    grad_mixed = (vectors[1:2] * gm_ref[...]).astype(narrow_type)
+    out_up = as_matrix(fa[:, :, features + 128 : wide])
+    grad_rank_out = (matmul(grad_mixed, out_up) * sel_ref[...]).astype(narrow_type)
+
+    def gradient_piece(k):
+        return remote(
+            gatt_t.at[k], gy_ref.at[lax.rem(me, own)], b_send.at[k], b_receive.at[lax.rem(me, own)], *swap.holder(k)
+        )
+
+    def gradient_arrival(k):
+        return remote(gatt_t.at[0], gy_ref.at[k], b_send.at[k], b_receive.at[k], seq ^ CORES, fsdp)
+
+    gradient_kept = pltpu.make_async_copy(gatt_t.at[head], gy_ref.at[lax.rem(me, own)], own_local.at[1])
+
+    @pl.loop(0, 4)
+    def _(j):
+        slots = pl.ds(j * 8, 8)
+        weight = as_matrix(fa[slots, :, 0:features])
+        down = as_matrix(fa[slots, :, features : features + 128])
+        rows = transposed_right(grad_mixed, weight) + transposed_right(grad_rank_out, down)
+        gatt_t[pl.ds(j * 4, 4)] = rows.T.astype(narrow_type).reshape(4, 64, 256)
+
+        @pl.loop(0, 4)
+        def _(i):
+            k = j * 4 + i
+
+            @pl.when(swap.away_head(k))
+            def _():
+                gradient_piece(k).start()
+
+    @pl.when(half == core)
+    def _():
+        gradient_kept.start()
+
+    up_rows = transposed_right(rank_contract, contract_up)
+    result_ref[...] = (
+        middle[...] + vectors[3:4] * (branch[...] + vectors[8:9] + up_rows)
+    ).astype(narrow_type)
+    shaped = (devices, share, 128)
+    terms[:, 0:32] = matmul(as_matrix(att_t[...]), grad_rank_out).astype(narrow_type).reshape(shaped)
+    terms[:, 32:64] = transposed_left(grad_mixed, rank_out).astype(narrow_type).reshape(shaped)
+    terms[:, 64:96] = transposed_left(normed[...], grad_rank_expand).astype(narrow_type).reshape(shaped)
+    terms[:, 352:384] = transposed_left(grad_branch[...], rank_contract).astype(narrow_type).reshape(shaped)
+
+    @pl.loop(0, own)
+    def _(k):
+        @pl.when(swap.away_block(k))
+        def _():
+            gradient_arrival(k).wait_recv()
+            attended_piece(k).wait_send()
+
+    @pl.when(half == core)
+    def _():
+        gradient_kept.wait()
+
+    @pl.loop(0, heads)
+    def _(k):
+        @pl.when(swap.away_head(k))
+        def _():
+            gradient_piece(k).wait_send()
+
+    @pl.loop(0, tiles)
+    def _(c):
+        gather.drain(c, chunk(c))
+
+
+def middle_part(att, tokens, cotangent, select, fa, ve, f2, w1, depth, collective):
+    heads, width, rows = att.shape
+    features = tokens.shape[1]
+    wide = features + 256
+    devices, hidden_share = f2.shape[0], f2.shape[1]
+    share, hidden_total = w1.shape
+    copies = Gather.STEPS * (hidden_total // HIDDEN_TILE)
+
+    def wide_rows():
+        return pltpu.VMEM((rows, features), float_type)
+
+    def narrow_rows():
+        return pltpu.VMEM((rows, features), narrow_type)
+
+    return pl.pallas_call(
+        functools.partial(middle_kernel, depth, heads),
+        out_shape=(
+            jax.ShapeDtypeStruct((rows, features), narrow_type),
+            jax.ShapeDtypeStruct((rows, features), float_type),
+            jax.ShapeDtypeStruct((devices, 384, 128), narrow_type),
+            jax.ShapeDtypeStruct((heads, width, rows), narrow_type),
+        ),
+        in_specs=[IN_VMEM, IN_VMEM, IN_VMEM, IN_VMEM, ANYWHERE, IN_VMEM, ANYWHERE, ANYWHERE],
+        out_specs=(IN_VMEM, IN_VMEM, IN_VMEM, ANYWHERE),
+        scratch_shapes=[
+            pltpu.VMEM((devices, share, wide + 256), narrow_type),
+            pltpu.VMEM(f2.shape, narrow_type),
+            pltpu.VMEM((devices, share, hidden_total), narrow_type),
+            pltpu.VMEM((heads, width, rows), narrow_type),
+            narrow_rows(),
+            pltpu.VMEM((heads, width, rows), narrow_type),
+            pltpu.VMEM((16, features), float_type),
+            pltpu.VMEM((8, hidden_total), float_type),
+            wide_rows(),
+            wide_rows(),
+            narrow_rows(),
+            wide_rows(),
+            narrow_rows(),
+            wide_rows(),
+            pltpu.VMEM((5, rows, 128), narrow_type),
+            pltpu.VMEM((2, rows, 128), float_type),
+            pltpu.SemaphoreType.DMA((copies,)),
+            pltpu.SemaphoreType.DMA((copies,)),
+            pltpu.SemaphoreType.DMA((3,)),
+            pltpu.SemaphoreType.DMA((heads,)),
+            pltpu.SemaphoreType.DMA((heads,)),
+            pltpu.SemaphoreType.DMA((heads,)),
+            pltpu.SemaphoreType.DMA((heads,)),
+            pltpu.SemaphoreType.DMA((2,)),
+        ],
+        compiler_params=pltpu.CompilerParams(
+            collective_id=collective, has_side_effects=True, vmem_limit_bytes=60 << 20
+        ),
+    )(att, tokens, cotangent, select, fa, ve, f2, w1)
+
+
+class Reduce:
+    COPIES = 16
+
+    def __init__(self, depth, base, terms, first, second, third, fourth, send, receive):
+        self.depth, self.base, self.terms = depth, base, terms
+        self.buffers = first, second, third, fourth
+        self.send, self.receive = send, receive
+        self.seq, self.fsdp = place_here()
+        self.core, self.x, self.y = lax.rem(self.seq, 2), lax.rem(lax.div(self.seq, 2), 2), lax.div(self.seq, 4)
+        half = terms.shape[1] // 2
+        self.halves = (slice(0, half), slice(half, 2 * half))
+
+    def copy(self, step, source, target, seq, fsdp):
+        at = self.base + step
+        return remote(source, target, self.send.at[at], self.receive.at[at], seq, fsdp)
+
+    def to_core(self):
+        first = self.buffers[0]
+        lines = [self.terms.at[pl.ds((2 * t + 1 - self.core) * self.depth, self.depth)] for t in range(4)]
+        return [self.copy(t, lines[t], first.at[t], self.seq ^ CORES, self.fsdp) for t in range(4)]
+
+    def to_sides(self):
+        first, second = self.buffers[:2]
+        x, y = self.x, self.y
+        copies = []
+        for j in range(2):
+            copies.append(
+                self.copy(
+                    4 + j,
+                    first.at[2 * j + 1 - x, :, self.halves[0]],
+                    second.at[0, j],
+                    self.seq ^ SIDE_X,
+                    self.fsdp,
+                )
+            )
+            copies.append(
+                self.copy(
+                    6 + j,
+                    first.at[2 * (1 - y) + j, :, self.halves[1]],
+                    second.at[1, j],
+                    self.seq ^ SIDE_Y,
+                    self.fsdp,
+                )
+            )
+        return copies
+
+    def to_corner(self):
+        second, third = self.buffers[1:3]
+        return [
+            self.copy(8, second.at[0, 1 - self.y], third.at[0], self.seq ^ SIDE_Y, self.fsdp),
+            self.copy(9, second.at[1, 1 - self.x], third.at[1], self.seq ^ SIDE_X, self.fsdp),
+        ]
+
+    def to_line(self):
+        third, fourth = self.buffers[2:]
+        copies = []
+        for step in range(1, self.depth):
+            to = lax.rem(self.fsdp + step, self.depth)
+            for j in range(2):
+                copies.append(
+                    self.copy(8 + 2 * step + j, third.at[j, to], fourth.at[j, step], self.seq, to)
+                )
+        return copies
+
+    def add(self, target, other):
+        @pl.loop(0, self.depth)
+        def _(i):
+            target[i] = (target[i].astype(float_type) + other[i].astype(float_type)).astype(narrow_type)
+
+    def begin(self):
+        for copy in self.to_core():
+            copy.start()
+
+    def sides(self):
+        first = self.buffers[0]
+        for t, copy in enumerate(self.to_core()):
+            copy.wait_recv()
+            self.add(first.at[t], self.terms.at[pl.ds((2 * t + self.core) * self.depth, self.depth)])
+        for copy in self.to_sides():
+            copy.start()
+
+    def corner(self):
+        first, second = self.buffers[:2]
+        copies = self.to_sides()
+        for j in range(2):
+            copies[2 * j].wait_recv()
+            self.add(second.at[0, j], first.at[2 * j + self.x, :, self.halves[0]])
+            copies[2 * j + 1].wait_recv()
+            self.add(second.at[1, j], first.at[2 * self.y + j, :, self.halves[1]])
+        for copy in self.to_corner():
+            copy.start()
+
+    def line(self):
+        second, third = self.buffers[1:3]
+        copies = self.to_corner()
+        copies[0].wait_recv()
+        self.add(third.at[0], second.at[0, self.y])
+        copies[1].wait_recv()
+        self.add(third.at[1], second.at[1, self.x])
+        for copy in self.to_line():
+            copy.start()
+
+    def end(self, out):
+        third, fourth = self.buffers[2:]
+        for copy in self.to_line():
+            copy.wait_recv()
+        for j in range(2):
+            total = third[j, self.fsdp].astype(float_type)
+            for step in range(1, self.depth):
+                total = total + fourth[j, step].astype(float_type)
+            out[self.halves[j]] = total
+
+    def drain(self):
+        for copy in self.to_core() + self.to_sides() + self.to_corner() + self.to_line():
+            copy.wait_send()
+
+
+def last_kernel(
+    depth,
+    heads,
+    halo,
+    dx_ref,
+    dh_ref,
+    tok_ref,
+    gm_ref,
+    sel_ref,
+    fa_in,
+    ve,
+    rank_ref,
+    early_terms,
+    gradient_ref,
+    early_ref,
+    late_ref,
+    fa,
+    vectors,
+    normed,
+    total,
+    arrived,
+    arrived_rows,
+    merged,
+    other,
+    late_terms,
+    early_buffers,
+    late_buffers,
+    send,
+    receive,
+    local,
+    piece_send,
+    piece_receive,
+    piece_local,
+):
+    swap = Exchange(depth, heads)
+    me, seq, fsdp = swap.me, swap.seq, swap.fsdp
+    core, half, head, own = swap.core, swap.half, swap.head, heads
+    row_count, features = tok_ref.shape
+    devices, share = fa.shape[0], fa.shape[1]
+    wide = features + 256
+    barrier = pltpu.get_barrier_semaphore()
+    greet_neighbours(barrier, seq, fsdp, depth)
+    waits = 3 + depth - 1 + swap.greet_holders(barrier)
+    load = pltpu.make_async_copy(fa_in.at[:, :, pl.ds(0, 3 * wide)], fa, local.at[0])
+    load.start()
+    pl.semaphore_wait(barrier, waits)
+    over = remote(dh_ref, other, piece_send.at[3, 0], piece_receive.at[3, 0], seq ^ CORES, fsdp)
+    over.start()
+    early = Reduce(depth, 0, early_terms, *early_buffers, send, receive)
+    late = [
+        Reduce(
+            depth, Reduce.COPIES * (p + 1), late_terms.at[p], *[b.at[p] for b in late_buffers], send, receive
+        )
+        for p in range(3)
+    ]
+    shared = jnp.where(core == 0, own - halo, 0)
+
+    def in_shared(k):
+        return (k >= shared) & (k < shared + halo)
+
+    def sent(p, k, source):
+        return remote(
+            source, arrived.at[p, head], piece_send.at[p, k], piece_receive.at[p, head], *swap.owner(k)
+        )
+
+    def launch(p, k, source):
+        @pl.when(swap.away_block(k))
+        def _():
+            sent(p, k, source).start()
+
+        @pl.when(core * own + k == me)
+        def _():
+            pltpu.make_async_copy(source, arrived.at[p, head], piece_local.at[p]).start()
+
+    def arrival(p, k):
+        return remote(
+            dx_ref.at[0, 0], arrived.at[p, k], piece_send.at[p, k], piece_receive.at[p, k], seq ^ CORES, fsdp
+        )
+
+    @pl.loop(0, own)
+    def _(step):
+        k = lax.rem(step + me, own)
+        launch(0, k, dx_ref.at[k, 0])
+
+    over.wait_recv()
+
+    @pl.loop(0, halo)
+    def _(i):
+        for part in range(2):
+            merged[i, part] = (
+                dx_ref[shared + i, 1 + part].astype(float_type) + other[i, part].astype(float_type)
+            ).astype(narrow_type)
+
+    for p in (1, 2):
+
+        @pl.loop(0, own)
+        def _(step, p=p):
+            k = lax.rem(step + me, own)
+
+            @pl.when(in_shared(k))
+            def _():
+                launch(p, k, merged.at[jnp.clip(k - shared, 0, halo - 1), p - 1])
+
+            @pl.when(jnp.logical_not(in_shared(k)))
+            def _():
+                launch(p, k, dx_ref.at[k, p])
+
+    early.begin()
+    rows_of_vectors(ve, vectors)
+    early.sides()
+    shifted, normal, scaling = layer_norm(tok_ref[...].astype(float_type), vectors[0:1], vectors[4:5])
+    normed[...] = shifted.astype(narrow_type)
+    early.corner()
+    load.wait()
+
+    def gather_part(p):
+        @pl.loop(0, heads)
+        def _(k):
+            @pl.when(swap.away_head(k))
+            def _():
+                arrival(p, k).wait_recv()
+
+        @pl.when(half == core)
+        def _():
+            pltpu.make_async_copy(dx_ref.at[0, p], arrived.at[p, head], piece_local.at[p]).wait()
+
+    def project_back(p):
+        for j in range(4):
+            arrived_rows[:, j * 256 : (j + 1) * 256] = turned(as_matrix(arrived[p, 4 * j : 4 * j + 4]))
+        up = as_matrix(fa[:, :, p * wide + features + 128 : (p + 1) * wide])
+        grad_rank = (matmul(arrived_rows[...], up) * sel_ref[...]).astype(narrow_type)
+
+        @pl.loop(0, 4)
+        def _(j):
+            at = pl.ds(pl.multiple_of(j * 256, 128), 256)
+            slots = pl.ds(j * 8, 8)
+            weight = as_matrix(fa[slots, :, p * wide : p * wide + features])
+            down = as_matrix(fa[slots, :, p * wide + features : p * wide + features + 128])
+            term = transposed_right(arrived_rows[...], weight) + transposed_right(grad_rank, down)
+            if p == 0:
+                total[:, at] = term
+            else:
+                total[:, at] += term
+
+        shaped = (devices, share, 128)
+        late_terms[p, :, 0:32] = transposed_left(normed[...], grad_rank).astype(narrow_type).reshape(shaped)
+        late_terms[p, :, 32:64] = (
+            matmul(as_matrix(arrived[p]), rank_ref[p]).astype(narrow_type).reshape(shaped)
+        )
+
+    gather_part(0)
+    project_back(0)
+    late[0].begin()
+    early.line()
+    late[0].sides()
+    gather_part(1)
+    project_back(1)
+    late[1].begin()
+    late[0].corner()
+    late[1].sides()
+    gather_part(2)
+    project_back(2)
+    late[2].begin()
+    late[0].line()
+    late[1].corner()
+    late[2].sides()
+    gradient_ref[...] = gm_ref[...] + norm_backward(total[...], vectors[0:1], normal, scaling)
+    late[1].line()
+    late[2].corner()
+    early.end(early_ref)
+    late[0].end(late_ref.at[0])
+    late[2].line()
+    late[1].end(late_ref.at[1])
+    late[2].end(late_ref.at[2])
+    for reduce in [early] + late:
+        reduce.drain()
+
+    @pl.loop(0, own)
+    def _(k):
+        @pl.when(swap.away_block(k))
+        def _():
+            for p in range(3):
+                sent(p, k, dx_ref.at[k, p]).wait_send()
+
+    over.wait_send()
+
+
+def last_part(dx, dh, tokens, grad_middle, select, fa, ve, rank, terms, depth, collective):
+    heads = dx.shape[0]
+    halo = dh.shape[0]
+    rows, features = tokens.shape
+    wide = features + 256
+    devices, share = fa.shape[0], fa.shape[1]
+
+    def buffers(count, size):
+        return [
+            pltpu.VMEM(count + (4, depth, size, 128), narrow_type),
+            pltpu.VMEM(count + (2, 2, depth, size // 2, 128), narrow_type),
+            pltpu.VMEM(count + (2, depth, size // 2, 128), narrow_type),
+            pltpu.VMEM(count + (2, depth, size // 2, 128), narrow_type),
+        ]
+
+    return pl.pallas_call(
+        functools.partial(last_kernel, depth, heads, halo),
+        out_shape=(
+            jax.ShapeDtypeStruct((rows, features), float_type),
+            jax.ShapeDtypeStruct((terms.shape[1], 128), float_type),
+            jax.ShapeDtypeStruct((3, 2 * share, 128), float_type),
+        ),
+        in_specs=[IN_VMEM] * 5 + [ANYWHERE] + [IN_VMEM] * 3,
+        out_specs=(IN_VMEM, IN_VMEM, IN_VMEM),
+        scratch_shapes=[
+            pltpu.VMEM((devices, share, 3 * wide), narrow_type),
+            pltpu.VMEM((16, features), float_type),
+            pltpu.VMEM((rows, features), narrow_type),
+            pltpu.VMEM((rows, features), float_type),
+            pltpu.VMEM((3, heads, features // heads, rows), narrow_type),
+            pltpu.VMEM((rows, features), narrow_type),
+            pltpu.VMEM(dh.shape, narrow_type),
+            pltpu.VMEM(dh.shape, narrow_type),
+            pltpu.VMEM((3, devices, 2 * share, 128), narrow_type),
+            buffers((), terms.shape[1]),
+            buffers((3,), 2 * share),
+            pltpu.SemaphoreType.DMA((4 * Reduce.COPIES,)),
+            pltpu.SemaphoreType.DMA((4 * Reduce.COPIES,)),
+            pltpu.SemaphoreType.DMA((1,)),
+            pltpu.SemaphoreType.DMA((4, heads)),
+            pltpu.SemaphoreType.DMA((4, heads)),
+            pltpu.SemaphoreType.DMA((3,)),
+        ],
+        compiler_params=pltpu.CompilerParams(
+            collective_id=collective, has_side_effects=True, vmem_limit_bytes=56 << 20
+        ),
+    )(dx, dh, tokens, grad_middle, select, fa, ve, rank, terms)
+
+
+BIG = 32768.0
+
+
+def bounds(lens_ref, n, base_block, rows, i):
+    first=(base_block+i)*rows; last=first+rows-1
+    lo=jnp.int32(0); hi=jnp.int32(0); start=jnp.int32(0)
+    for m in range(n):
+        end=start+lens_ref[m]
+        lo=jnp.where((start<=first)&(first<end),start,lo)
+        hi=jnp.where((start<=last)&(last<end),end-1,hi)
+        start=end
+    return lax.div(lo,rows), lax.div(hi,rows)
+
+def image_marks(lens_ref, n, marks, rows):
+    r=lax.broadcasted_iota(jnp.int32,(marks,rows),0)
+    st=jnp.full((marks,rows),1<<30,jnp.int32); en=jnp.zeros((marks,rows),jnp.int32)
+    start=jnp.int32(0)
+    for m in range(n):
+        end=start+lens_ref[m]
+        st=jnp.where(r==m,start,st); en=jnp.where(r==m,end,en)
+        start=end
+    return st,en
+
+def fwd_kernel(n,own,slots,halo,rows,width,marks, lens_ref,x_ref,att_ref,lse_ref,o_ref,qa,ka):
+    core=lax.rem(lax.axis_index("seq"),2)
+    base=core*(own-halo)
+    shift=core*halo
+    st,en=image_marks(lens_ref,n,marks,rows)
+    pos=lax.broadcasted_iota(jnp.int32,(marks,rows),1)
+    def prep(s,_):
+        p=pos+(base+s)*rows
+        inside=(p>=st)&(p<en)
+        oh=jnp.where(inside,1.0,0.0).astype(float_type)
+        kt=jnp.concatenate([x_ref[s,1].astype(float_type),(oh-1.0)*BIG],axis=0)
+        ka[s]=kt.T.astype(narrow_type)
+        return 0
+    lax.fori_loop(0,slots,prep,0)
+    def one_q(i,_):
+        s_q=i+shift
+        p=pos+(base+s_q)*rows
+        oh=jnp.where((p>=st)&(p<en),1.0,0.0).astype(narrow_type)
+        q=jnp.concatenate([(x_ref[s_q,0].astype(float_type)*(width**-0.5)).astype(narrow_type),oh],axis=0)
+        lo,hi=bounds(lens_ref,n,base+shift,rows,i)
+        lo=lo-base; hi=hi-base
+        def tile(m,l,o,s):
+            sc=matmul(ka[s],q)
+            m2=jnp.maximum(m,jnp.max(sc,axis=0,keepdims=True))
+            pr=jnp.exp(sc-m2)
+            al=jnp.exp(m-m2)
+            return m2, l*al+jnp.sum(pr,axis=0,keepdims=True), o*al+matmul(x_ref[s,2],pr.astype(narrow_type))
+        def tile2(m,l,o,s):
+            sa=matmul(ka[s],q); sb=matmul(ka[s+1],q)
+            m2=jnp.maximum(m,jnp.maximum(jnp.max(sa,axis=0,keepdims=True),jnp.max(sb,axis=0,keepdims=True)))
+            pa=jnp.exp(sa-m2); pb=jnp.exp(sb-m2)
+            al=jnp.exp(m-m2)
+            l=l*al+jnp.sum(pa,axis=0,keepdims=True)+jnp.sum(pb,axis=0,keepdims=True)
+            return m2,l,o*al+matmul(x_ref[s,2],pa.astype(narrow_type))+matmul(x_ref[s+1,2],pb.astype(narrow_type))
+        m=jnp.full((1,rows),-1e30,float_type); l=jnp.zeros((1,rows),float_type); o=jnp.zeros((width,rows),float_type)
+        cnt=hi-lo+1
+        m,l,o=lax.fori_loop(0,cnt//2,lambda t,c: tile2(*c,lo+2*t),(m,l,o))
+        m,l,o=lax.fori_loop(0,cnt%2,lambda t,c: tile(*c,hi),(m,l,o))
+        o=o/l
+        att_ref[i]=o.astype(narrow_type)
+        o_ref[i]=o
+        lse_ref[i]=jnp.broadcast_to(m+jnp.log(l),(8,rows))
+        return 0
+    lax.fori_loop(0,own,one_q,0)
+
+def attention_forward(lengths,x,own,halo):
+    slots,_,width,rows=x.shape
+    n=lengths.shape[0]; marks=-(-n//16)*16
+    V=pl.BlockSpec(memory_space=pltpu.VMEM)
+    return pl.pallas_call(functools.partial(fwd_kernel,n,own,slots,halo,rows,width,marks),
+        out_shape=(jax.ShapeDtypeStruct((own,width,rows),narrow_type),jax.ShapeDtypeStruct((own,8,rows),float_type),jax.ShapeDtypeStruct((own,width,rows),float_type)),
+        in_specs=[pl.BlockSpec(memory_space=pltpu.SMEM),V],out_specs=(V,V,V),
+        scratch_shapes=[pltpu.VMEM((width+marks,rows),narrow_type),pltpu.VMEM((slots,rows,width+marks),narrow_type)],
+        compiler_params=pltpu.CompilerParams(vmem_limit_bytes=40<<20))(lengths,x)
+
+def bwd_kernel(n,own,slots,halo,rows,width,marks, lens_ref,x_ref,g_ref,lse_ref,o_ref,dx_ref,dh_ref,ka,vv,qa,qn,gn,dd,dq):
+    core=lax.rem(lax.axis_index("seq"),2)
+    base=core*(own-halo); shift=core*halo
+    st,en=image_marks(lens_ref,n,marks,rows)
+    pos=lax.broadcasted_iota(jnp.int32,(marks,rows),1)
+    def prep(s,_):
+        p=pos+(base+s)*rows
+        oh=jnp.where((p>=st)&(p<en),1.0,0.0).astype(float_type)
+        kt=jnp.concatenate([x_ref[s,1].astype(float_type),(oh-1.0)*BIG],axis=0)
+        ka[s]=kt.T.astype(narrow_type)
+        vv[s]=x_ref[s,2].astype(float_type).T.astype(narrow_type)
+        return 0
+    lax.fori_loop(0,slots,prep,0)
+    def prepq(i,_):
+        s=i+shift
+        p=pos+(base+s)*rows
+        oh=jnp.where((p>=st)&(p<en),1.0,0.0).astype(narrow_type)
+        qs=x_ref[s,0].astype(float_type)*(width**-0.5)
+        qa[i]=jnp.concatenate([qs.astype(narrow_type),oh],axis=0)
+        qn[i]=qs.T.astype(narrow_type)
+        g=g_ref[i].astype(float_type)
+        gn[i]=g.T.astype(narrow_type)
+        dd[i]=jnp.broadcast_to(jnp.sum(g*o_ref[i],axis=0,keepdims=True),(8,rows))
+        dq[i]=jnp.zeros((width,rows),float_type)
+        return 0
+    lax.fori_loop(0,own,prepq,0)
+    def one_k(s,_):
+        lo,hi=bounds(lens_ref,n,base,rows,s)
+        lo=jnp.maximum(lo-base-shift,0); hi=jnp.minimum(hi-base-shift,own-1)
+        kt=x_ref[s,1]
+        def tile(i,dk,dv):
+            sc=matmul(ka[s],qa[i])
+            pr=jnp.exp(sc-lse_ref[i][0:1])
+            dp=matmul(vv[s],g_ref[i])
+            ds=(pr*(dp-dd[i][0:1])).astype(narrow_type)
+            dq[i]+=matmul(kt,ds)
+            return dk+matmul(ds,qn[i]), dv+matmul(pr.astype(narrow_type),gn[i])
+        z=jnp.zeros((rows,width),float_type)
+        cnt=jnp.maximum(hi-lo+1,0)
+        def two(t,c):
+            c=tile(lo+2*t,*c)
+            return tile(lo+2*t+1,*c)
+        dk,dv=lax.fori_loop(0,cnt//2,two,(z,z))
+        dk,dv=lax.fori_loop(0,cnt%2,lambda t,c: tile(hi,*c),(dk,dv))
+        i=s-shift
+        @pl.when((i>=0)&(i<own))
+        def _():
+            dx_ref[i,1]=dk.T.astype(narrow_type)
+            dx_ref[i,2]=dv.T.astype(narrow_type)
+        @pl.when((i<0)|(i>=own))
+        def _():
+            j=jnp.where(i<0,s,i-own)
+            dh_ref[j,0]=dk.T.astype(narrow_type)
+            dh_ref[j,1]=dv.T.astype(narrow_type)
+        return 0
+    lax.fori_loop(0,slots,one_k,0)
+    def fin(i,_):
+        dx_ref[i,0]=(dq[i]*(width**-0.5)).astype(narrow_type)
+        return 0
+    lax.fori_loop(0,own,fin,0)
+
+def attention_backward(lengths,x,g,lse,o,own,halo):
+    slots,_,width,rows=x.shape
+    n=lengths.shape[0]; marks=-(-n//16)*16
+    V=pl.BlockSpec(memory_space=pltpu.VMEM)
+    return pl.pallas_call(functools.partial(bwd_kernel,n,own,slots,halo,rows,width,marks),
+        out_shape=(jax.ShapeDtypeStruct((own,3,width,rows),narrow_type),jax.ShapeDtypeStruct((halo,2,width,rows),narrow_type)),
+        in_specs=[pl.BlockSpec(memory_space=pltpu.SMEM),V,V,V,V],out_specs=(V,V),
+        scratch_shapes=[pltpu.VMEM((slots,rows,width+marks),narrow_type),pltpu.VMEM((slots,rows,width),narrow_type),
+          pltpu.VMEM((own,width+marks,rows),narrow_type),pltpu.VMEM((own,rows,width),narrow_type),pltpu.VMEM((own,rows,width),narrow_type),
+          pltpu.VMEM((own,8,rows),float_type),pltpu.VMEM((own,width,rows),float_type)],
+        compiler_params=pltpu.CompilerParams(vmem_limit_bytes=48<<20))(lengths,x,g,lse,o)
+
+
+def layer_on_slice(
+    tokens,
+    lengths,
+    adapter_choice,
+    gain_rows,
+    bias_rows,
+    query_key_value,
+    output_weight,
+    expand_weight,
+    expand_bias,
+    contract_weight,
+    adapter_in_attention,
+    adapter_out_attention,
+    adapter_in_expand,
+    adapter_out_expand,
+    adapter_in_contract,
+    adapter_out_contract,
+    cotangent,
+):
+    row_count, features = tokens.shape
+    depth = lax.axis_size("fsdp")
+    devices = lax.axis_size(("seq", "fsdp"))
+    position = lax.axis_index(("seq", "fsdp"))
+    own = devices // 2
+    head_width = features // HEADS
+    rank_width = adapter_in_attention.shape[2]
+    share = features // devices
+    halo = -(-(LONGEST - 1) // row_count)
+
+    vectors = jnp.concatenate([gain_rows.T, bias_rows.T], axis=1)
+    vectors = jnp.pad(vectors, ((0, 16), (0, rank_width - vectors.shape[1])))
+    vectors = lax.dynamic_update_slice(vectors, expand_bias[None], (share, 0))
+    arrays = (
+        query_key_value,
+        output_weight,
+        adapter_in_attention,
+        adapter_out_attention.transpose(0, 2, 1),
+        adapter_in_expand,
+        adapter_out_contract.T,
+        contract_weight,
+        adapter_in_contract,
+        adapter_out_expand.T,
+        vectors,
+    )
+    image_ends = jnp.cumsum(lengths)
+    places = position * row_count + jnp.arange(row_count, dtype=jnp.int32)
+    own_image = jnp.sum((places[:, None] >= image_ends[None, :]).astype(jnp.int32), axis=1)
+    matches = own_image[:, None] == jnp.arange(lengths.shape[0], dtype=jnp.int32)[None, :]
+    chosen = jnp.sum(jnp.where(matches, adapter_choice[None, :], 0), axis=1)
+    select = (jnp.arange(rank_width, dtype=jnp.int32)[None, :] // RANK == chosen[:, None]).astype(float_type)
+
+    fa, ve, f2, on_heads, rank = attention_in(tokens, select, arrays, halo, depth, HEADS, devices, 1)
+    attended, log_totals, attended_wide = attention_forward(lengths, on_heads, own, halo)
+    result, grad_middle, terms, grad_on_heads = middle_part(
+        attended, tokens, cotangent, select, fa, ve, f2, expand_weight, depth, 2
+    )
+    grad_blocks, grad_halo = attention_backward(
+        lengths, on_heads, grad_on_heads, log_totals, attended_wide, own, halo
+    )
+    input_gradient, early, late = last_part(
+        grad_blocks, grad_halo, tokens, grad_middle, select, fa, ve, rank, terms, depth, 3
+    )
+    down = jnp.concatenate([late[:, :share], early[None, :share]], axis=0)
+    up = jnp.concatenate([late[:, share:], early[None, share : 2 * share]], axis=0)
+    return (
+        result,
+        input_gradient,
+        down,
+        up.transpose(0, 2, 1),
+        early[64:96],
+        early[96:224],
+        early[224:352].T,
+        early[352:384].T,
+    )
+
+
 def solution(mesh):
+    per_device = layer_on_slice if dict(mesh.shape) == {"seq": 8, "fsdp": 4} else general_layer
     placed = (
         P(("seq", "fsdp"), None),
         P(),

time: 2280 us -> 386 us (0.17)
  waiting for transfers between devices: 1020 us -> 0 us
  blocking collectives: 707 us -> 0 us
  Pallas kernels: 0 us -> 359 us
  matrix products: 212 us -> 0 us
  local copies, waits for them, and re-layouts: 149 us -> 23.2 us
  starting transfers between devices: 72.9 us -> 0 us
  other arithmetic: 60.9 us -> 2.51 us
  loops' own time: 24.4 us -> 0 us
    all_gather x8 -> x0, blocking collectives: 707 us -> none  [the longest x1 121 us: per_device(): lax.all_gather(renewed[12], ('seq', 'fsdp'), axis=1, tiled=True)]
    reduce_scatter x4 -> x0, waiting for transfers between devices: 542 us -> none  [the longest x1 139 us: per_device(): lax.psum_scatter(grad_contract_down, ('seq', 'fsdp'), scatter_dimension=0...]
    pallas_call x0 -> x5, Pallas kernels: none -> 359 us  [the longest x1 129 us: attention_in(): pl.pallas_call(functools.partial(attention_in_kernel, depth, halo, heads,...]
    ppermute x24 -> x0, waiting for transfers between devices: 354 us -> none  [passed_along(): return lax.ppermute(block, axis, route)]
    dot_general x88 -> x0, matrix products: 212 us -> none  [the longest x16 47.5 us: pair_slices(): jnp.einsum('qhd,khd->hqk', query_part, key_part, preferred_element_type=f...]
    ppermute x24 -> x0, starting transfers between devices: 72 us -> none  [passed_along(): return lax.ppermute(block, axis, route)]
    unnamed x22 -> x0, waiting for transfers between devices: 68.1 us -> none
    all_gather x16 -> x0, waiting for transfers between devices: 60 us -> none  [the longest x1 51.2 us: per_device(): lax.all_gather(renewed[7], ('seq', 'fsdp'), axis=1, tiled=True)]
  transfers between devices with their start and end apart: 45 -> 0, of which waited for: 17 -> 0; matrix products, arithmetic and copies ran while one was open for 18% -> 0% of each run, Pallas kernels for 0% -> 0%
where the time goes in v2:
time: 386 us
  Pallas kernels  359 us (93%)
  local copies, waits for them, and re-layouts  23.2 us (6%)
    pallas_call x1, Pallas kernels, attention_in(): pl.pallas_call(functools.partial(attention_in_kernel, depth, halo, heads,...  129 us
    pallas_call x1, Pallas kernels, middle_part(): pl.pallas_call(functools.partial(middle_kernel, depth, heads), out_shape=...  91.6 us
    pallas_call x1, Pallas kernels, last_part(): pl.pallas_call(functools.partial(last_kernel, depth, heads, halo), out_sh...  72.8 us
    pallas_call x1, Pallas kernels, attention_backward(): pl.pallas_call(functools.partial(bwd_kernel, n, own, slots, halo, rows, w...  40.7 us
    pallas_call x1, Pallas kernels, attention_forward(): pl.pallas_call(functools.partial(fwd_kernel, n, own, slots, halo, rows, w...  24.8 us
    unnamed x44, local copies, waits for them, and re-layouts  18.8 us

profile of v2, /device:TPU:0, one launch (start us, length us, event | category | flops | bytes accessed | tf_op | source)
XLA Modules:
  0.0 385.8 jit_solution(9987392354458887965)
XLA Ops:
  0.6 0.8 reduce-window.8
  1.5 0.1 convert_reduce_fusion
  1.6 0.7 select_reduce_fusion
  2.3 0.8 copy.30
  3.1 0.8 copy.31
  3.9 0.1 fusion.5
  3.9 0.7 dynamic_update_slice.3.vec
  4.6 0.9 copy.29
  5.5 0.1 compare_convert_fusion.sel_ref
  5.6 0.0 copy-start
  5.6 1.0 copy-done
  6.6 0.0 copy-start.7
  6.6 0.9 copy-done.7
  7.6 0.0 copy-start.9
  7.6 0.9 copy-done.9
  8.5 0.0 copy-start.10
  8.5 0.8 copy-done.10
  9.4 0.0 copy-start.11
  9.4 0.8 copy-done.11
  10.1 0.0 copy-start.12
  10.1 0.8 copy-done.12
  10.9 0.0 copy-start.13
  10.9 0.8 copy-done.13
  11.6 0.0 copy-start.14
  11.6 0.7 copy-done.14
  12.3 0.0 copy-start.15
  12.3 0.7 copy-done.15
  13.0 0.0 copy-start.1
  13.0 129.4 %shard_map.224 = (bf16[32,32,5376]{2,1,0:T(8,128)(2,1)}, bf16[32,48,128]{2,1,0:T(8,128)(2,1)S(1)}, bf16[32,128,1280]{2,1,0:T(8,128)(2,1)}, bf16[22,3,64,256]{3,2,1,0:T(8,128)(2,1)S(1)}, bf16[3,256,128]{2,1,0:T(8,128)(2,1)S(1)}) custom-call(bf16[256,1024]{1,0:T(8,128)(2,1)S(1)} %copy-done, f32[256,128]{1,0:T(8,128)S(1)} %compare_convert_fusion.sel_ref, ...), custom_call_target="tpu_custom_call" | custom-call | tf_op jit(solution)/shard_map/pallas_call | solution.py:746
  142.4 0.0 copy-start.3
  142.5 0.7 copy-done.3
  143.2 0.0 copy-start.8
  143.2 0.0 copy-start.16
  143.2 0.7 copy-done.16
  143.9 24.8 %shard_map.225 = (bf16[16,64,256]{2,1,0:T(8,128)(2,1)S(1)}, f32[16,8,256]{2,1,0:T(8,128)S(1)}, f32[16,64,256]{2,1,0:T(8,128)S(1)}) custom-call(s32[8]{0:T(128)S(1)} %copy-done.16, bf16[22,3,64,256]{3,2,1,0:T(8,128)(2,1)S(1)} %get-tuple-element.25.x_ref), custom_call_target="tpu_custom_call" | custom-call | tf_op jit(solution)/shard_map/pallas_call | solution.py:1517
  168.7 0.0 copy-done.8
  168.7 0.0 copy-start.4
  168.7 0.8 copy-done.4
  169.5 0.0 copy-done.1
  169.5 0.0 copy-start.17
  169.5 91.6 %shard_map.226 = (bf16[256,1024]{1,0:T(8,128)(2,1)}, f32[256,1024]{1,0:T(8,128)}, bf16[32,384,128]{2,1,0:T(8,128)(2,1)}, bf16[16,64,256]{2,1,0:T(8,128)(2,1)}) custom-call(bf16[16,64,256]{2,1,0:T(8,128)(2,1)} %copy-done.4, bf16[256,1024]{1,0:T(8,128)(2,1)} %tok_ref.5, bf16[256,1024]{1,0:T(8,128)(2,1)} %cot_ref.1, f32[256,128]{1,0:T(8,128)} %copy-done.1, ...), custom_call_target="tpu_custom_call" | custom-call | tf_op jit(solution)/shard_map/pallas_call | solution.py:1050
  261.1 0.0 copy-done.17
  261.2 0.0 copy-start.5
  261.2 1.0 copy-done.5
  262.2 40.7 %shard_map.227 = (bf16[16,3,64,256]{3,2,1,0:T(8,128)(2,1)S(1)}, bf16[6,2,64,256]{3,2,1,0:T(8,128)(2,1)S(1)}) custom-call(s32[8]{0:T(128)S(1)} %copy-done.17, bf16[22,3,64,256]{3,2,1,0:T(8,128)(2,1)S(1)} %get-tuple-element.25.x_ref, bf16[16,64,256]{2,1,0:T(8,128)(2,1)S(1)} %copy-done.5, f32[16,8,256]{2,1,0:T(8,128)S(1)} %get-tuple-element.32.lse_ref, ...), custom_call_target="tpu_custom_call" | custom-call | tf_op jit(solution)/shard_map/pallas_call | solution.py:1588
  302.9 0.0 copy-start.2
  302.9 1.2 copy-done.2
  304.0 0.0 copy-start.6
  304.1 0.7 copy-done.6
  304.8 0.0 copy-start.18
  304.8 72.8 %shard_map.228 = (f32[256,1024]{1,0:T(8,128)}, f32[384,128]{1,0:T(8,128)}, f32[3,64,128]{2,1,0:T(8,128)}) custom-call(bf16[16,3,64,256]{3,2,1,0:T(8,128)(2,1)} %copy-done.2, bf16[6,2,64,256]{3,2,1,0:T(8,128)(2,1)} %copy-done.6, bf16[256,1024]{1,0:T(8,128)(2,1)} %tok_ref.5, f32[256,1024]{1,0:T(8,128)} %get-tuple-element.36.gm_ref, f32[256,128]{1,0:T(8,128)} %copy-done.1, ...), custom_call_target="tpu_custom_call" | custom-call | tf_op jit(solution)/shard_map/pallas_call | solution.py:1411
  377.6 1.4 slice_bitcast_fusion.1
  378.9 1.5 slice_bitcast_fusion
  380.5 0.7 copy.32
  381.2 0.8 fusion.6
  382.0 0.7 pad_maximum_fusion
  382.7 0.0 copy-done.18
  382.7 0.8 copy.36
  383.5 2.3 copy.37
  (2 shorter events, 0.0 us)
Async XLA Ops:
  5.6 1.0 copy-start
  6.6 0.9 copy-start.7
  7.6 0.9 copy-start.9
  8.5 0.8 copy-start.10
  9.4 0.8 copy-start.11
  10.1 0.8 copy-start.12
  10.9 0.8 copy-start.13
  11.6 0.7 copy-start.14
  12.3 0.7 copy-start.15
  13.0 156.5 %copy-start.1 = (f32[256,128]{1,0:T(8,128)}, f32[256,128]{1,0:T(8,128)S(1)}, u32[]{:S(2)}) copy-start(f32[256,128]{1,0:T(8,128)S(1)} %compare_convert_fusion.sel_ref) | copy-start | bytes 393220
  142.4 0.7 copy-start.3
  143.2 25.5 %copy-start.8 = (bf16[3,256,128]{2,1,0:T(8,128)(2,1)}, bf16[3,256,128]{2,1,0:T(8,128)(2,1)S(1)}, u32[]{:S(2)}) copy-start(bf16[3,256,128]{2,1,0:T(8,128)(2,1)S(1)} %get-tuple-element.37.rank_ref) | copy-start | bytes 589828
  143.2 0.7 copy-start.16
  168.7 0.8 copy-start.4
  169.5 91.6 %copy-start.17 = (s32[8]{0:T(128)S(1)}, s32[8]{0:T(128)}, u32[]{:S(2)}) copy-start(s32[8]{0:T(128)} %lens_ref.3) | copy-start | bytes 100
  261.2 1.0 copy-start.5
  302.9 1.2 copy-start.2
  304.0 0.7 copy-start.6
  304.8 77.9 %copy-start.18 = (bf16[256,1024]{1,0:T(8,128)(2,1)S(1)}, bf16[256,1024]{1,0:T(8,128)(2,1)}, u32[]{:S(2)}) copy-start(bf16[256,1024]{1,0:T(8,128)(2,1)} %get-tuple-element.76) | copy-start | bytes 1572868

commit v3 on v2

--- a/solution.py
+++ b/solution.py
@@ -415,6 +415,9 @@
         greet(barrier, seq, lax.rem(fsdp + step, depth))
 
 
+WHOLE, OPEN, LINE = 0, 1, 2
+
+
 class Gather:
     STEPS = 10
 
@@ -422,78 +425,104 @@
         self.depth, self.send, self.receive = depth, send, receive
         self.seq, self.fsdp = place_here()
         self.me = self.seq * depth + self.fsdp
+        self.inside = (self.fsdp == 1) | (self.fsdp == 2)
 
     def copy(self, index, step, source, target, seq, fsdp):
         at = index * self.STEPS + step
         return remote(source, target, self.send.at[at], self.receive.at[at], seq, fsdp)
 
+    def part(self, chunk, at_seq, first, count):
+        full, rows, columns, _, kind, _ = chunk
+        base = 0 if kind == LINE else at_seq * self.depth
+        return full.at[pl.ds(base + first, count), rows, columns]
+
     def group(self, chunk, at_seq):
-        full, rows, columns, _ = chunk
-        return full.at[pl.ds(at_seq * self.depth, self.depth), rows, columns]
+        return self.part(chunk, at_seq, 0, self.depth)
 
     def sides(self, chunk):
-        flip = chunk[3]
-        if isinstance(flip, int):
-            return (SIDE_X, SIDE_Y) if flip else (SIDE_Y, SIDE_X)
-        return SIDE_Y - flip * (SIDE_Y - SIDE_X), SIDE_X + flip * (SIDE_Y - SIDE_X)
-
-    def line(self, index, chunk):
-        full, rows, columns, _ = chunk
-        piece = full.at[self.me, rows, columns]
-        return [
-            self.copy(index, step - 1, piece, piece, self.seq, lax.rem(self.fsdp + step, self.depth))
-            for step in range(1, self.depth)
-        ]
-
-    def over(self, index, chunk):
+        return (SIDE_X, SIDE_Y) if chunk[3] else (SIDE_Y, SIDE_X)
+
+    def line(self, index, chunk, step):
+        pair = lax.div(self.fsdp, 2)
+        if step == 0:
+            piece, to = self.part(chunk, self.seq, self.fsdp, 1), self.fsdp ^ 1
+            if chunk[5] is not None:
+                source = chunk[5].at[pl.ds(0, 1), chunk[1], chunk[2]]
+                return self.copy(index, step, source, piece, self.seq, to)
+        elif step == 1:
+            piece, to = self.part(chunk, self.seq, 2 * pair, 2), 3 - self.fsdp
+        else:
+            piece, to = self.part(chunk, self.seq, 2 - 2 * pair, 2), self.fsdp ^ 1
+        return self.copy(index, step, piece, piece, self.seq, to)
+
+    def over(self, index, chunk, step):
         a, b = self.sides(chunk)
-        mine, theirs = self.group(chunk, self.seq), self.group(chunk, self.seq ^ a)
-        return [
-            self.copy(index, 3, mine, mine, self.seq ^ a, self.fsdp),
-            self.copy(index, 4, mine, mine, self.seq ^ b, self.fsdp),
-            self.copy(index, 5, theirs, theirs, self.seq ^ b, self.fsdp),
-        ]
-
-    def across(self, index, chunk):
+        piece = self.group(chunk, self.seq ^ a if step == 2 else self.seq)
+        return self.copy(index, 3 + step, piece, piece, self.seq ^ (b if step else a), self.fsdp)
+
+    def across(self, index, chunk, step):
         a, b = self.sides(chunk)
-        copies = []
-        for i, at_seq in enumerate((self.seq, self.seq ^ a, self.seq ^ b, self.seq ^ a ^ b)):
-            piece = self.group(chunk, at_seq)
-            copies.append(self.copy(index, 6 + i, piece, piece, self.seq ^ CORES, self.fsdp))
-        return copies
-
-    def along(self, index, chunk):
-        for copy in self.line(index, chunk):
-            copy.start()
+        piece = self.group(chunk, self.seq ^ (0, a, b, a ^ b)[step])
+        return self.copy(index, 6 + step, piece, piece, self.seq ^ CORES, self.fsdp)
+
+    def own(self, index, chunk):
+        self.line(index, chunk, 0).start()
+
+    def inner(self, index, chunk):
+        @pl.when(self.inside)
+        def _():
+            self.line(index, chunk, 0).wait_recv()
+            self.line(index, chunk, 1).start()
+
+    def outer(self, index, chunk):
+        @pl.when(self.inside)
+        def _():
+            self.line(index, chunk, 1).wait_recv()
+            self.line(index, chunk, 2).start()
+
+    def arrive(self, index, chunk):
+        @pl.when(jnp.logical_not(self.inside))
+        def _():
+            self.line(index, chunk, 0).wait_recv()
+            self.line(index, chunk, 2).wait_recv()
 
     def first(self, index, chunk):
-        for copy in self.line(index, chunk):
-            copy.wait_recv()
-        over = self.over(index, chunk)
-        over[0].start()
-        over[1].start()
-        self.across(index, chunk)[0].start()
+        self.arrive(index, chunk)
+        self.over(index, chunk, 0).start()
+        self.over(index, chunk, 1).start()
+        self.across(index, chunk, 0).start()
 
     def second(self, index, chunk):
-        over = self.over(index, chunk)
-        over[0].wait_recv()
-        over[2].start()
-        self.across(index, chunk)[1].start()
+        self.over(index, chunk, 0).wait_recv()
+        if chunk[4] == WHOLE:
+            self.over(index, chunk, 2).start()
+        self.across(index, chunk, 1).start()
 
     def third(self, index, chunk):
-        over, across = self.over(index, chunk), self.across(index, chunk)
-        over[1].wait_recv()
-        across[2].start()
-        over[2].wait_recv()
-        across[3].start()
+        self.over(index, chunk, 1).wait_recv()
+        self.across(index, chunk, 2).start()
+        if chunk[4] == WHOLE:
+            self.over(index, chunk, 2).wait_recv()
+            self.across(index, chunk, 3).start()
 
     def finish(self, index, chunk):
-        for copy in self.across(index, chunk):
-            copy.wait_recv()
+        for step in range(4 if chunk[4] == WHOLE else 3):
+            self.across(index, chunk, step).wait_recv()
 
     def drain(self, index, chunk):
-        for copy in self.line(index, chunk) + self.over(index, chunk) + self.across(index, chunk):
-            copy.wait_send()
+        self.line(index, chunk, 0).wait_send()
+
+        @pl.when(self.inside)
+        def _():
+            self.line(index, chunk, 1).wait_send()
+            self.line(index, chunk, 2).wait_send()
+
+        if chunk[4] == LINE:
+            return
+        for step in range(3 if chunk[4] == WHOLE else 2):
+            self.over(index, chunk, step).wait_send()
+        for step in range(4 if chunk[4] == WHOLE else 3):
+            self.across(index, chunk, step).wait_send()
 
 
 class Exchange:
@@ -550,13 +579,43 @@
     target[...] = flat.T[0:16]
 
 
+def by_feature_wide(block):
+    return jnp.concatenate([block, jnp.zeros((112, block.shape[1]), block.dtype)], axis=0)
+
+
+def selected(lens_ref, choice_ref, block, rows, lanes):
+    place = lax.broadcasted_iota(jnp.int32, (rows, lanes), 0) + block * rows
+    lane = lax.broadcasted_iota(jnp.int32, (rows, lanes), 1)
+    chosen = jnp.zeros((rows, lanes), jnp.int32)
+    start = jnp.int32(0)
+    for image in range(lens_ref.shape[0]):
+        end = start + lens_ref[image]
+        chosen = jnp.where((place >= start) & (place < end), choice_ref[image] * RANK, chosen)
+        start = end
+    return jnp.where((lane >= chosen) & (lane < chosen + RANK), 1.0, 0.0).astype(float_type)
+
+
+def stood_up(block):
+    n, m = block.shape
+    block = block.astype(float_type)
+    if m < 128:
+        block = jnp.concatenate([block, jnp.zeros((n, 128 - m), float_type)], axis=1)
+    if n < 128:
+        block = jnp.concatenate([block, jnp.zeros((128 - n, 128), float_type)], axis=0)
+    return block.T[0:m].astype(narrow_type)
+
+
 def attention_in_kernel(
     depth,
     halo,
     heads,
     chunks,
-    tok_ref,
-    sel_ref,
+    lens_ref,
+    choice_ref,
+    tok_in,
+    gains_in,
+    biases_in,
+    bias_in,
     wqkv,
     wout,
     a_att,
@@ -565,11 +624,13 @@
     b_con,
     w2,
     a_con,
-    b_exp,
-    vec,
+    b_exp_in,
+    w1,
     fa_out,
     ve_out,
     f2,
+    line_a,
+    line_b,
     y_ref,
     rank_ref,
     fa,
@@ -577,6 +638,15 @@
     proj,
     normed,
     vectors,
+    tok,
+    gains,
+    biases,
+    bias,
+    b_exp,
+    shard_f2,
+    shard_a,
+    shard_b,
+    select,
     send,
     receive,
     local,
@@ -592,7 +662,15 @@
     barrier = pltpu.get_barrier_semaphore()
     greet_neighbours(barrier, seq, fsdp, depth)
     waits = 3 + depth - 1 + swap.greet_owners(barrier)
-    places = [(vec, ve.at[me])]
+    half_columns = line_a.shape[2]
+    small = [
+        (gains_in, gains.at[0:4]),
+        (biases_in, biases.at[0:5]),
+        (bias_in, bias),
+        (b_exp_in, b_exp),
+        (tok_in, tok),
+    ]
+    places = []
     for p in range(4):
         source = wqkv.at[:, pl.ds(p * features, features)] if p < 3 else wout
         places.append((source, fa.at[me, :, pl.ds(p * wide, features)]))
@@ -600,19 +678,45 @@
         places.append((b_att.at[p], fa.at[me, :, pl.ds(p * wide + features + 128, 128)]))
     places.append((a_exp, fa.at[me, :, pl.ds(4 * wide, 128)]))
     places.append((b_con, fa.at[me, :, pl.ds(4 * wide + 128, 128)]))
-    places.append((w2, f2.at[me, :, pl.ds(0, features)]))
-    places.append((a_con, f2.at[me, :, pl.ds(features, 128)]))
-    places.append((b_exp, f2.at[me, :, pl.ds(features + 128, 128)]))
-    placed = [pltpu.make_async_copy(a, b, local.at[i]) for i, (a, b) in enumerate(places)]
+    places.append((w2, shard_f2.at[0, :, pl.ds(0, features)]))
+    places.append((a_con, shard_f2.at[0, :, pl.ds(features, 128)]))
+    places.append((w1.at[:, pl.ds(0, half_columns)], shard_a.at[0]))
+    places.append((w1.at[:, pl.ds(half_columns, half_columns)], shard_b.at[0]))
+    placed = [pltpu.make_async_copy(a, b, local.at[i]) for i, (a, b) in enumerate(small + places)]
     for copy in placed:
         copy.start()
-    for copy in placed:
+    for copy in placed[: len(small) - 1]:
         copy.wait()
-    refs = {"ve": ve, "fa": fa, "f2": f2}
-    chunks = [(refs[name], rows, columns, flip) for name, rows, columns, flip in chunks]
+    shard_f2[0, :, features + 128 : wide] = stood_up(b_exp[...])
+    by_feature = jnp.concatenate(
+        [gains[0:4].astype(float_type), biases[0:5].astype(float_type), jnp.zeros((7, 32), float_type)], axis=0
+    )
+    ve[me, 0:32] = stood_up(by_feature_wide(by_feature))
+    ve[me, 32:48] = jnp.broadcast_to(bias[...].astype(float_type), (16, 128)).astype(narrow_type)
+    for copy in placed[len(small) - 1 :]:
+        copy.wait()
+    own_shards = [
+        pltpu.make_async_copy(shard.at[0], full.at[slot], local.at[i])
+        for i, (shard, full, slot) in enumerate(((shard_f2, f2, me), (shard_a, line_a, fsdp), (shard_b, line_b, fsdp)))
+    ]
+    for copy in own_shards:
+        copy.start()
+    refs = {
+        "ve": (ve, WHOLE, None),
+        "fa": (fa, WHOLE, None),
+        "f2": (f2, OPEN, shard_f2),
+        "a": (line_a, LINE, shard_a),
+        "b": (line_b, LINE, shard_b),
+    }
+    chunks = [
+        (refs[name][0], rows, columns, flip) + refs[name][1:] for name, rows, columns, flip in chunks
+    ]
+    first_hidden = [i for i, chunk in enumerate(chunks) if chunk[4] != WHOLE][:1]
     pl.semaphore_wait(barrier, waits)
-    for index, chunk in enumerate(chunks):
-        gather.along(index, chunk)
+    early = [i for i, chunk in enumerate(chunks) if chunk[0] is fa or chunk[0] is ve]
+    for index in early:
+        gather.own(index, chunks[index])
+    select[...] = selected(lens_ref, choice_ref, me, *select.shape)
     base = core * (own - halo)
     slot = me - half * (own - halo)
 
@@ -640,12 +744,12 @@
 
     def norm():
         rows_of_vectors(ve, vectors)
-        rows = tok_ref[...].astype(float_type)
+        rows = tok[...].astype(float_type)
         normed[...] = layer_norm(rows, vectors[0:1], vectors[4:5])[0].astype(narrow_type)
 
     def project(p):
         down = as_matrix(fa[:, :, p * wide + features : p * wide + features + 128])
-        rank = (matmul(normed[...], down) * sel_ref[...]).astype(narrow_type)
+        rank = (matmul(normed[...], down) * select[...]).astype(narrow_type)
         rank_ref[p] = rank
 
         @pl.loop(0, features // 256)
@@ -672,23 +776,33 @@
     after = {0: norm, 2: lambda: project(0), 4: lambda: project(1), 6: lambda: project(2)}
     after_attention = [i for i, chunk in enumerate(chunks) if chunk[0] is fa][-1]
     outs = [
-        pltpu.make_async_copy(fa, fa_out, local.at[0]),
-        pltpu.make_async_copy(ve, ve_out, local.at[1]),
+        pltpu.make_async_copy(fa, fa_out, local.at[3]),
+        pltpu.make_async_copy(ve, ve_out, local.at[4]),
     ]
 
     def store():
         for copy in outs:
             copy.start()
 
-    for turn in range(len(chunks) + 3):
-        for delay, step in enumerate((gather.first, gather.second, gather.third, gather.finish)):
+    steps = (gather.own, gather.inner, gather.outer, gather.first, gather.second, gather.third, gather.finish)
+    for turn in range(-LOOKAHEAD, len(chunks) + 3):
+        for delay, step in zip((-LOOKAHEAD, -2, -1, 0, 1, 2, 3), steps):
             index = turn - delay
-            if 0 <= index < len(chunks):
-                step(index, chunks[index])
-                if delay == 3:
-                    after.get(index, lambda: None)()
-                    if index == after_attention:
-                        store()
+            if not 0 <= index < len(chunks) or (delay == -LOOKAHEAD and index in early):
+                continue
+            chunk = chunks[index]
+            if delay == -2 and index in first_hidden:
+                for copy in own_shards:
+                    copy.wait()
+            if chunk[4] == LINE and delay == 0:
+                step = gather.arrive
+            if chunk[4] == LINE and delay > 0:
+                continue
+            step(index, chunk)
+            if delay == 3:
+                after.get(index, lambda: None)()
+                if index == after_attention:
+                    store()
 
     @pl.loop(0, own)
     def _(k):
@@ -727,11 +841,11 @@
         copy.wait()
 
 
-def attention_in(tokens, select, arrays, halo, depth, heads, devices, collective):
+def attention_in(lengths, choice, tokens, arrays, halo, depth, heads, devices, collective):
     rows, features = tokens.shape
     wide = features + 256
     total = 4 * wide + 256
-    share, hidden_share = features // devices, arrays[6].shape[0]
+    share, hidden_share, hidden_total = features // devices, arrays[9].shape[0], arrays[12].shape[1]
     chunks = [("ve", slice(0, 48), slice(0, 128), 0)]
     for p in range(3):
         chunks.append(("fa", slice(0, share), slice(p * wide, p * wide + wide // 2), 0))
@@ -742,6 +856,9 @@
     for part in range(0, hidden_share, 32):
         chunks.append(("f2", slice(part, part + 32), slice(0, wide // 2), 0))
         chunks.append(("f2", slice(part, part + 32), slice(wide // 2, wide), 1))
+    for part in range(0, hidden_total // 2, 1024):
+        chunks.append(("a", slice(0, share), slice(part, part + 1024), 0))
+        chunks.append(("b", slice(0, share), slice(part, part + 1024), 1))
     copies = Gather.STEPS * len(chunks)
     return pl.pallas_call(
         functools.partial(attention_in_kernel, depth, halo, heads, chunks),
@@ -749,44 +866,62 @@
             jax.ShapeDtypeStruct((devices, share, total), narrow_type),
             jax.ShapeDtypeStruct((devices, 48, 128), narrow_type),
             jax.ShapeDtypeStruct((devices, hidden_share, wide), narrow_type),
+            jax.ShapeDtypeStruct((depth, share, hidden_total // 2), narrow_type),
+            jax.ShapeDtypeStruct((depth, share, hidden_total // 2), narrow_type),
             jax.ShapeDtypeStruct((heads + halo, 3, features // heads, rows), narrow_type),
             jax.ShapeDtypeStruct((3, rows, 128), narrow_type),
         ),
-        in_specs=[IN_VMEM, IN_VMEM] + [ANYWHERE] * len(arrays),
-        out_specs=(ANYWHERE, ANYWHERE, ANYWHERE, ANYWHERE, IN_VMEM),
+        in_specs=[IN_SMEM, IN_SMEM] + [ANYWHERE] * (1 + len(arrays)),
+        out_specs=(ANYWHERE,) * 6 + (IN_VMEM,),
         scratch_shapes=[
             pltpu.VMEM((devices, share, total), narrow_type),
             pltpu.VMEM((devices, 48, 128), narrow_type),
             pltpu.VMEM((3, heads, features // heads, rows), narrow_type),
             pltpu.VMEM((rows, features), narrow_type),
             pltpu.VMEM((16, features), float_type),
+            pltpu.VMEM((rows, features), narrow_type),
+            pltpu.VMEM((4, share), narrow_type),
+            pltpu.VMEM((5, share), narrow_type),
+            pltpu.VMEM((1, 128), narrow_type),
+            pltpu.VMEM((128, 128), narrow_type),
+            pltpu.VMEM((1, hidden_share, wide), narrow_type),
+            pltpu.VMEM((1, share, hidden_total // 2), narrow_type),
+            pltpu.VMEM((1, share, hidden_total // 2), narrow_type),
+            pltpu.VMEM((rows, 128), float_type),
             pltpu.SemaphoreType.DMA((copies,)),
             pltpu.SemaphoreType.DMA((copies,)),
-            pltpu.SemaphoreType.DMA((20,)),
+            pltpu.SemaphoreType.DMA((24,)),
             pltpu.SemaphoreType.DMA((4, heads)),
             pltpu.SemaphoreType.DMA((4, heads)),
             pltpu.SemaphoreType.DMA((3,)),
         ],
         compiler_params=pltpu.CompilerParams(
-            collective_id=collective, has_side_effects=True, vmem_limit_bytes=48 << 20
+            collective_id=collective, has_side_effects=True, vmem_limit_bytes=60 << 20
         ),
-    )(tokens, select, *arrays)
-
-
+    )(lengths, choice, tokens, *arrays)
+
+
+LOOKAHEAD = 5
 HIDDEN_TILE = 512
 
 
 def middle_kernel(
     depth,
     heads,
+    lens_ref,
+    choice_ref,
     att_ref,
     tok_ref,
     cot_ref,
-    sel_ref,
     fa_in,
     ve,
     f2_in,
-    w1,
+    line_a,
+    line_b,
+    ya,
+    yb,
+    xa,
+    xb,
     result_ref,
     gm_ref,
     terms,
@@ -807,6 +942,7 @@
     grad_normed,
     ranks,
     rank_sums,
+    select,
     send,
     receive,
     local,
@@ -816,7 +952,7 @@
     b_receive,
     own_local,
 ):
-    gather, swap = Gather(depth, send, receive), Exchange(depth, heads)
+    swap = Exchange(depth, heads)
     me, seq, fsdp = swap.me, swap.seq, swap.fsdp
     core, half, head, own = swap.core, swap.half, swap.head, heads
     devices, share = f1.shape[0], f1.shape[1]
@@ -827,15 +963,56 @@
     barrier = pltpu.get_barrier_semaphore()
     greet_neighbours(barrier, seq, fsdp, depth)
     waits = 3 + depth - 1 + swap.greet_owners(barrier) + swap.greet_holders(barrier)
-    loads = [
-        pltpu.make_async_copy(w1, f1.at[me], local.at[0]),
-        pltpu.make_async_copy(fa_in.at[:, :, pl.ds(3 * wide, wide + 256)], fa, local.at[1]),
-        pltpu.make_async_copy(f2_in, f2, local.at[2]),
+    half_columns = line_a.shape[2]
+    left, right = pl.ds(0, half_columns), pl.ds(half_columns, half_columns)
+    lines = [
+        (line, f1.at[pl.ds((seq ^ bit) * depth, depth), :, columns])
+        for line, bit, columns in (
+            (line_a, 0, left),
+            (line_b, 0, right),
+            (ya, SIDE_Y, left),
+            (yb, SIDE_Y, right),
+            (xa, SIDE_X, left),
+            (xb, SIDE_X, right),
+        )
     ]
+    groups = [pl.ds((seq ^ k) * depth, depth) for k in range(8)]
+    loads = (
+        [pltpu.make_async_copy(fa_in.at[:, :, pl.ds(3 * wide, wide + 256)], fa, local.at[0])]
+        + [pltpu.make_async_copy(line, place, local.at[1 + i]) for i, (line, place) in enumerate(lines)]
+        + [pltpu.make_async_copy(f2_in.at[groups[k]], f2.at[groups[k]], local.at[7 + k]) for k in range(6)]
+    )
     for copy in loads:
         copy.start()
-    loads[0].wait()
     pl.semaphore_wait(barrier, waits)
+    corners = [
+        remote(ya, lines[2][1], send.at[0], receive.at[0], seq ^ SIDE_X, fsdp),
+        remote(xb, lines[5][1], send.at[1], receive.at[1], seq ^ SIDE_Y, fsdp),
+    ]
+    tops, tails = pl.ds(0, wide // 2), pl.ds(wide // 2, wide // 2)
+    f2_parts = ((SIDE_Y, SIDE_X, tops), (SIDE_X, SIDE_Y, tails))
+    for i, (via, to, columns) in enumerate(f2_parts):
+        line = pl.ds((seq ^ via) * depth, depth)
+        corners.append(
+            remote(
+                f2_in.at[line, :, columns],
+                f2.at[line, :, columns],
+                send.at[10 + i],
+                receive.at[10 + i],
+                seq ^ to,
+                fsdp,
+            )
+        )
+    across = [
+        remote(line, place, send.at[2 + i], receive.at[2 + i], seq ^ CORES, fsdp)
+        for i, (line, place) in enumerate(lines)
+    ]
+    for i, columns in enumerate((left, right)):
+        place = f1.at[pl.ds((seq ^ SIDE_X ^ SIDE_Y) * depth, depth), :, columns]
+        across.append(remote(place, place, send.at[8 + i], receive.at[8 + i], seq ^ CORES, fsdp))
+    f2_across = remote(
+        f2.at[groups[6]], f2.at[groups[6]], send.at[12], receive.at[12], seq ^ CORES, fsdp
+    )
 
     def attended_piece(k):
         return remote(att_ref.at[k], att_t.at[head], a_send.at[k], a_receive.at[head], *swap.owner(k))
@@ -857,32 +1034,19 @@
         def _():
             attended_piece(k).start()
 
-    def chunk(c):
-        flip = c % 2 if isinstance(c, int) else lax.rem(c, 2)
-        start = c * HIDDEN_TILE if isinstance(c, int) else pl.multiple_of(c * HIDDEN_TILE, 128)
-        return (f1, slice(0, share), pl.ds(start, HIDDEN_TILE), flip)
-
-    @pl.loop(0, tiles)
-    def _(c):
-        gather.along(c, chunk(c))
-
+    for copy in corners + across[:6]:
+        copy.start()
+    select[...] = selected(lens_ref, choice_ref, me, *select.shape)
     rows_of_vectors(ve, vectors)
     for d in range(devices):
         hidden_bias[:, d * 128 : (d + 1) * 128] = ve[d, 32:48, :].astype(float_type)[0:8]
     grad_branch[...] = (vectors[3:4] * cot_ref[...].astype(float_type)).astype(narrow_type)
-    loads[1].wait()
+    loads[0].wait()
     contract_up = as_matrix(fa[:, :, wide + 128 : wide + 256])
-    ranks[1] = (matmul(grad_branch[...], contract_up) * sel_ref[...]).astype(narrow_type)
+    ranks[1] = (matmul(grad_branch[...], contract_up) * select[...]).astype(narrow_type)
     branch[...] = jnp.zeros_like(branch)
     grad_normed[...] = jnp.zeros_like(grad_normed)
     rank_sums[...] = jnp.zeros_like(rank_sums)
-
-    gather.first(0, chunk(0))
-    gather.first(1, chunk(1))
-    gather.second(0, chunk(0))
-    gather.first(2, chunk(2))
-    gather.second(1, chunk(1))
-    gather.third(0, chunk(0))
 
     @pl.loop(0, heads)
     def _(k):
@@ -894,10 +1058,13 @@
     def _():
         attended_kept.wait()
 
+    for i in range(2):
+        corners[i].wait_recv()
+        across[6 + i].start()
     for j in range(4):
         att[:, j * 256 : (j + 1) * 256] = turned(as_matrix(att_t[4 * j : 4 * j + 4]))
     out_down = as_matrix(fa[:, :, features : features + 128])
-    rank_out = (matmul(att[...], out_down) * sel_ref[...]).astype(narrow_type)
+    rank_out = (matmul(att[...], out_down) * select[...]).astype(narrow_type)
     ranks[2] = rank_out
 
     @pl.loop(0, 4)
@@ -912,15 +1079,29 @@
     normal[...] = normal_rows
     normed[...] = shifted.astype(narrow_type)
     expand_down = as_matrix(fa[:, :, wide : wide + 128])
-    rank_expand = (matmul(normed[...], expand_down) * sel_ref[...]).astype(narrow_type)
+    rank_expand = (matmul(normed[...], expand_down) * select[...]).astype(narrow_type)
     ranks[0] = rank_expand
     ranks[3, 0:128] = turned(rank_expand)[:, 0:128]
     ranks[3, 128:256] = turned(rank_expand)[:, 128:256]
     ranks[4, 0:128] = turned(ranks[1])[:, 0:128]
     ranks[4, 128:256] = turned(ranks[1])[:, 128:256]
-    loads[2].wait()
-
-    def hidden(c):
+    for copy in loads[1:]:
+        copy.wait()
+    for copy in across:
+        copy.wait_recv()
+
+    def hidden(k):
+        @pl.when(k == 6)
+        def _():
+            corners[2].wait_recv()
+            corners[3].wait_recv()
+            f2_across.start()
+
+        @pl.when(k == 7)
+        def _():
+            f2_across.wait_recv()
+
+        c = seq ^ k
         at = pl.ds(pl.multiple_of(c * HIDDEN_TILE, 128), HIDDEN_TILE)
         slots = pl.ds(c * in_tile, in_tile)
         expand = as_matrix(f1[:, :, at])
@@ -946,30 +1127,14 @@
             terms[c * in_tile + i, 96:224] = grad_up[:, i * 128 : (i + 1) * 128]
             terms[c * in_tile + i, 224:352] = grad_down[:, i * 128 : (i + 1) * 128]
 
-    @pl.loop(3, tiles + 3)
-    def _(turn):
-        @pl.when(turn < tiles)
-        def _():
-            gather.first(turn, chunk(turn))
-
-        @pl.when(turn - 1 < tiles)
-        def _():
-            gather.second(turn - 1, chunk(turn - 1))
-
-        @pl.when(turn - 2 < tiles)
-        def _():
-            gather.third(turn - 2, chunk(turn - 2))
-
-        gather.finish(turn - 3, chunk(turn - 3))
-        hidden(turn - 3)
-
-    rank_contract = (rank_sums[0] * sel_ref[...]).astype(narrow_type)
-    grad_rank_expand = (rank_sums[1] * sel_ref[...]).astype(narrow_type)
+    pl.loop(0, tiles)(hidden)
+    rank_contract = (rank_sums[0] * select[...]).astype(narrow_type)
+    grad_rank_expand = (rank_sums[1] * select[...]).astype(narrow_type)
     gradient = grad_normed[...] + transposed_right(grad_rank_expand, expand_down)
     gm_ref[...] = cot_ref[...].astype(float_type) + norm_backward(gradient, vectors[2:3], normal[...], scaling)
     grad_mixed = (vectors[1:2] * gm_ref[...]).astype(narrow_type)
     out_up = as_matrix(fa[:, :, features + 128 : wide])
-    grad_rank_out = (matmul(grad_mixed, out_up) * sel_ref[...]).astype(narrow_type)
+    grad_rank_out = (matmul(grad_mixed, out_up) * select[...]).astype(narrow_type)
 
     def gradient_piece(k):
         return remote(
@@ -1028,18 +1193,17 @@
         def _():
             gradient_piece(k).wait_send()
 
-    @pl.loop(0, tiles)
-    def _(c):
-        gather.drain(c, chunk(c))
-
-
-def middle_part(att, tokens, cotangent, select, fa, ve, f2, w1, depth, collective):
+    for copy in corners + across + [f2_across]:
+        copy.wait_send()
+
+
+def middle_part(lengths, choice, att, tokens, cotangent, fa, ve, f2, lines, depth, collective):
     heads, width, rows = att.shape
     features = tokens.shape[1]
     wide = features + 256
     devices, hidden_share = f2.shape[0], f2.shape[1]
-    share, hidden_total = w1.shape
-    copies = Gather.STEPS * (hidden_total // HIDDEN_TILE)
+    share, hidden_total = features // devices, 2 * lines[0].shape[2]
+    copies = 13
 
     def wide_rows():
         return pltpu.VMEM((rows, features), float_type)
@@ -1055,7 +1219,7 @@
             jax.ShapeDtypeStruct((devices, 384, 128), narrow_type),
             jax.ShapeDtypeStruct((heads, width, rows), narrow_type),
         ),
-        in_specs=[IN_VMEM, IN_VMEM, IN_VMEM, IN_VMEM, ANYWHERE, IN_VMEM, ANYWHERE, ANYWHERE],
+        in_specs=[IN_SMEM, IN_SMEM, IN_VMEM, IN_VMEM, IN_VMEM, ANYWHERE, IN_VMEM] + [ANYWHERE] * 7,
         out_specs=(IN_VMEM, IN_VMEM, IN_VMEM, ANYWHERE),
         scratch_shapes=[
             pltpu.VMEM((devices, share, wide + 256), narrow_type),
@@ -1074,9 +1238,10 @@
             wide_rows(),
             pltpu.VMEM((5, rows, 128), narrow_type),
             pltpu.VMEM((2, rows, 128), float_type),
+            pltpu.VMEM((rows, 128), float_type),
             pltpu.SemaphoreType.DMA((copies,)),
             pltpu.SemaphoreType.DMA((copies,)),
-            pltpu.SemaphoreType.DMA((3,)),
+            pltpu.SemaphoreType.DMA((13,)),
             pltpu.SemaphoreType.DMA((heads,)),
             pltpu.SemaphoreType.DMA((heads,)),
             pltpu.SemaphoreType.DMA((heads,)),
@@ -1084,9 +1249,9 @@
             pltpu.SemaphoreType.DMA((2,)),
         ],
         compiler_params=pltpu.CompilerParams(
-            collective_id=collective, has_side_effects=True, vmem_limit_bytes=60 << 20
+            collective_id=collective, has_side_effects=True, vmem_limit_bytes=54 << 20
         ),
-    )(att, tokens, cotangent, select, fa, ve, f2, w1)
+    )(lengths, choice, att, tokens, cotangent, fa, ve, f2, *lines)
 
 
 class Reduce:
@@ -1210,11 +1375,12 @@
     depth,
     heads,
     halo,
-    dx_ref,
-    dh_ref,
+    lens_ref,
+    choice_ref,
+    dq_ref,
+    dkv_ref,
     tok_ref,
     gm_ref,
-    sel_ref,
     fa_in,
     ve,
     rank_ref,
@@ -1233,6 +1399,7 @@
     late_terms,
     early_buffers,
     late_buffers,
+    select,
     send,
     receive,
     local,
@@ -1252,7 +1419,10 @@
     load = pltpu.make_async_copy(fa_in.at[:, :, pl.ds(0, 3 * wide)], fa, local.at[0])
     load.start()
     pl.semaphore_wait(barrier, waits)
-    over = remote(dh_ref, other, piece_send.at[3, 0], piece_receive.at[3, 0], seq ^ CORES, fsdp)
+    over = remote(
+        dkv_ref.at[pl.ds(jnp.where(core == 0, own, 0), halo)],
+        other,
+        piece_send.at[3, 0], piece_receive.at[3, 0], seq ^ CORES, fsdp)
     over.start()
     early = Reduce(depth, 0, early_terms, *early_buffers, send, receive)
     late = [
@@ -1262,6 +1432,7 @@
         for p in range(3)
     ]
     shared = jnp.where(core == 0, own - halo, 0)
+    shift = core * halo
 
     def in_shared(k):
         return (k >= shared) & (k < shared + halo)
@@ -1282,13 +1453,13 @@
 
     def arrival(p, k):
         return remote(
-            dx_ref.at[0, 0], arrived.at[p, k], piece_send.at[p, k], piece_receive.at[p, k], seq ^ CORES, fsdp
+            dq_ref.at[0], arrived.at[p, k], piece_send.at[p, k], piece_receive.at[p, k], seq ^ CORES, fsdp
         )
 
     @pl.loop(0, own)
     def _(step):
         k = lax.rem(step + me, own)
-        launch(0, k, dx_ref.at[k, 0])
+        launch(0, k, dq_ref.at[k])
 
     over.wait_recv()
 
@@ -1296,7 +1467,7 @@
     def _(i):
         for part in range(2):
             merged[i, part] = (
-                dx_ref[shared + i, 1 + part].astype(float_type) + other[i, part].astype(float_type)
+                dkv_ref[shared + shift + i, part].astype(float_type) + other[i, part].astype(float_type)
             ).astype(narrow_type)
 
     for p in (1, 2):
@@ -1311,10 +1482,11 @@
 
             @pl.when(jnp.logical_not(in_shared(k)))
             def _():
-                launch(p, k, dx_ref.at[k, p])
+                launch(p, k, dkv_ref.at[k + shift, p - 1])
 
     early.begin()
     rows_of_vectors(ve, vectors)
+    select[...] = selected(lens_ref, choice_ref, me, *select.shape)
     early.sides()
     shifted, normal, scaling = layer_norm(tok_ref[...].astype(float_type), vectors[0:1], vectors[4:5])
     normed[...] = shifted.astype(narrow_type)
@@ -1330,13 +1502,13 @@
 
         @pl.when(half == core)
         def _():
-            pltpu.make_async_copy(dx_ref.at[0, p], arrived.at[p, head], piece_local.at[p]).wait()
+            pltpu.make_async_copy(dq_ref.at[0], arrived.at[p, head], piece_local.at[p]).wait()
 
     def project_back(p):
         for j in range(4):
             arrived_rows[:, j * 256 : (j + 1) * 256] = turned(as_matrix(arrived[p, 4 * j : 4 * j + 4]))
         up = as_matrix(fa[:, :, p * wide + features + 128 : (p + 1) * wide])
-        grad_rank = (matmul(arrived_rows[...], up) * sel_ref[...]).astype(narrow_type)
+        grad_rank = (matmul(arrived_rows[...], up) * select[...]).astype(narrow_type)
 
         @pl.loop(0, 4)
         def _(j):
@@ -1388,14 +1560,14 @@
         @pl.when(swap.away_block(k))
         def _():
             for p in range(3):
-                sent(p, k, dx_ref.at[k, p]).wait_send()
+                sent(p, k, dq_ref.at[k]).wait_send()
 
     over.wait_send()
 
 
-def last_part(dx, dh, tokens, grad_middle, select, fa, ve, rank, terms, depth, collective):
-    heads = dx.shape[0]
-    halo = dh.shape[0]
+def last_part(lengths, choice, dq, dkv, tokens, grad_middle, fa, ve, rank, terms, depth, collective):
+    heads = dq.shape[0]
+    halo = dkv.shape[0] - heads
     rows, features = tokens.shape
     wide = features + 256
     devices, share = fa.shape[0], fa.shape[1]
@@ -1415,7 +1587,7 @@
             jax.ShapeDtypeStruct((terms.shape[1], 128), float_type),
             jax.ShapeDtypeStruct((3, 2 * share, 128), float_type),
         ),
-        in_specs=[IN_VMEM] * 5 + [ANYWHERE] + [IN_VMEM] * 3,
+        in_specs=[IN_SMEM] * 2 + [IN_VMEM] * 4 + [ANYWHERE] + [IN_VMEM] * 3,
         out_specs=(IN_VMEM, IN_VMEM, IN_VMEM),
         scratch_shapes=[
             pltpu.VMEM((devices, share, 3 * wide), narrow_type),
@@ -1424,11 +1596,12 @@
             pltpu.VMEM((rows, features), float_type),
             pltpu.VMEM((3, heads, features // heads, rows), narrow_type),
             pltpu.VMEM((rows, features), narrow_type),
-            pltpu.VMEM(dh.shape, narrow_type),
-            pltpu.VMEM(dh.shape, narrow_type),
+            pltpu.VMEM((halo,) + dkv.shape[1:], narrow_type),
+            pltpu.VMEM((halo,) + dkv.shape[1:], narrow_type),
             pltpu.VMEM((3, devices, 2 * share, 128), narrow_type),
             buffers((), terms.shape[1]),
             buffers((3,), 2 * share),
+            pltpu.VMEM((rows, 128), float_type),
             pltpu.SemaphoreType.DMA((4 * Reduce.COPIES,)),
             pltpu.SemaphoreType.DMA((4 * Reduce.COPIES,)),
             pltpu.SemaphoreType.DMA((1,)),
@@ -1437,161 +1610,309 @@
             pltpu.SemaphoreType.DMA((3,)),
         ],
         compiler_params=pltpu.CompilerParams(
-            collective_id=collective, has_side_effects=True, vmem_limit_bytes=56 << 20
+            collective_id=collective, has_side_effects=True, vmem_limit_bytes=44 << 20
         ),
-    )(dx, dh, tokens, grad_middle, select, fa, ve, rank, terms)
+    )(lengths, choice, dq, dkv, tokens, grad_middle, fa, ve, rank, terms)
+
+
+def spread_kernel(result_in, gradient_in, early, late, result, gradient, down, up, exp_down, exp_up, con_down, con_up):
+    share = down.shape[1]
+    result[...] = result_in[...]
+    gradient[...] = gradient_in[...]
+    for p in range(4):
+        first = late[p, 0:share] if p < 3 else early[0:share]
+        second = late[p, share : 2 * share] if p < 3 else early[share : 2 * share]
+        down[p] = first
+        up[p] = second
+    exp_down[...] = early[64:96]
+    exp_up[...] = early[96:224]
+    con_down[...] = early[224:352].T
+    con_up[...] = early[352:384]
+
+
+def spread(result, gradient, early, late):
+    share = late.shape[1] // 2
+    shapes = ((4, share, 128), (4, share, 128), (share, 128), (128, 128), (128, 128), (share, 128))
+    return pl.pallas_call(
+        spread_kernel,
+        out_shape=tuple(jax.ShapeDtypeStruct(a.shape, a.dtype) for a in (result, gradient))
+        + tuple(jax.ShapeDtypeStruct(shape, float_type) for shape in shapes),
+        in_specs=[IN_VMEM] * 4,
+        out_specs=(IN_VMEM,) * 8,
+        compiler_params=pltpu.CompilerParams(vmem_limit_bytes=24 << 20),
+    )(result, gradient, early, late)
 
 
 BIG = 32768.0
 
 
-def bounds(lens_ref, n, base_block, rows, i):
-    first=(base_block+i)*rows; last=first+rows-1
-    lo=jnp.int32(0); hi=jnp.int32(0); start=jnp.int32(0)
-    for m in range(n):
-        end=start+lens_ref[m]
-        lo=jnp.where((start<=first)&(first<end),start,lo)
-        hi=jnp.where((start<=last)&(last<end),end-1,hi)
-        start=end
-    return lax.div(lo,rows), lax.div(hi,rows)
-
-def image_marks(lens_ref, n, marks, rows):
-    r=lax.broadcasted_iota(jnp.int32,(marks,rows),0)
-    st=jnp.full((marks,rows),1<<30,jnp.int32); en=jnp.zeros((marks,rows),jnp.int32)
-    start=jnp.int32(0)
-    for m in range(n):
-        end=start+lens_ref[m]
-        st=jnp.where(r==m,start,st); en=jnp.where(r==m,end,en)
-        start=end
-    return st,en
-
-def fwd_kernel(n,own,slots,halo,rows,width,marks, lens_ref,x_ref,att_ref,lse_ref,o_ref,qa,ka):
-    core=lax.rem(lax.axis_index("seq"),2)
-    base=core*(own-halo)
-    shift=core*halo
-    st,en=image_marks(lens_ref,n,marks,rows)
-    pos=lax.broadcasted_iota(jnp.int32,(marks,rows),1)
-    def prep(s,_):
-        p=pos+(base+s)*rows
-        inside=(p>=st)&(p<en)
-        oh=jnp.where(inside,1.0,0.0).astype(float_type)
-        kt=jnp.concatenate([x_ref[s,1].astype(float_type),(oh-1.0)*BIG],axis=0)
-        ka[s]=kt.T.astype(narrow_type)
-        return 0
-    lax.fori_loop(0,slots,prep,0)
-    def one_q(i,_):
-        s_q=i+shift
-        p=pos+(base+s_q)*rows
-        oh=jnp.where((p>=st)&(p<en),1.0,0.0).astype(narrow_type)
-        q=jnp.concatenate([(x_ref[s_q,0].astype(float_type)*(width**-0.5)).astype(narrow_type),oh],axis=0)
-        lo,hi=bounds(lens_ref,n,base+shift,rows,i)
-        lo=lo-base; hi=hi-base
-        def tile(m,l,o,s):
-            sc=matmul(ka[s],q)
-            m2=jnp.maximum(m,jnp.max(sc,axis=0,keepdims=True))
-            pr=jnp.exp(sc-m2)
-            al=jnp.exp(m-m2)
-            return m2, l*al+jnp.sum(pr,axis=0,keepdims=True), o*al+matmul(x_ref[s,2],pr.astype(narrow_type))
-        def tile2(m,l,o,s):
-            sa=matmul(ka[s],q); sb=matmul(ka[s+1],q)
-            m2=jnp.maximum(m,jnp.maximum(jnp.max(sa,axis=0,keepdims=True),jnp.max(sb,axis=0,keepdims=True)))
-            pa=jnp.exp(sa-m2); pb=jnp.exp(sb-m2)
-            al=jnp.exp(m-m2)
-            l=l*al+jnp.sum(pa,axis=0,keepdims=True)+jnp.sum(pb,axis=0,keepdims=True)
-            return m2,l,o*al+matmul(x_ref[s,2],pa.astype(narrow_type))+matmul(x_ref[s+1,2],pb.astype(narrow_type))
-        m=jnp.full((1,rows),-1e30,float_type); l=jnp.zeros((1,rows),float_type); o=jnp.zeros((width,rows),float_type)
-        cnt=hi-lo+1
-        m,l,o=lax.fori_loop(0,cnt//2,lambda t,c: tile2(*c,lo+2*t),(m,l,o))
-        m,l,o=lax.fori_loop(0,cnt%2,lambda t,c: tile(*c,hi),(m,l,o))
-        o=o/l
-        att_ref[i]=o.astype(narrow_type)
-        o_ref[i]=o
-        lse_ref[i]=jnp.broadcast_to(m+jnp.log(l),(8,rows))
-        return 0
-    lax.fori_loop(0,own,one_q,0)
-
-def attention_forward(lengths,x,own,halo):
-    slots,_,width,rows=x.shape
-    n=lengths.shape[0]; marks=-(-n//16)*16
-    V=pl.BlockSpec(memory_space=pltpu.VMEM)
-    return pl.pallas_call(functools.partial(fwd_kernel,n,own,slots,halo,rows,width,marks),
-        out_shape=(jax.ShapeDtypeStruct((own,width,rows),narrow_type),jax.ShapeDtypeStruct((own,8,rows),float_type),jax.ShapeDtypeStruct((own,width,rows),float_type)),
-        in_specs=[pl.BlockSpec(memory_space=pltpu.SMEM),V],out_specs=(V,V,V),
-        scratch_shapes=[pltpu.VMEM((width+marks,rows),narrow_type),pltpu.VMEM((slots,rows,width+marks),narrow_type)],
-        compiler_params=pltpu.CompilerParams(vmem_limit_bytes=40<<20))(lengths,x)
-
-def bwd_kernel(n,own,slots,halo,rows,width,marks, lens_ref,x_ref,g_ref,lse_ref,o_ref,dx_ref,dh_ref,ka,vv,qa,qn,gn,dd,dq):
-    core=lax.rem(lax.axis_index("seq"),2)
-    base=core*(own-halo); shift=core*halo
-    st,en=image_marks(lens_ref,n,marks,rows)
-    pos=lax.broadcasted_iota(jnp.int32,(marks,rows),1)
-    def prep(s,_):
-        p=pos+(base+s)*rows
-        oh=jnp.where((p>=st)&(p<en),1.0,0.0).astype(float_type)
-        kt=jnp.concatenate([x_ref[s,1].astype(float_type),(oh-1.0)*BIG],axis=0)
-        ka[s]=kt.T.astype(narrow_type)
-        vv[s]=x_ref[s,2].astype(float_type).T.astype(narrow_type)
-        return 0
-    lax.fori_loop(0,slots,prep,0)
-    def prepq(i,_):
-        s=i+shift
-        p=pos+(base+s)*rows
-        oh=jnp.where((p>=st)&(p<en),1.0,0.0).astype(narrow_type)
-        qs=x_ref[s,0].astype(float_type)*(width**-0.5)
-        qa[i]=jnp.concatenate([qs.astype(narrow_type),oh],axis=0)
-        qn[i]=qs.T.astype(narrow_type)
-        g=g_ref[i].astype(float_type)
-        gn[i]=g.T.astype(narrow_type)
-        dd[i]=jnp.broadcast_to(jnp.sum(g*o_ref[i],axis=0,keepdims=True),(8,rows))
-        dq[i]=jnp.zeros((width,rows),float_type)
-        return 0
-    lax.fori_loop(0,own,prepq,0)
-    def one_k(s,_):
-        lo,hi=bounds(lens_ref,n,base,rows,s)
-        lo=jnp.maximum(lo-base-shift,0); hi=jnp.minimum(hi-base-shift,own-1)
-        kt=x_ref[s,1]
-        def tile(i,dk,dv):
-            sc=matmul(ka[s],qa[i])
-            pr=jnp.exp(sc-lse_ref[i][0:1])
-            dp=matmul(vv[s],g_ref[i])
-            ds=(pr*(dp-dd[i][0:1])).astype(narrow_type)
-            dq[i]+=matmul(kt,ds)
-            return dk+matmul(ds,qn[i]), dv+matmul(pr.astype(narrow_type),gn[i])
-        z=jnp.zeros((rows,width),float_type)
-        cnt=jnp.maximum(hi-lo+1,0)
-        def two(t,c):
-            c=tile(lo+2*t,*c)
-            return tile(lo+2*t+1,*c)
-        dk,dv=lax.fori_loop(0,cnt//2,two,(z,z))
-        dk,dv=lax.fori_loop(0,cnt%2,lambda t,c: tile(hi,*c),(dk,dv))
-        i=s-shift
-        @pl.when((i>=0)&(i<own))
-        def _():
-            dx_ref[i,1]=dk.T.astype(narrow_type)
-            dx_ref[i,2]=dv.T.astype(narrow_type)
-        @pl.when((i<0)|(i>=own))
-        def _():
-            j=jnp.where(i<0,s,i-own)
-            dh_ref[j,0]=dk.T.astype(narrow_type)
-            dh_ref[j,1]=dv.T.astype(narrow_type)
-        return 0
-    lax.fori_loop(0,slots,one_k,0)
-    def fin(i,_):
-        dx_ref[i,0]=(dq[i]*(width**-0.5)).astype(narrow_type)
-        return 0
-    lax.fori_loop(0,own,fin,0)
-
-def attention_backward(lengths,x,g,lse,o,own,halo):
-    slots,_,width,rows=x.shape
-    n=lengths.shape[0]; marks=-(-n//16)*16
-    V=pl.BlockSpec(memory_space=pltpu.VMEM)
-    return pl.pallas_call(functools.partial(bwd_kernel,n,own,slots,halo,rows,width,marks),
-        out_shape=(jax.ShapeDtypeStruct((own,3,width,rows),narrow_type),jax.ShapeDtypeStruct((halo,2,width,rows),narrow_type)),
-        in_specs=[pl.BlockSpec(memory_space=pltpu.SMEM),V,V,V,V],out_specs=(V,V),
-        scratch_shapes=[pltpu.VMEM((slots,rows,width+marks),narrow_type),pltpu.VMEM((slots,rows,width),narrow_type),
-          pltpu.VMEM((own,width+marks,rows),narrow_type),pltpu.VMEM((own,rows,width),narrow_type),pltpu.VMEM((own,rows,width),narrow_type),
-          pltpu.VMEM((own,8,rows),float_type),pltpu.VMEM((own,width,rows),float_type)],
-        compiler_params=pltpu.CompilerParams(vmem_limit_bytes=48<<20))(lengths,x,g,lse,o)
+def image_range(lens_ref, first, last):
+    low = high = start = jnp.int32(0)
+    for image in range(lens_ref.shape[0]):
+        end = start + lens_ref[image]
+        low = jnp.where((start <= first) & (first < end), start, low)
+        high = jnp.where((start <= last) & (last < end), end - 1, high)
+        start = end
+    return low, high
+
+
+def image_edges(lens_ref, marks, rows):
+    row = lax.broadcasted_iota(jnp.int32, (marks, rows), 0)
+    starts = jnp.full((marks, rows), 1 << 30, jnp.int32)
+    ends = jnp.zeros((marks, rows), jnp.int32)
+    start = jnp.int32(0)
+    for image in range(lens_ref.shape[0]):
+        end = start + lens_ref[image]
+        starts, ends = jnp.where(row == image, start, starts), jnp.where(row == image, end, ends)
+        start = end
+    return starts, ends
+
+
+class Blocks:
+    def __init__(self, lens_ref, own, halo, rows, marks):
+        core = lax.rem(lax.axis_index("seq"), 2)
+        self.lens_ref, self.own, self.rows, self.slots = lens_ref, own, rows, own + halo
+        self.base = core * (own - halo)
+        self.shift = core * halo
+        self.starts, self.ends = image_edges(lens_ref, marks, rows)
+        self.lane = lax.broadcasted_iota(jnp.int32, (marks, rows), 1)
+
+    def marks(self, slot):
+        place = self.lane + (self.base + slot) * self.rows
+        return jnp.where((place >= self.starts) & (place < self.ends), 1.0, 0.0).astype(float_type)
+
+    def reach(self, slot):
+        first = (self.base + slot) * self.rows
+        low, high = image_range(self.lens_ref, first, first + self.rows - 1)
+        return lax.div(low, self.rows) - self.base, lax.div(high, self.rows) - self.base
+
+
+def forward_kernel(
+    own, halo, step, lens_ref, x_ref, att_ref, lse_ref, out_ref, keys, queries, score, weight, item_row, item_low
+):
+    slots, _, width, rows = x_ref.shape
+    blocks = Blocks(lens_ref, own, halo, rows, keys.shape[1] - width)
+    scale = width**-0.5
+
+    @pl.loop(0, slots)
+    def _(slot):
+        block = jnp.concatenate([x_ref[slot, 1].astype(float_type), (blocks.marks(slot) - 1.0) * BIG], axis=0)
+        keys[pl.ds(pl.multiple_of(slot * rows, rows), rows)] = block.T.astype(narrow_type)
+
+    def prepare(i, total):
+        slot = i + blocks.shift
+        queries[i] = jnp.concatenate([x_ref[slot, 0].astype(float_type) * scale, blocks.marks(slot)], axis=0).astype(narrow_type)
+        low, high = blocks.reach(slot)
+        count = lax.div(high - low + step, step)
+        low = jnp.minimum(low, slots - step * count)
+
+        @pl.loop(0, count)
+        def _(j):
+            item_row[total + j] = i
+            item_low[total + j] = low + j * step
+
+        return total + count
+
+    total = lax.fori_loop(0, own, prepare, jnp.int32(0))
+    item_row[total] = item_row[total - 1]
+    item_low[total] = item_low[total - 1]
+
+    def scored(t, side):
+        at = pl.multiple_of(item_low[t] * rows, rows)
+        score[side] = matmul(keys[pl.ds(at, step * rows)], queries[item_row[t]])
+
+    def mixed(t):
+        low = item_low[t]
+        result = matmul(x_ref[low, 2], weight[0:rows])
+        for j in range(1, step):
+            result += matmul(x_ref[low + j, 2], weight[j * rows : (j + 1) * rows])
+        return result
+
+    def soften(fresh, side, highest, summed):
+        highest = jnp.where(fresh, -1e30, highest)
+        summed = jnp.where(fresh, 0.0, summed)
+        s = score[side]
+        higher = jnp.maximum(highest, jnp.max(s, axis=0, keepdims=True))
+        p = jnp.exp(s - higher)
+        fade = jnp.where(fresh, 0.0, jnp.exp(highest - higher))
+        return higher, summed * fade + jnp.sum(p, axis=0, keepdims=True), fade, p
+
+    def finish(t, out, fade, highest, summed):
+        i = item_row[t]
+        out = out * fade + mixed(t)
+        whole = out / summed
+        att_ref[i] = whole.astype(narrow_type)
+        out_ref[i] = whole
+        lse_ref[i] = jnp.broadcast_to(highest + jnp.log(summed), (8, rows))
+        return out
+
+    def turn(t, side, carry):
+        highest, summed, out, fade = carry
+        out = finish(t - 1, out, fade, highest, summed)
+        scored(t + 1, 1 - side)
+        fresh = item_row[t] != item_row[t - 1]
+        highest, summed, fade, p = soften(fresh, side, highest, summed)
+        weight[...] = p.astype(narrow_type)
+        return highest, summed, out, fade
+
+    scored(0, 0)
+    scored(1, 1)
+    highest, summed, fade, p = soften(True, 0, jnp.zeros((1, rows), float_type), jnp.zeros((1, rows), float_type))
+    weight[...] = p.astype(narrow_type)
+    carry = (highest, summed, jnp.zeros((width, rows), float_type), fade)
+    pairs = lax.div(total - 1, 2)
+    carry = lax.fori_loop(0, pairs, lambda j, c: turn(2 * j + 2, 0, turn(2 * j + 1, 1, c)), carry)
+    carry = lax.fori_loop(2 * pairs + 1, total, lambda t, c: turn(t, 1, c), carry)
+    highest, summed, out, fade = carry
+    finish(total - 1, out, fade, highest, summed)
+
+
+def attention_forward(lengths, x, own, halo, step=2):
+    slots, _, width, rows = x.shape
+    marks = -(-lengths.shape[0] // 16) * 16
+    most = own * (slots // step + 2) + 8
+    return pl.pallas_call(
+        functools.partial(forward_kernel, own, halo, step),
+        out_shape=(
+            jax.ShapeDtypeStruct((own, width, rows), narrow_type),
+            jax.ShapeDtypeStruct((own, 8, rows), float_type),
+            jax.ShapeDtypeStruct((own, width, rows), float_type),
+        ),
+        in_specs=[IN_SMEM, IN_VMEM],
+        out_specs=(IN_VMEM, IN_VMEM, IN_VMEM),
+        scratch_shapes=[
+            pltpu.VMEM((slots * rows, width + marks), narrow_type),
+            pltpu.VMEM((own, width + marks, rows), narrow_type),
+            pltpu.VMEM((2, step * rows, rows), float_type),
+            pltpu.VMEM((step * rows, rows), narrow_type),
+            pltpu.SMEM((most,), jnp.int32),
+            pltpu.SMEM((most,), jnp.int32),
+        ],
+        compiler_params=pltpu.CompilerParams(vmem_limit_bytes=32 << 20),
+    )(lengths, x)
+
+
+def backward_kernel(
+    own, halo, step, lens_ref, x_ref, g_ref, lse_ref, out_ref, dq_ref, dkv_ref,
+    keys, values, queries, offset, dq, score, grad_prob, weight, grad_score, item_slot, item_low,
+):
+    slots, _, width, rows = x_ref.shape
+    blocks = Blocks(lens_ref, own, halo, rows, keys.shape[2] - width)
+    scale = width**-0.5
+
+    def prepare(slot, total):
+        block = jnp.concatenate([x_ref[slot, 1].astype(float_type), (blocks.marks(slot) - 1.0) * BIG], axis=0)
+        keys[slot] = block.T.astype(narrow_type)
+        values[slot] = x_ref[slot, 2].astype(float_type).T.astype(narrow_type)
+        dkv_ref[slot] = jnp.zeros((2, width, rows), narrow_type)
+        low, high = blocks.reach(slot)
+        low = jnp.maximum(low - blocks.shift, 0)
+        high = jnp.minimum(high - blocks.shift, own - 1)
+        count = jnp.maximum(lax.div(high - low + step, step), 0)
+        low = jnp.minimum(low, own - step * count)
+
+        @pl.loop(0, count)
+        def _(j):
+            item_slot[total + j] = slot
+            item_low[total + j] = low + j * step
+
+        return total + count
+
+    total = lax.fori_loop(0, slots, prepare, jnp.int32(0))
+    item_slot[total] = item_slot[total - 1]
+    item_low[total] = item_low[total - 1]
+
+    @pl.loop(0, own)
+    def _(i):
+        slot = i + blocks.shift
+        q = x_ref[slot, 0].astype(float_type) * scale
+        queries[i] = jnp.concatenate([q, blocks.marks(slot)], axis=0).astype(narrow_type)
+        g = g_ref[i].astype(float_type)
+        offset[i] = jnp.broadcast_to(jnp.sum(g * out_ref[i], axis=0, keepdims=True), (8, rows))
+        dq[i] = jnp.zeros((width, rows), float_type)
+
+    def scored(t, side):
+        slot, low = item_slot[t], item_low[t]
+        for j in range(step):
+            score[side, j] = matmul(keys[slot], queries[low + j])
+            grad_prob[side, j] = matmul(values[slot], g_ref[low + j])
+
+    def soften(t, side):
+        low = item_low[t]
+        done = []
+        for j in range(step):
+            p = jnp.exp(score[side, j] - lse_ref[low + j, 0:1])
+            d = p * (grad_prob[side, j] - offset[low + j, 0:1])
+            done.append((p.astype(narrow_type), d.astype(narrow_type)))
+        return done
+
+    def keep(done):
+        for j in range(step):
+            weight[j] = done[j][0]
+            grad_score[j] = done[j][1]
+
+    def mixed(t, fresh, dk, dv):
+        slot, low = item_slot[t], item_low[t]
+        dk = jnp.where(fresh, 0.0, dk)
+        dv = jnp.where(fresh, 0.0, dv)
+        key = x_ref[slot, 1]
+        for j in range(step):
+            dk += transposed_right(queries[low + j, 0:width], grad_score[j])
+            dv += transposed_right(g_ref[low + j], weight[j])
+        for j in range(step):
+            dq[low + j] += matmul(key, grad_score[j])
+        dkv_ref[slot, 0] = dk.astype(narrow_type)
+        dkv_ref[slot, 1] = dv.astype(narrow_type)
+        return dk, dv
+
+    def turn(t, side, carry):
+        fresh = (t == 1) | (item_slot[t - 1] != item_slot[jnp.maximum(t - 2, 0)])
+        carry = mixed(t - 1, fresh, *carry)
+        scored(t + 1, 1 - side)
+        keep(soften(t, side))
+        return carry
+
+    scored(0, 0)
+    scored(1, 1)
+    keep(soften(0, 0))
+    zero = jnp.zeros((width, rows), float_type)
+    pairs = lax.div(total - 1, 2)
+    carry = lax.fori_loop(0, pairs, lambda j, c: turn(2 * j + 2, 0, turn(2 * j + 1, 1, c)), (zero, zero))
+    carry = lax.fori_loop(2 * pairs + 1, total, lambda t, c: turn(t, 1, c), carry)
+    mixed(total - 1, item_slot[total - 1] != item_slot[jnp.maximum(total - 2, 0)], *carry)
+
+    @pl.loop(0, own)
+    def _(i):
+        dq_ref[i] = (dq[i] * scale).astype(narrow_type)
+
+
+def attention_backward(lengths, x, g, lse, out, own, halo, step=2):
+    slots, _, width, rows = x.shape
+    marks = -(-lengths.shape[0] // 16) * 16
+    most = slots * (own // step + 2) + 8
+    return pl.pallas_call(
+        functools.partial(backward_kernel, own, halo, step),
+        out_shape=(
+            jax.ShapeDtypeStruct((own, width, rows), narrow_type),
+            jax.ShapeDtypeStruct((slots, 2, width, rows), narrow_type),
+        ),
+        in_specs=[IN_SMEM] + [IN_VMEM] * 4,
+        out_specs=(IN_VMEM, IN_VMEM),
+        scratch_shapes=[
+            pltpu.VMEM((slots, rows, width + marks), narrow_type),
+            pltpu.VMEM((slots, rows, width), narrow_type),
+            pltpu.VMEM((own, width + marks, rows), narrow_type),
+            pltpu.VMEM((own, 8, rows), float_type),
+            pltpu.VMEM((own, width, rows), float_type),
+            pltpu.VMEM((2, step, rows, rows), float_type),
+            pltpu.VMEM((2, step, rows, rows), float_type),
+            pltpu.VMEM((step, rows, rows), narrow_type),
+            pltpu.VMEM((step, rows, rows), narrow_type),
+            pltpu.SMEM((most,), jnp.int32),
+            pltpu.SMEM((most,), jnp.int32),
+        ],
+        compiler_params=pltpu.CompilerParams(vmem_limit_bytes=40 << 20),
+    )(lengths, x, g, lse, out)
 
 
 def layer_on_slice(
@@ -1613,20 +1934,16 @@
     adapter_out_contract,
     cotangent,
 ):
-    row_count, features = tokens.shape
+    row_count = tokens.shape[0]
     depth = lax.axis_size("fsdp")
     devices = lax.axis_size(("seq", "fsdp"))
-    position = lax.axis_index(("seq", "fsdp"))
     own = devices // 2
-    head_width = features // HEADS
-    rank_width = adapter_in_attention.shape[2]
-    share = features // devices
     halo = -(-(LONGEST - 1) // row_count)
 
-    vectors = jnp.concatenate([gain_rows.T, bias_rows.T], axis=1)
-    vectors = jnp.pad(vectors, ((0, 16), (0, rank_width - vectors.shape[1])))
-    vectors = lax.dynamic_update_slice(vectors, expand_bias[None], (share, 0))
     arrays = (
+        gain_rows,
+        bias_rows,
+        expand_bias[None],
         query_key_value,
         output_weight,
         adapter_in_attention,
@@ -1635,39 +1952,41 @@
         adapter_out_contract.T,
         contract_weight,
         adapter_in_contract,
-        adapter_out_expand.T,
-        vectors,
-    )
-    image_ends = jnp.cumsum(lengths)
-    places = position * row_count + jnp.arange(row_count, dtype=jnp.int32)
-    own_image = jnp.sum((places[:, None] >= image_ends[None, :]).astype(jnp.int32), axis=1)
-    matches = own_image[:, None] == jnp.arange(lengths.shape[0], dtype=jnp.int32)[None, :]
-    chosen = jnp.sum(jnp.where(matches, adapter_choice[None, :], 0), axis=1)
-    select = (jnp.arange(rank_width, dtype=jnp.int32)[None, :] // RANK == chosen[:, None]).astype(float_type)
-
-    fa, ve, f2, on_heads, rank = attention_in(tokens, select, arrays, halo, depth, HEADS, devices, 1)
+        adapter_out_expand,
+        expand_weight,
+    )
+    fa, ve, f2, line_a, line_b, on_heads, rank = attention_in(
+        lengths, adapter_choice, tokens, arrays, halo, depth, HEADS, devices, 1
+    )
+
+    def swapped(line, bit):
+        route = [
+            (seq * depth + fsdp, (seq ^ bit) * depth + fsdp)
+            for seq in range(devices // depth)
+            for fsdp in range(depth)
+        ]
+        return lax.ppermute(line, ("seq", "fsdp"), route)
+
+    lines = (
+        line_a,
+        line_b,
+        swapped(line_a, SIDE_Y),
+        swapped(line_b, SIDE_Y),
+        swapped(line_a, SIDE_X),
+        swapped(line_b, SIDE_X),
+    )
     attended, log_totals, attended_wide = attention_forward(lengths, on_heads, own, halo)
     result, grad_middle, terms, grad_on_heads = middle_part(
-        attended, tokens, cotangent, select, fa, ve, f2, expand_weight, depth, 2
-    )
-    grad_blocks, grad_halo = attention_backward(
+        lengths, adapter_choice, attended, tokens, cotangent, fa, ve, f2, lines, depth, 2
+    )
+    grad_queries, grad_key_values = attention_backward(
         lengths, on_heads, grad_on_heads, log_totals, attended_wide, own, halo
     )
     input_gradient, early, late = last_part(
-        grad_blocks, grad_halo, tokens, grad_middle, select, fa, ve, rank, terms, depth, 3
-    )
-    down = jnp.concatenate([late[:, :share], early[None, :share]], axis=0)
-    up = jnp.concatenate([late[:, share:], early[None, share : 2 * share]], axis=0)
-    return (
-        result,
-        input_gradient,
-        down,
-        up.transpose(0, 2, 1),
-        early[64:96],
-        early[96:224],
-        early[224:352].T,
-        early[352:384].T,
-    )
+        lengths, adapter_choice, grad_queries, grad_key_values, tokens, grad_middle, fa, ve, rank, terms, depth, 3
+    )
+    outs = spread(result, input_gradient, early, late)
+    return outs[:3] + (outs[3].transpose(0, 2, 1),) + outs[4:7] + (outs[7].T,)
 
 
 def solution(mesh):

time: 386 us -> 306 us (0.79)
  Pallas kernels: 359 us -> 294 us
  local copies, waits for them, and re-layouts: 23.2 us -> 6.28 us
  starting transfers between devices: 0 us -> 4.14 us
    pallas_call x1, Pallas kernels: 91.6 us -> 55.7 us  [middle_part(): pl.pallas_call(functools.partial(middle_kernel, depth, heads), out_shape=...]
    pallas_call x2 -> x3, Pallas kernels: 65.5 us -> 45.8 us  [the longest x1 27.1 us: attention_backward(): pl.pallas_call(functools.partial(backward_kernel, own, halo, step), out_s...]
    unnamed x44 -> x34, local copies, waits for them, and re-layouts: 18.8 us -> 6.28 us
    pallas_call x1, Pallas kernels: 72.8 us -> 63.6 us  [last_part(): pl.pallas_call(functools.partial(last_kernel, depth, heads, halo), out_sh...]
    ppermute x0 -> x4, starting transfers between devices: none -> 4.14 us  [swapped(): return lax.ppermute(line, ('seq', 'fsdp'), route)]
  transfers between devices with their start and end apart: 0 -> 4, of which waited for: 0 -> 2; matrix products, arithmetic and copies ran while one was open for 0% -> 0% of each run, Pallas kernels for 0% -> 6%
where the time goes in v3:
time: 306 us; the launch traced here: 308 us
  Pallas kernels  294 us (96%)
  local copies, waits for them, and re-layouts  6.28 us (2%)
  starting transfers between devices  4.14 us (1%)
    pallas_call x1, Pallas kernels, attention_in(): pl.pallas_call(functools.partial(attention_in_kernel, depth, halo, heads,...  129 us
    pallas_call x1, Pallas kernels, last_part(): pl.pallas_call(functools.partial(last_kernel, depth, heads, halo), out_sh...  63.6 us
    pallas_call x1, Pallas kernels, middle_part(): pl.pallas_call(functools.partial(middle_kernel, depth, heads), out_shape=...  55.7 us
    pallas_call x1, Pallas kernels, attention_backward(): pl.pallas_call(functools.partial(backward_kernel, own, halo, step), out_s...  27.1 us
    pallas_call x1, Pallas kernels, attention_forward(): pl.pallas_call(functools.partial(forward_kernel, own, halo, step), out_sh...  17.4 us
    unnamed x34, local copies, waits for them, and re-layouts  6.28 us
  transfers between devices with their start and end apart: 4, of which 2 were waited for; matrix products, arithmetic and copies ran while one was open for 0% of the time, Pallas kernels for 6%

profile of v3, /device:TPU:0, one launch (start us, length us, event | category | flops | bytes accessed | tf_op | source)
XLA Modules:
  0.0 307.7 jit_solution(12527168788880158993)
XLA Ops:
  0.6 129.2 %shard_map.224 = (bf16[32,32,5376]{2,1,0:T(8,128)(2,1)}, bf16[32,48,128]{2,1,0:T(8,128)(2,1)}, bf16[32,128,1280]{2,1,0:T(8,128)(2,1)}, bf16[4,32,2048]{2,1,0:T(8...) custom-call(s32[8]{0:T(128)} %lens_ref.9, s32[8]{0:T(128)} %choice_ref.5, ...), custom_call_target="tpu_custom_call" | custom-call | tf_op jit(solution)/shard_map/pallas_call | solution.py:863
  129.9 0.4 collective-permute-start.2
  130.3 2.7 collective-permute-start
  133.0 0.1 collective-permute-start.3
  133.1 0.9 collective-permute-start.1
  134.0 0.0 copy-start
  134.0 1.6 copy-done
  135.6 0.0 copy-start.10
  135.6 0.7 copy-done.10
  136.3 17.4 %shard_map.225 = (bf16[16,64,256]{2,1,0:T(8,128)(2,1)S(1)}, f32[16,8,256]{2,1,0:T(8,128)S(1)}, f32[16,64,256]{2,1,0:T(8,128)S(1)}) custom-call(s32[8]{0:T(128)S(1)} %copy-done.10, bf16[22,3,64,256]{3,2,1,0:T(8,128)(2,1)S(1)} %copy-done), custom_call_target="tpu_custom_call" | custom-call | tf_op jit(solution)/shard_map/pallas_call | solution.py:1774
  153.6 0.0 copy-start.7
  153.6 0.8 copy-done.7
  154.4 0.0 collective-permute-done.2.xa
  154.4 0.0 copy-start.13
  154.4 0.0 collective-permute-done.ya
  154.4 0.0 copy-start.14
  154.5 1.1 collective-permute-done.3.xb
  155.6 0.0 copy-start.15
  155.6 1.0 collective-permute-done.1.yb
  156.6 0.0 copy-start.16
  156.6 0.0 copy-done.13
  156.6 0.0 copy-done.14
  156.6 0.0 copy-done.15
  156.6 0.8 copy-done.16
  157.4 0.0 copy-start.1
  157.4 0.0 copy-start.11
  157.4 0.0 copy-start.4
  157.4 0.0 copy-start.9
  157.4 0.0 copy-start.12
  157.4 55.7 %shard_map.226 = (bf16[256,1024]{1,0:T(8,128)(2,1)}, f32[256,1024]{1,0:T(8,128)}, bf16[32,384,128]{2,1,0:T(8,128)(2,1)}, bf16[16,64,256]{2,1,0:T(8,128)(2,1)}) custom-call(s32[8]{0:T(128)} %lens_ref.9, s32[8]{0:T(128)} %choice_ref.5, bf16[16,64,256]{2,1,0:T(8,128)(2,1)} %copy-done.7, bf16[256,1024]{1,0:T(8,128)(2,1)} %tok_ref.3, bf16[256,1024]{1,0:T(8,128)(2,1)} %cot_ref.1, ...), custom_call_target="tpu_custom_call" | custom-call | tf_op jit(solution)/shard_map/pallas_call | solution.py:1214
  213.1 0.0 copy-start.2
  213.1 0.0 copy-start.3
  213.1 0.0 copy-done.1
  213.1 0.0 copy-done.11
  213.2 0.0 copy-start.8
  213.2 1.2 copy-done.8
  214.3 27.1 %shard_map.227 = (bf16[16,64,256]{2,1,0:T(8,128)(2,1)S(1)}, bf16[22,2,64,256]{3,2,1,0:T(8,128)(2,1)S(1)}) custom-call(s32[8]{0:T(128)S(1)} %copy-done.11, bf16[22,3,64,256]{3,2,1,0:T(8,128)(2,1)S(1)} %copy-done.1, bf16[16,64,256]{2,1,0:T(8,128)(2,1)S(1)} %copy-done.8, f32[16,8,256]{2,1,0:T(8,128)S(1)} %get-tuple-element.44.lse_ref, ...), custom_call_target="tpu_custom_call" | custom-call | tf_op jit(solution)/shard_map/pallas_call | solution.py:1893
  241.5 0.0 copy-done.4
  241.5 0.0 copy-done.9
  241.5 0.0 copy-done.12
  241.5 0.0 copy-done.2
  241.5 0.0 copy-done.3
  241.5 0.0 copy-start.5
  241.5 1.2 copy-done.5
  242.7 0.0 copy-start.6
  242.8 63.6 %shard_map.228 = (f32[256,1024]{1,0:T(8,128)S(1)}, f32[384,128]{1,0:T(8,128)S(1)}, f32[3,64,128]{2,1,0:T(8,128)S(1)}) custom-call(s32[8]{0:T(128)S(1)} %copy-done.11, s32[8]{0:T(128)S(1)} %copy-done.12, bf16[16,64,256]{2,1,0:T(8,128)(2,1)S(1)} %get-tuple-element.46.dq_ref, bf16[22,2,64,256]{3,2,1,0:T(8,128)(2,1)S(1)} %get-tuple-element.47.dkv_ref, ...), custom_call_target="tpu_custom_call" | custom-call | tf_op jit(solution)/shard_map/pallas_call | solution.py:1583
  306.4 0.0 copy-done.6
  306.4 1.3 shard_map.229
Async XLA Ops:
  129.9 24.6 %collective-permute-start.2 = (bf16[4,32,2048]{2,1,0:T(8,128)(2,1)}, bf16[4,32,2048]{2,1,0:T(8,128)(2,1)S(1)}, u32[]{:S(2)}, u32[]{:S(2)}) collective-permute-start(bf16[4,32,2048]{2,1,0:T(8,128)(2,1)} %get-tuple-element.40.line_a), channel_id=1, source_target_pairs={{0,8},{1,9},{2,10},{3,11},{4,12},{5,13},{6,14},{7,15},{8,0},{9,1},... | collective-permute-start | bytes 1572872 | tf_op jit(solution)/shard_map/ppermute | solution.py:1968
  130.3 24.2 %collective-permute-start = (bf16[4,32,2048]{2,1,0:T(8,128)(2,1)}, bf16[4,32,2048]{2,1,0:T(8,128)(2,1)S(1)}, u32[]{:S(2)}, u32[]{:S(2)}) collective-permute-start(bf16[4,32,2048]{2,1,0:T(8,128)(2,1)} %get-tuple-element.40.line_a), channel_id=1, source_target_pairs={{0,16},{1,17},{2,18},{3,19},{4,20},{5,21},{6,22},{7,23},{8,24},{9,... | collective-permute-start | bytes 1572872 | tf_op jit(solution)/shard_map/ppermute | solution.py:1968
  133.0 22.6 %collective-permute-start.3 = (bf16[4,32,2048]{2,1,0:T(8,128)(2,1)}, bf16[4,32,2048]{2,1,0:T(8,128)(2,1)S(1)}, u32[]{:S(2)}, u32[]{:S(2)}) collective-permute-start(bf16[4,32,2048]{2,1,0:T(8,128)(2,1)} %get-tuple-element.41.line_b), channel_id=1, source_target_pairs={{0,8},{1,9},{2,10},{3,11},{4,12},{5,13},{6,14},{7,15},{8,0},{9,1},... | collective-permute-start | bytes 1572872 | tf_op jit(solution)/shard_map/ppermute | solution.py:1968
  133.1 23.6 %collective-permute-start.1 = (bf16[4,32,2048]{2,1,0:T(8,128)(2,1)}, bf16[4,32,2048]{2,1,0:T(8,128)(2,1)S(1)}, u32[]{:S(2)}, u32[]{:S(2)}) collective-permute-start(bf16[4,32,2048]{2,1,0:T(8,128)(2,1)} %get-tuple-element.41.line_b), channel_id=1, source_target_pairs={{0,16},{1,17},{2,18},{3,19},{4,20},{5,21},{6,22},{7,23},{8,24},{9,... | collective-permute-start | bytes 1572872 | tf_op jit(solution)/shard_map/ppermute | solution.py:1968
  134.0 1.6 copy-start
  135.6 0.7 copy-start.10
  153.6 0.8 copy-start.7
  154.4 2.2 copy-start.13
  154.4 2.2 copy-start.14
  155.6 1.1 copy-start.15
  156.6 0.8 copy-start.16
  157.4 55.7 %copy-start.1 = (bf16[22,3,64,256]{3,2,1,0:T(8,128)(2,1)S(1)}, bf16[22,3,64,256]{3,2,1,0:T(8,128)(2,1)}, u32[]{:S(2)}) copy-start(bf16[22,3,64,256]{3,2,1,0:T(8,128)(2,1)} %get-tuple-element.35.x_ref) | copy-start | bytes 6488068
  157.4 55.7 %copy-start.11 = (s32[8]{0:T(128)S(1)}, s32[8]{0:T(128)}, u32[]{:S(2)}) copy-start(s32[8]{0:T(128)} %lens_ref.9) | copy-start | bytes 100
  157.4 84.1 %copy-start.4 = (bf16[32,48,128]{2,1,0:T(8,128)(2,1)S(1)}, bf16[32,48,128]{2,1,0:T(8,128)(2,1)}, u32[]{:S(2)}) copy-start(bf16[32,48,128]{2,1,0:T(8,128)(2,1)} %get-tuple-element.38.ve) | copy-start | bytes 1179652
  157.4 84.1 %copy-start.9 = (bf16[3,256,128]{2,1,0:T(8,128)(2,1)S(1)}, bf16[3,256,128]{2,1,0:T(8,128)(2,1)}, u32[]{:S(2)}) copy-start(bf16[3,256,128]{2,1,0:T(8,128)(2,1)} %get-tuple-element.49.rank_ref) | copy-start | bytes 589828
  157.4 84.1 %copy-start.12 = (s32[8]{0:T(128)S(1)}, s32[8]{0:T(128)}, u32[]{:S(2)}) copy-start(s32[8]{0:T(128)} %choice_ref.5) | copy-start | bytes 100
  213.1 28.4 %copy-start.2 = (bf16[256,1024]{1,0:T(8,128)(2,1)S(1)}, bf16[256,1024]{1,0:T(8,128)(2,1)}, u32[]{:S(2)}) copy-start(bf16[256,1024]{1,0:T(8,128)(2,1)} %tok_ref.3) | copy-start | bytes 1572868
  213.1 28.4 %copy-start.3 = (bf16[32,384,128]{2,1,0:T(8,128)(2,1)S(1)}, bf16[32,384,128]{2,1,0:T(8,128)(2,1)}, u32[]{:S(2)}) copy-start(bf16[32,384,128]{2,1,0:T(8,128)(2,1)} %get-tuple-element.50.early_terms) | copy-start | bytes 9437188
  213.2 1.2 copy-start.8
  241.5 1.2 copy-start.5
  242.7 63.6 %copy-start.6 = (bf16[256,1024]{1,0:T(8,128)(2,1)S(1)}, bf16[256,1024]{1,0:T(8,128)(2,1)}, u32[]{:S(2)}) copy-start(bf16[256,1024]{1,0:T(8,128)(2,1)} %get-tuple-element.42.result_in) | copy-start | bytes 1572868

commit v4 on v3

--- a/solution.py
+++ b/solution.py
@@ -784,14 +784,41 @@
         for copy in outs:
             copy.start()
 
+    def exchanged():
+        @pl.loop(0, own)
+        def _(k):
+            @pl.when(swap.away_block(k))
+            def _():
+                for p in range(3):
+                    arrival(p, k).wait_recv()
+
+        @pl.when(half == core)
+        def _():
+            for p in range(3):
+                kept(p).wait()
+
+        first = jnp.where(core == 0, own - halo, own)
+        over = remote(
+            y_ref.at[pl.ds(first - base, halo), 1:3],
+            y_ref.at[pl.ds(first - (own - halo) * (1 - core), halo), 1:3],
+            piece_send.at[3, 0],
+            piece_receive.at[3, 0],
+            seq ^ CORES,
+            fsdp,
+        )
+        over.start()
+        return over
+
     steps = (gather.own, gather.inner, gather.outer, gather.first, gather.second, gather.third, gather.finish)
-    for turn in range(-LOOKAHEAD, len(chunks) + 3):
-        for delay, step in zip((-LOOKAHEAD, -2, -1, 0, 1, 2, 3), steps):
+    for turn in range(DELAYS[0], len(chunks) + DELAYS[-1]):
+        if turn == len(chunks) - 2:
+            over = exchanged()
+        for delay, step in zip(DELAYS, steps):
             index = turn - delay
-            if not 0 <= index < len(chunks) or (delay == -LOOKAHEAD and index in early):
+            if not 0 <= index < len(chunks) or (delay == DELAYS[0] and index in early):
                 continue
             chunk = chunks[index]
-            if delay == -2 and index in first_hidden:
+            if delay == DELAYS[1] and index in first_hidden:
                 for copy in own_shards:
                     copy.wait()
             if chunk[4] == LINE and delay == 0:
@@ -804,28 +831,6 @@
                 if index == after_attention:
                     store()
 
-    @pl.loop(0, own)
-    def _(k):
-        @pl.when(swap.away_block(k))
-        def _():
-            for p in range(3):
-                arrival(p, k).wait_recv()
-
-    @pl.when(half == core)
-    def _():
-        for p in range(3):
-            kept(p).wait()
-
-    first = jnp.where(core == 0, own - halo, own)
-    over = remote(
-        y_ref.at[pl.ds(first - base, halo), 1:3],
-        y_ref.at[pl.ds(first - (own - halo) * (1 - core), halo), 1:3],
-        piece_send.at[3, 0],
-        piece_receive.at[3, 0],
-        seq ^ CORES,
-        fsdp,
-    )
-    over.start()
     over.wait()
 
     @pl.loop(0, heads)
@@ -853,12 +858,12 @@
     middle = 3 * wide + (total - 3 * wide) // 2
     chunks.append(("fa", slice(0, share), slice(3 * wide, middle), 0))
     chunks.append(("fa", slice(0, share), slice(middle, total), 1))
-    for part in range(0, hidden_share, 32):
-        chunks.append(("f2", slice(part, part + 32), slice(0, wide // 2), 0))
-        chunks.append(("f2", slice(part, part + 32), slice(wide // 2, wide), 1))
-    for part in range(0, hidden_total // 2, 1024):
-        chunks.append(("a", slice(0, share), slice(part, part + 1024), 0))
-        chunks.append(("b", slice(0, share), slice(part, part + 1024), 1))
+    for part in range(0, hidden_share, 64):
+        chunks.append(("f2", slice(part, part + 64), slice(0, wide // 2), 0))
+        chunks.append(("f2", slice(part, part + 64), slice(wide // 2, wide), 1))
+    for part in range(0, hidden_total // 2, 2048):
+        chunks.append(("a", slice(0, share), slice(part, part + 2048), 0))
+        chunks.append(("b", slice(0, share), slice(part, part + 2048), 1))
     copies = Gather.STEPS * len(chunks)
     return pl.pallas_call(
         functools.partial(attention_in_kernel, depth, halo, heads, chunks),
@@ -901,7 +906,7 @@
     )(lengths, choice, tokens, *arrays)
 
 
-LOOKAHEAD = 5
+DELAYS = (-9, -6, -3, 0, 1, 2, 3)
 HIDDEN_TILE = 512
 
 
@@ -1688,7 +1693,7 @@
 
 
 def forward_kernel(
-    own, halo, step, lens_ref, x_ref, att_ref, lse_ref, out_ref, keys, queries, score, weight, item_row, item_low
+    own, halo, step, lens_ref, x_ref, att_ref, lse_ref, out_ref, keys, queries, values, score, weight, item_row, item_low
 ):
     slots, _, width, rows = x_ref.shape
     blocks = Blocks(lens_ref, own, halo, rows, keys.shape[1] - width)
@@ -1698,6 +1703,8 @@
     def _(slot):
         block = jnp.concatenate([x_ref[slot, 1].astype(float_type), (blocks.marks(slot) - 1.0) * BIG], axis=0)
         keys[pl.ds(pl.multiple_of(slot * rows, rows), rows)] = block.T.astype(narrow_type)
+        values[slot, 0:width] = x_ref[slot, 2]
+        values[slot, width:] = jnp.ones((16, rows), narrow_type)
 
     def prepare(i, total):
         slot = i + blocks.shift
@@ -1723,48 +1730,46 @@
 
     def mixed(t):
         low = item_low[t]
-        result = matmul(x_ref[low, 2], weight[0:rows])
+        result = matmul(values[low], weight[0:rows])
         for j in range(1, step):
-            result += matmul(x_ref[low + j, 2], weight[j * rows : (j + 1) * rows])
+            result += matmul(values[low + j], weight[j * rows : (j + 1) * rows])
         return result
 
-    def soften(fresh, side, highest, summed):
+    def soften(fresh, side, highest):
         highest = jnp.where(fresh, -1e30, highest)
-        summed = jnp.where(fresh, 0.0, summed)
         s = score[side]
         higher = jnp.maximum(highest, jnp.max(s, axis=0, keepdims=True))
-        p = jnp.exp(s - higher)
         fade = jnp.where(fresh, 0.0, jnp.exp(highest - higher))
-        return higher, summed * fade + jnp.sum(p, axis=0, keepdims=True), fade, p
-
-    def finish(t, out, fade, highest, summed):
+        return higher, fade, jnp.exp(s - higher).astype(narrow_type)
+
+    def finish(t, out, fade, highest):
         i = item_row[t]
         out = out * fade + mixed(t)
-        whole = out / summed
+        summed = out[width : width + 1]
+        whole = out[0:width] / summed
         att_ref[i] = whole.astype(narrow_type)
         out_ref[i] = whole
         lse_ref[i] = jnp.broadcast_to(highest + jnp.log(summed), (8, rows))
         return out
 
     def turn(t, side, carry):
-        highest, summed, out, fade = carry
-        out = finish(t - 1, out, fade, highest, summed)
+        highest, out, fade = carry
+        out = finish(t - 1, out, fade, highest)
         scored(t + 1, 1 - side)
-        fresh = item_row[t] != item_row[t - 1]
-        highest, summed, fade, p = soften(fresh, side, highest, summed)
-        weight[...] = p.astype(narrow_type)
-        return highest, summed, out, fade
+        highest, fade, p = soften(item_row[t] != item_row[t - 1], side, highest)
+        weight[...] = p
+        return highest, out, fade
 
     scored(0, 0)
     scored(1, 1)
-    highest, summed, fade, p = soften(True, 0, jnp.zeros((1, rows), float_type), jnp.zeros((1, rows), float_type))
-    weight[...] = p.astype(narrow_type)
-    carry = (highest, summed, jnp.zeros((width, rows), float_type), fade)
+    highest, fade, p = soften(True, 0, jnp.zeros((1, rows), float_type))
+    weight[...] = p
+    carry = (highest, jnp.zeros((width + 16, rows), float_type), fade)
     pairs = lax.div(total - 1, 2)
     carry = lax.fori_loop(0, pairs, lambda j, c: turn(2 * j + 2, 0, turn(2 * j + 1, 1, c)), carry)
     carry = lax.fori_loop(2 * pairs + 1, total, lambda t, c: turn(t, 1, c), carry)
-    highest, summed, out, fade = carry
-    finish(total - 1, out, fade, highest, summed)
+    highest, out, fade = carry
+    finish(total - 1, out, fade, highest)
 
 
 def attention_forward(lengths, x, own, halo, step=2):
@@ -1783,6 +1788,7 @@
         scratch_shapes=[
             pltpu.VMEM((slots * rows, width + marks), narrow_type),
             pltpu.VMEM((own, width + marks, rows), narrow_type),
+            pltpu.VMEM((slots, width + 16, rows), narrow_type),
             pltpu.VMEM((2, step * rows, rows), float_type),
             pltpu.VMEM((step * rows, rows), narrow_type),
             pltpu.SMEM((most,), jnp.int32),
@@ -1867,9 +1873,10 @@
 
     def turn(t, side, carry):
         fresh = (t == 1) | (item_slot[t - 1] != item_slot[jnp.maximum(t - 2, 0)])
+        scored(t + 1, 1 - side)
+        done = soften(t, side)
         carry = mixed(t - 1, fresh, *carry)
-        scored(t + 1, 1 - side)
-        keep(soften(t, side))
+        keep(done)
         return carry
 
     scored(0, 0)
@@ -1886,7 +1893,7 @@
         dq_ref[i] = (dq[i] * scale).astype(narrow_type)
 
 
-def attention_backward(lengths, x, g, lse, out, own, halo, step=2):
+def attention_backward(lengths, x, g, lse, out, own, halo, step=1):
     slots, _, width, rows = x.shape
     marks = -(-lengths.shape[0] // 16) * 16
     most = slots * (own // step + 2) + 8

time: 306 us -> 293 us (0.958)
  Pallas kernels: 294 us -> 278 us
    pallas_call x1, Pallas kernels: 129 us -> 118 us  [attention_in(): pl.pallas_call(functools.partial(attention_in_kernel, depth, halo, heads,...]
  transfers between devices with their start and end apart: 4 -> 4, of which waited for: 2 -> 2; matrix products, arithmetic and copies ran while one was open for 0% -> 0% of each run, Pallas kernels for 6% -> 5%
where the time goes in v4:
time: 293 us; the launch traced here: 294 us
  Pallas kernels  278 us (95%)
  local copies, waits for them, and re-layouts  6.28 us (2%)
  waiting for transfers between devices  4.13 us (1%)
  starting transfers between devices  4.12 us (1%)
    pallas_call x1, Pallas kernels, attention_in(): pl.pallas_call(functools.partial(attention_in_kernel, depth, halo, heads,...  118 us
    pallas_call x1, Pallas kernels, last_part(): pl.pallas_call(functools.partial(last_kernel, depth, heads, halo), out_sh...  63.7 us
    pallas_call x1, Pallas kernels, middle_part(): pl.pallas_call(functools.partial(middle_kernel, depth, heads), out_shape=...  54.9 us
    pallas_call x1, Pallas kernels, attention_backward(): pl.pallas_call(functools.partial(backward_kernel, own, halo, step), out_s...  24.4 us
    pallas_call x1, Pallas kernels, attention_forward(): pl.pallas_call(functools.partial(forward_kernel, own, halo, step), out_sh...  15.8 us
    unnamed x34, local copies, waits for them, and re-layouts  6.28 us
  transfers between devices with their start and end apart: 4, of which 2 were waited for; matrix products, arithmetic and copies ran while one was open for 0% of the time, Pallas kernels for 5%

profile of v4, /device:TPU:0, one launch (start us, length us, event | category | flops | bytes accessed | tf_op | source)
XLA Modules:
  0.0 293.7 jit_solution(2814248711819625673)
XLA Ops:
  0.6 118.3 %shard_map.224 = (bf16[32,32,5376]{2,1,0:T(8,128)(2,1)}, bf16[32,48,128]{2,1,0:T(8,128)(2,1)}, bf16[32,128,1280]{2,1,0:T(8,128)(2,1)}, bf16[4,32,2048]{2,1,0:T(8...) custom-call(s32[8]{0:T(128)} %lens_ref.9, s32[8]{0:T(128)} %choice_ref.5, ...), custom_call_target="tpu_custom_call" | custom-call | tf_op jit(solution)/shard_map/pallas_call | solution.py:868
  119.0 1.4 collective-permute-start.2
  120.4 0.0 collective-permute-start
  120.4 0.7 collective-permute-start.3
  121.1 2.0 collective-permute-start.1
  123.1 0.0 copy-start
  123.1 1.6 copy-done
  124.7 0.0 copy-start.10
  124.7 0.7 copy-done.10
  125.3 15.8 %shard_map.225 = (bf16[16,64,256]{2,1,0:T(8,128)(2,1)S(1)}, f32[16,8,256]{2,1,0:T(8,128)S(1)}, f32[16,64,256]{2,1,0:T(8,128)S(1)}) custom-call(s32[8]{0:T(128)S(1)} %copy-done.10, bf16[22,3,64,256]{3,2,1,0:T(8,128)(2,1)S(1)} %copy-done), custom_call_target="tpu_custom_call" | custom-call | tf_op jit(solution)/shard_map/pallas_call | solution.py:1779
  141.1 0.0 copy-start.7
  141.1 0.8 copy-done.7
  141.9 0.0 collective-permute-done.2.xa
  141.9 0.0 copy-start.13
  141.9 0.0 collective-permute-done.ya
  141.9 0.0 copy-start.14
  142.0 3.0 %collective-permute-done.3.xb = bf16[4,32,2048]{2,1,0:T(8,128)(2,1)S(1)} collective-permute-done((bf16[4,32,2048]{2,1,0:T(8,128)(2,1)}, bf16[4,32,2048]{2,1,0:T(8,128)(2,1)S(1)}, u32[]{:S(2)}, u32[]{:S(2)}) %collective-permute-start.3) | collective-permute-done | bytes 524320 | tf_op jit(solution)/shard_map/ppermute | solution.py:1975
  145.0 0.0 copy-start.15
  145.0 1.1 collective-permute-done.1.yb
  146.1 0.0 copy-start.16
  146.1 0.0 copy-done.13
  146.1 0.0 copy-done.14
  146.1 0.0 copy-done.15
  146.1 0.8 copy-done.16
  146.9 0.0 copy-start.1
  146.9 0.0 copy-start.11
  146.9 0.0 copy-start.4
  146.9 0.0 copy-start.9
  146.9 0.0 copy-start.12
  146.9 54.9 %shard_map.226 = (bf16[256,1024]{1,0:T(8,128)(2,1)}, f32[256,1024]{1,0:T(8,128)}, bf16[32,384,128]{2,1,0:T(8,128)(2,1)}, bf16[16,64,256]{2,1,0:T(8,128)(2,1)}) custom-call(s32[8]{0:T(128)} %lens_ref.9, s32[8]{0:T(128)} %choice_ref.5, bf16[16,64,256]{2,1,0:T(8,128)(2,1)} %copy-done.7, bf16[256,1024]{1,0:T(8,128)(2,1)} %tok_ref.3, bf16[256,1024]{1,0:T(8,128)(2,1)} %cot_ref.1, ...), custom_call_target="tpu_custom_call" | custom-call | tf_op jit(solution)/shard_map/pallas_call | solution.py:1219
  201.8 0.0 copy-start.2
  201.8 0.0 copy-start.3
  201.8 0.0 copy-done.1
  201.8 0.0 copy-done.11
  201.8 0.0 copy-start.8
  201.8 1.2 copy-done.8
  203.0 24.4 %shard_map.227 = (bf16[16,64,256]{2,1,0:T(8,128)(2,1)S(1)}, bf16[22,2,64,256]{3,2,1,0:T(8,128)(2,1)S(1)}) custom-call(s32[8]{0:T(128)S(1)} %copy-done.11, bf16[22,3,64,256]{3,2,1,0:T(8,128)(2,1)S(1)} %copy-done.1, bf16[16,64,256]{2,1,0:T(8,128)(2,1)S(1)} %copy-done.8, f32[16,8,256]{2,1,0:T(8,128)S(1)} %get-tuple-element.44.lse_ref, ...), custom_call_target="tpu_custom_call" | custom-call | tf_op jit(solution)/shard_map/pallas_call | solution.py:1900
  227.4 0.0 copy-done.4
  227.5 0.0 copy-done.9
  227.5 0.0 copy-done.12
  227.5 0.0 copy-done.2
  227.5 0.0 copy-done.3
  227.5 0.0 copy-start.5
  227.5 1.2 copy-done.5
  228.7 0.0 copy-start.6
  228.7 63.7 %shard_map.228 = (f32[256,1024]{1,0:T(8,128)S(1)}, f32[384,128]{1,0:T(8,128)S(1)}, f32[3,64,128]{2,1,0:T(8,128)S(1)}) custom-call(s32[8]{0:T(128)S(1)} %copy-done.11, s32[8]{0:T(128)S(1)} %copy-done.12, bf16[16,64,256]{2,1,0:T(8,128)(2,1)S(1)} %get-tuple-element.46.dq_ref, bf16[22,2,64,256]{3,2,1,0:T(8,128)(2,1)S(1)} %get-tuple-element.47.dkv_ref, ...), custom_call_target="tpu_custom_call" | custom-call | tf_op jit(solution)/shard_map/pallas_call | solution.py:1588
  292.4 0.0 copy-done.6
  292.4 1.3 shard_map.229
Async XLA Ops:
  119.0 23.0 %collective-permute-start.2 = (bf16[4,32,2048]{2,1,0:T(8,128)(2,1)}, bf16[4,32,2048]{2,1,0:T(8,128)(2,1)S(1)}, u32[]{:S(2)}, u32[]{:S(2)}) collective-permute-start(bf16[4,32,2048]{2,1,0:T(8,128)(2,1)} %get-tuple-element.40.line_a), channel_id=1, source_target_pairs={{0,8},{1,9},{2,10},{3,11},{4,12},{5,13},{6,14},{7,15},{8,0},{9,1},... | collective-permute-start | bytes 1572872 | tf_op jit(solution)/shard_map/ppermute | solution.py:1975
  120.4 21.6 %collective-permute-start = (bf16[4,32,2048]{2,1,0:T(8,128)(2,1)}, bf16[4,32,2048]{2,1,0:T(8,128)(2,1)S(1)}, u32[]{:S(2)}, u32[]{:S(2)}) collective-permute-start(bf16[4,32,2048]{2,1,0:T(8,128)(2,1)} %get-tuple-element.40.line_a), channel_id=1, source_target_pairs={{0,16},{1,17},{2,18},{3,19},{4,20},{5,21},{6,22},{7,23},{8,24},{9,... | collective-permute-start | bytes 1572872 | tf_op jit(solution)/shard_map/ppermute | solution.py:1975
  120.4 24.6 %collective-permute-start.3 = (bf16[4,32,2048]{2,1,0:T(8,128)(2,1)}, bf16[4,32,2048]{2,1,0:T(8,128)(2,1)S(1)}, u32[]{:S(2)}, u32[]{:S(2)}) collective-permute-start(bf16[4,32,2048]{2,1,0:T(8,128)(2,1)} %get-tuple-element.41.line_b), channel_id=1, source_target_pairs={{0,8},{1,9},{2,10},{3,11},{4,12},{5,13},{6,14},{7,15},{8,0},{9,1},... | collective-permute-start | bytes 1572872 | tf_op jit(solution)/shard_map/ppermute | solution.py:1975
  121.1 25.0 %collective-permute-start.1 = (bf16[4,32,2048]{2,1,0:T(8,128)(2,1)}, bf16[4,32,2048]{2,1,0:T(8,128)(2,1)S(1)}, u32[]{:S(2)}, u32[]{:S(2)}) collective-permute-start(bf16[4,32,2048]{2,1,0:T(8,128)(2,1)} %get-tuple-element.41.line_b), channel_id=1, source_target_pairs={{0,16},{1,17},{2,18},{3,19},{4,20},{5,21},{6,22},{7,23},{8,24},{9,... | collective-permute-start | bytes 1572872 | tf_op jit(solution)/shard_map/ppermute | solution.py:1975
  123.1 1.6 copy-start
  124.7 0.7 copy-start.10
  141.1 0.8 copy-start.7
  141.9 4.2 %copy-start.13 = (bf16[4,32,2048]{2,1,0:T(8,128)(2,1)}, bf16[4,32,2048]{2,1,0:T(8,128)(2,1)S(1)}, u32[]{:S(2)}) copy-start(bf16[4,32,2048]{2,1,0:T(8,128)(2,1)S(1)} %collective-permute-done.2.xa) | copy-start | bytes 1572868
  141.9 4.1 %copy-start.14 = (bf16[4,32,2048]{2,1,0:T(8,128)(2,1)}, bf16[4,32,2048]{2,1,0:T(8,128)(2,1)S(1)}, u32[]{:S(2)}) copy-start(bf16[4,32,2048]{2,1,0:T(8,128)(2,1)S(1)} %collective-permute-done.ya) | copy-start | bytes 1572868
  145.0 1.1 copy-start.15
  146.1 0.8 copy-start.16
  146.9 54.9 %copy-start.1 = (bf16[22,3,64,256]{3,2,1,0:T(8,128)(2,1)S(1)}, bf16[22,3,64,256]{3,2,1,0:T(8,128)(2,1)}, u32[]{:S(2)}) copy-start(bf16[22,3,64,256]{3,2,1,0:T(8,128)(2,1)} %get-tuple-element.35.x_ref) | copy-start | bytes 6488068
  146.9 55.0 %copy-start.11 = (s32[8]{0:T(128)S(1)}, s32[8]{0:T(128)}, u32[]{:S(2)}) copy-start(s32[8]{0:T(128)} %lens_ref.9) | copy-start | bytes 100
  146.9 80.6 %copy-start.4 = (bf16[32,48,128]{2,1,0:T(8,128)(2,1)S(1)}, bf16[32,48,128]{2,1,0:T(8,128)(2,1)}, u32[]{:S(2)}) copy-start(bf16[32,48,128]{2,1,0:T(8,128)(2,1)} %get-tuple-element.38.ve) | copy-start | bytes 1179652
  146.9 80.6 %copy-start.9 = (bf16[3,256,128]{2,1,0:T(8,128)(2,1)S(1)}, bf16[3,256,128]{2,1,0:T(8,128)(2,1)}, u32[]{:S(2)}) copy-start(bf16[3,256,128]{2,1,0:T(8,128)(2,1)} %get-tuple-element.49.rank_ref) | copy-start | bytes 589828
  146.9 80.6 %copy-start.12 = (s32[8]{0:T(128)S(1)}, s32[8]{0:T(128)}, u32[]{:S(2)}) copy-start(s32[8]{0:T(128)} %choice_ref.5) | copy-start | bytes 100
  201.8 25.7 %copy-start.2 = (bf16[256,1024]{1,0:T(8,128)(2,1)S(1)}, bf16[256,1024]{1,0:T(8,128)(2,1)}, u32[]{:S(2)}) copy-start(bf16[256,1024]{1,0:T(8,128)(2,1)} %tok_ref.3) | copy-start | bytes 1572868
  201.8 25.7 %copy-start.3 = (bf16[32,384,128]{2,1,0:T(8,128)(2,1)S(1)}, bf16[32,384,128]{2,1,0:T(8,128)(2,1)}, u32[]{:S(2)}) copy-start(bf16[32,384,128]{2,1,0:T(8,128)(2,1)} %get-tuple-element.50.early_terms) | copy-start | bytes 9437188
  201.8 1.2 copy-start.8
  227.5 1.2 copy-start.5
  228.7 63.7 %copy-start.6 = (bf16[256,1024]{1,0:T(8,128)(2,1)S(1)}, bf16[256,1024]{1,0:T(8,128)(2,1)}, u32[]{:S(2)}) copy-start(bf16[256,1024]{1,0:T(8,128)(2,1)} %get-tuple-element.42.result_in) | copy-start | bytes 1572868

commit v5 on v4

--- a/solution.py
+++ b/solution.py
@@ -685,22 +685,15 @@
     placed = [pltpu.make_async_copy(a, b, local.at[i]) for i, (a, b) in enumerate(small + places)]
     for copy in placed:
         copy.start()
-    for copy in placed[: len(small) - 1]:
+    for copy in placed[:3]:
         copy.wait()
-    shard_f2[0, :, features + 128 : wide] = stood_up(b_exp[...])
     by_feature = jnp.concatenate(
         [gains[0:4].astype(float_type), biases[0:5].astype(float_type), jnp.zeros((7, 32), float_type)], axis=0
     )
     ve[me, 0:32] = stood_up(by_feature_wide(by_feature))
     ve[me, 32:48] = jnp.broadcast_to(bias[...].astype(float_type), (16, 128)).astype(narrow_type)
-    for copy in placed[len(small) - 1 :]:
+    for copy in placed[len(small) : len(small) + 14]:
         copy.wait()
-    own_shards = [
-        pltpu.make_async_copy(shard.at[0], full.at[slot], local.at[i])
-        for i, (shard, full, slot) in enumerate(((shard_f2, f2, me), (shard_a, line_a, fsdp), (shard_b, line_b, fsdp)))
-    ]
-    for copy in own_shards:
-        copy.start()
     refs = {
         "ve": (ve, WHOLE, None),
         "fa": (fa, WHOLE, None),
@@ -716,6 +709,15 @@
     early = [i for i, chunk in enumerate(chunks) if chunk[0] is fa or chunk[0] is ve]
     for index in early:
         gather.own(index, chunks[index])
+    for copy in placed[3 : len(small)] + placed[len(small) + 14 :]:
+        copy.wait()
+    shard_f2[0, :, features + 128 : wide] = stood_up(b_exp[...])
+    own_shards = [
+        pltpu.make_async_copy(shard.at[0], full.at[slot], local.at[i])
+        for i, (shard, full, slot) in enumerate(((shard_f2, f2, me), (shard_a, line_a, fsdp), (shard_b, line_b, fsdp)))
+    ]
+    for copy in own_shards:
+        copy.start()
     select[...] = selected(lens_ref, choice_ref, me, *select.shape)
     base = core * (own - halo)
     slot = me - half * (own - halo)
@@ -990,33 +992,75 @@
     for copy in loads:
         copy.start()
     pl.semaphore_wait(barrier, waits)
-    corners = [
-        remote(ya, lines[2][1], send.at[0], receive.at[0], seq ^ SIDE_X, fsdp),
-        remote(xb, lines[5][1], send.at[1], receive.at[1], seq ^ SIDE_Y, fsdp),
-    ]
+    quarter = half_columns // 2
+    x_side = lax.rem(lax.div(seq, 2), 2)
+
+    def columns_of(start, parity):
+        return pl.ds(pl.multiple_of(start + parity * quarter, 128), quarter)
+
+    corners, diagonal = [], []
+    for turn in range(2):
+        for i, (line, via, to, start, parity) in enumerate(
+            ((ya, SIDE_Y, SIDE_X, 0, 1 - x_side), (xb, SIDE_X, SIDE_Y, half_columns, x_side))
+        ):
+            at = 2 * turn + i
+            parity = 1 - parity if turn else parity
+            corners.append(
+                remote(
+                    line.at[:, :, columns_of(0, parity)],
+                    f1.at[pl.ds((seq ^ via) * depth, depth), :, columns_of(start, parity)],
+                    send.at[at],
+                    receive.at[at],
+                    seq ^ to,
+                    fsdp,
+                )
+            )
+            here = f1.at[
+                pl.ds((seq ^ SIDE_X ^ SIDE_Y) * depth, depth),
+                :,
+                columns_of(start, 1 - x_side if turn else x_side),
+            ]
+            diagonal.append(remote(here, here, send.at[4 + at], receive.at[4 + at], seq ^ CORES, fsdp))
+
     tops, tails = pl.ds(0, wide // 2), pl.ds(wide // 2, wide // 2)
     f2_parts = ((SIDE_Y, SIDE_X, tops), (SIDE_X, SIDE_Y, tails))
+    rows_over, rows_along = pl.ds(0, 64), pl.ds(64, 64)
     for i, (via, to, columns) in enumerate(f2_parts):
         line = pl.ds((seq ^ via) * depth, depth)
         corners.append(
             remote(
-                f2_in.at[line, :, columns],
-                f2.at[line, :, columns],
-                send.at[10 + i],
-                receive.at[10 + i],
+                f2_in.at[line, rows_over, columns],
+                f2.at[line, rows_over, columns],
+                send.at[8 + i],
+                receive.at[8 + i],
                 seq ^ to,
                 fsdp,
             )
         )
+    single = [
+        remote(
+            f2_in.at[pl.ds((seq ^ via) * depth + fsdp, 1), rows_along, columns],
+            f2.at[pl.ds((seq ^ via) * depth + fsdp, 1), rows_along, columns],
+            send.at[10 + i],
+            receive.at[10 + i],
+            seq ^ to,
+            fsdp,
+        )
+        for i, (via, to, columns) in enumerate(f2_parts)
+    ]
+    far = f2.at[pl.ds((seq ^ SIDE_X ^ SIDE_Y) * depth + fsdp, 1), rows_along]
+    along = [
+        remote(
+            far, far, send.at[11 + step], receive.at[11 + step], seq, lax.rem(fsdp + step, depth)
+        )
+        for step in range(1, depth)
+    ]
     across = [
-        remote(line, place, send.at[2 + i], receive.at[2 + i], seq ^ CORES, fsdp)
+        remote(line, place, send.at[15 + i], receive.at[15 + i], seq ^ CORES, fsdp)
         for i, (line, place) in enumerate(lines)
     ]
-    for i, columns in enumerate((left, right)):
-        place = f1.at[pl.ds((seq ^ SIDE_X ^ SIDE_Y) * depth, depth), :, columns]
-        across.append(remote(place, place, send.at[8 + i], receive.at[8 + i], seq ^ CORES, fsdp))
     f2_across = remote(
-        f2.at[groups[6]], f2.at[groups[6]], send.at[12], receive.at[12], seq ^ CORES, fsdp
+        f2.at[groups[6]], f2.at[groups[6]], send.at[21], receive.at[21], seq ^ CORES, fsdp
     )
 
     def attended_piece(k):
@@ -1039,7 +1083,7 @@
         def _():
             attended_piece(k).start()
 
-    for copy in corners + across[:6]:
+    for copy in single + corners[:2] + across:
         copy.start()
     select[...] = selected(lens_ref, choice_ref, me, *select.shape)
     rows_of_vectors(ve, vectors)
@@ -1063,9 +1107,16 @@
     def _():
         attended_kept.wait()
 
+    for copy in corners[2:]:
+        copy.start()
+    for copy in single:
+        copy.wait_recv()
+    for copy in along:
+        copy.start()
+
     for i in range(2):
         corners[i].wait_recv()
-        across[6 + i].start()
+        diagonal[i].start()
     for j in range(4):
         att[:, j * 256 : (j + 1) * 256] = turned(as_matrix(att_t[4 * j : 4 * j + 4]))
     out_down = as_matrix(fa[:, :, features : features + 128])
@@ -1092,14 +1143,22 @@
     ranks[4, 128:256] = turned(ranks[1])[:, 128:256]
     for copy in loads[1:]:
         copy.wait()
-    for copy in across:
+    for copy in across + diagonal[:2]:
         copy.wait_recv()
 
     def hidden(k):
-        @pl.when(k == 6)
+        @pl.when(k == 2)
         def _():
-            corners[2].wait_recv()
-            corners[3].wait_recv()
+            for i in (2, 3):
+                corners[i].wait_recv()
+                diagonal[i].start()
+            for i in (2, 3):
+                diagonal[i].wait_recv()
+
+        @pl.when(k == 5)
+        def _():
+            for copy in corners[4:] + along:
+                copy.wait_recv()
             f2_across.start()
 
         @pl.when(k == 7)
@@ -1198,7 +1257,7 @@
         def _():
             gradient_piece(k).wait_send()
 
-    for copy in corners + across + [f2_across]:
+    for copy in single + along + corners + diagonal + across + [f2_across]:
         copy.wait_send()
 
 
@@ -1208,7 +1267,7 @@
     wide = features + 256
     devices, hidden_share = f2.shape[0], f2.shape[1]
     share, hidden_total = features // devices, 2 * lines[0].shape[2]
-    copies = 13
+    copies = 22
 
     def wide_rows():
         return pltpu.VMEM((rows, features), float_type)
@@ -1395,7 +1454,9 @@
     late_ref,
     fa,
     vectors,
-    normed,
+    normed_t,
+    normal,
+    grad_rank,
     total,
     arrived,
     arrived_rows,
@@ -1493,8 +1554,10 @@
     rows_of_vectors(ve, vectors)
     select[...] = selected(lens_ref, choice_ref, me, *select.shape)
     early.sides()
-    shifted, normal, scaling = layer_norm(tok_ref[...].astype(float_type), vectors[0:1], vectors[4:5])
-    normed[...] = shifted.astype(narrow_type)
+    shifted, normal_rows, scaling = layer_norm(tok_ref[...].astype(float_type), vectors[0:1], vectors[4:5])
+    normal[...] = normal_rows
+    for j in range(4):
+        normed_t[j * 256 : (j + 1) * 256] = turned(shifted[:, j * 256 : (j + 1) * 256])
     early.corner()
     load.wait()
 
@@ -1509,52 +1572,56 @@
         def _():
             pltpu.make_async_copy(dq_ref.at[0], arrived.at[p, head], piece_local.at[p]).wait()
 
-    def project_back(p):
+    def ranks_back(p):
         for j in range(4):
             arrived_rows[:, j * 256 : (j + 1) * 256] = turned(as_matrix(arrived[p, 4 * j : 4 * j + 4]))
         up = as_matrix(fa[:, :, p * wide + features + 128 : (p + 1) * wide])
-        grad_rank = (matmul(arrived_rows[...], up) * select[...]).astype(narrow_type)
-
-        @pl.loop(0, 4)
+        grad_rank[...] = (matmul(arrived_rows[...], up) * select[...]).astype(narrow_type)
+        shaped = (devices, share, 128)
+        late_terms[p, :, 0:32] = matmul(normed_t[...], grad_rank[...]).astype(narrow_type).reshape(shaped)
+        late_terms[p, :, 32:64] = (
+            matmul(as_matrix(arrived[p]), rank_ref[p]).astype(narrow_type).reshape(shaped)
+        )
+
+    def project_back(p, tiles):
+        @pl.loop(*tiles)
         def _(j):
             at = pl.ds(pl.multiple_of(j * 256, 128), 256)
             slots = pl.ds(j * 8, 8)
             weight = as_matrix(fa[slots, :, p * wide : p * wide + features])
             down = as_matrix(fa[slots, :, p * wide + features : p * wide + features + 128])
-            term = transposed_right(arrived_rows[...], weight) + transposed_right(grad_rank, down)
+            term = transposed_right(arrived_rows[...], weight) + transposed_right(grad_rank[...], down)
             if p == 0:
                 total[:, at] = term
             else:
                 total[:, at] += term
 
-        shaped = (devices, share, 128)
-        late_terms[p, :, 0:32] = transposed_left(normed[...], grad_rank).astype(narrow_type).reshape(shaped)
-        late_terms[p, :, 32:64] = (
-            matmul(as_matrix(arrived[p]), rank_ref[p]).astype(narrow_type).reshape(shaped)
-        )
-
     gather_part(0)
-    project_back(0)
+    ranks_back(0)
     late[0].begin()
+    project_back(0, (0, 4))
     early.line()
     late[0].sides()
     gather_part(1)
-    project_back(1)
+    ranks_back(1)
     late[1].begin()
+    project_back(1, (0, 4))
     late[0].corner()
     late[1].sides()
     gather_part(2)
-    project_back(2)
+    ranks_back(2)
     late[2].begin()
     late[0].line()
     late[1].corner()
+    project_back(2, (0, 2))
     late[2].sides()
-    gradient_ref[...] = gm_ref[...] + norm_backward(total[...], vectors[0:1], normal, scaling)
+    project_back(2, (2, 4))
     late[1].line()
     late[2].corner()
+    gradient_ref[...] = gm_ref[...] + norm_backward(total[...], vectors[0:1], normal[...], scaling)
+    late[2].line()
     early.end(early_ref)
     late[0].end(late_ref.at[0])
-    late[2].line()
     late[1].end(late_ref.at[1])
     late[2].end(late_ref.at[2])
     for reduce in [early] + late:
@@ -1597,7 +1664,9 @@
         scratch_shapes=[
             pltpu.VMEM((devices, share, 3 * wide), narrow_type),
             pltpu.VMEM((16, features), float_type),
-            pltpu.VMEM((rows, features), narrow_type),
+            pltpu.VMEM((features, rows), narrow_type),
+            pltpu.VMEM((rows, features), float_type),
+            pltpu.VMEM((rows, 128), narrow_type),
             pltpu.VMEM((rows, features), float_type),
             pltpu.VMEM((3, heads, features // heads, rows), narrow_type),
             pltpu.VMEM((rows, features), narrow_type),

time: 293 us -> 290 us (0.990)
    pallas_call x1, Pallas kernels: 54.9 us -> 51.3 us  [middle_part(): pl.pallas_call(functools.partial(middle_kernel, depth, heads), out_shape=...]
  transfers between devices with their start and end apart: 4 -> 4, of which waited for: 2 -> 2; matrix products, arithmetic and copies ran while one was open for 0% -> 0% of each run, Pallas kernels for 5% -> 6%
where the time goes in v5:
time: 290 us; the launch traced here: 291 us
  Pallas kernels  276 us (95%)
  local copies, waits for them, and re-layouts  6.28 us (2%)
  starting transfers between devices  4.12 us (1%)
  waiting for transfers between devices  3.57 us (1%)
    pallas_call x1, Pallas kernels, attention_in(): pl.pallas_call(functools.partial(attention_in_kernel, depth, halo, heads,...  118 us
    pallas_call x1, Pallas kernels, last_part(): pl.pallas_call(functools.partial(last_kernel, depth, heads, halo), out_sh...  63.1 us
    pallas_call x1, Pallas kernels, middle_part(): pl.pallas_call(functools.partial(middle_kernel, depth, heads), out_shape=...  51.3 us
    pallas_call x1, Pallas kernels, attention_backward(): pl.pallas_call(functools.partial(backward_kernel, own, halo, step), out_s...  25.6 us
    pallas_call x1, Pallas kernels, attention_forward(): pl.pallas_call(functools.partial(forward_kernel, own, halo, step), out_sh...  16.3 us
    unnamed x34, local copies, waits for them, and re-layouts  6.28 us
  transfers between devices with their start and end apart: 4, of which 2 were waited for; matrix products, arithmetic and copies ran while one was open for 0% of the time, Pallas kernels for 6%

profile of v5, /device:TPU:0, one launch (start us, length us, event | category | flops | bytes accessed | tf_op | source)
XLA Modules:
  0.0 290.6 jit_solution(13357290856127815741)
XLA Ops:
  0.6 118.3 %shard_map.224 = (bf16[32,32,5376]{2,1,0:T(8,128)(2,1)}, bf16[32,48,128]{2,1,0:T(8,128)(2,1)}, bf16[32,128,1280]{2,1,0:T(8,128)(2,1)}, bf16[4,32,2048]{2,1,0:T(8...) custom-call(s32[8]{0:T(128)} %lens_ref.9, s32[8]{0:T(128)} %choice_ref.5, ...), custom_call_target="tpu_custom_call" | custom-call | tf_op jit(solution)/shard_map/pallas_call | solution.py:870
  119.0 1.4 collective-permute-start.2
  120.4 0.0 collective-permute-start
  120.4 0.7 collective-permute-start.3
  121.1 2.0 collective-permute-start.1
  123.1 0.0 copy-start
  123.1 1.6 copy-done
  124.7 0.0 copy-start.10
  124.7 0.7 copy-done.10
  125.3 16.3 %shard_map.225 = (bf16[16,64,256]{2,1,0:T(8,128)(2,1)S(1)}, f32[16,8,256]{2,1,0:T(8,128)S(1)}, f32[16,64,256]{2,1,0:T(8,128)S(1)}) custom-call(s32[8]{0:T(128)S(1)} %copy-done.10, bf16[22,3,64,256]{3,2,1,0:T(8,128)(2,1)S(1)} %copy-done), custom_call_target="tpu_custom_call" | custom-call | tf_op jit(solution)/shard_map/pallas_call | solution.py:1848
  141.7 0.0 copy-start.7
  141.7 0.8 copy-done.7
  142.5 0.0 collective-permute-done.2.xa
  142.5 0.0 copy-start.13
  142.5 0.0 collective-permute-done.ya
  142.5 0.0 copy-start.14
  142.5 2.5 collective-permute-done.3.xb
  145.0 0.0 copy-start.15
  145.0 1.1 collective-permute-done.1.yb
  146.1 0.0 copy-start.16
  146.1 0.0 copy-done.13
  146.1 0.0 copy-done.14
  146.1 0.0 copy-done.15
  146.1 0.8 copy-done.16
  146.9 0.0 copy-start.1
  146.9 0.0 copy-start.11
  146.9 0.0 copy-start.4
  146.9 0.0 copy-start.9
  146.9 0.0 copy-start.12
  146.9 51.3 %shard_map.226 = (bf16[256,1024]{1,0:T(8,128)(2,1)}, f32[256,1024]{1,0:T(8,128)}, bf16[32,384,128]{2,1,0:T(8,128)(2,1)}, bf16[16,64,256]{2,1,0:T(8,128)(2,1)}) custom-call(s32[8]{0:T(128)} %lens_ref.9, s32[8]{0:T(128)} %choice_ref.5, bf16[16,64,256]{2,1,0:T(8,128)(2,1)} %copy-done.7, bf16[256,1024]{1,0:T(8,128)(2,1)} %tok_ref.3, bf16[256,1024]{1,0:T(8,128)(2,1)} %cot_ref.1, ...), custom_call_target="tpu_custom_call" | custom-call | tf_op jit(solution)/shard_map/pallas_call | solution.py:1278
  198.2 0.0 copy-start.2
  198.2 0.0 copy-start.3
  198.2 0.0 copy-done.1
  198.2 0.0 copy-done.11
  198.2 0.0 copy-start.8
  198.2 1.2 copy-done.8
  199.4 25.6 %shard_map.227 = (bf16[16,64,256]{2,1,0:T(8,128)(2,1)S(1)}, bf16[22,2,64,256]{3,2,1,0:T(8,128)(2,1)S(1)}) custom-call(s32[8]{0:T(128)S(1)} %copy-done.11, bf16[22,3,64,256]{3,2,1,0:T(8,128)(2,1)S(1)} %copy-done.1, bf16[16,64,256]{2,1,0:T(8,128)(2,1)S(1)} %copy-done.8, f32[16,8,256]{2,1,0:T(8,128)S(1)} %get-tuple-element.44.lse_ref, ...), custom_call_target="tpu_custom_call" | custom-call | tf_op jit(solution)/shard_map/pallas_call | solution.py:1969
  225.0 0.0 copy-done.4
  225.0 0.0 copy-done.9
  225.0 0.0 copy-done.12
  225.0 0.0 copy-done.2
  225.0 0.0 copy-done.3
  225.0 0.0 copy-start.5
  225.0 1.2 copy-done.5
  226.3 0.0 copy-start.6
  226.3 63.1 %shard_map.228 = (f32[256,1024]{1,0:T(8,128)S(1)}, f32[384,128]{1,0:T(8,128)S(1)}, f32[3,64,128]{2,1,0:T(8,128)S(1)}) custom-call(s32[8]{0:T(128)S(1)} %copy-done.11, s32[8]{0:T(128)S(1)} %copy-done.12, bf16[16,64,256]{2,1,0:T(8,128)(2,1)S(1)} %get-tuple-element.46.dq_ref, bf16[22,2,64,256]{3,2,1,0:T(8,128)(2,1)S(1)} %get-tuple-element.47.dkv_ref, ...), custom_call_target="tpu_custom_call" | custom-call | tf_op jit(solution)/shard_map/pallas_call | solution.py:1655
  289.3 0.0 copy-done.6
  289.4 1.3 shard_map.229
Async XLA Ops:
  119.0 23.5 %collective-permute-start.2 = (bf16[4,32,2048]{2,1,0:T(8,128)(2,1)}, bf16[4,32,2048]{2,1,0:T(8,128)(2,1)S(1)}, u32[]{:S(2)}, u32[]{:S(2)}) collective-permute-start(bf16[4,32,2048]{2,1,0:T(8,128)(2,1)} %get-tuple-element.40.line_a), channel_id=1, source_target_pairs={{0,8},{1,9},{2,10},{3,11},{4,12},{5,13},{6,14},{7,15},{8,0},{9,1},... | collective-permute-start | bytes 1572872 | tf_op jit(solution)/shard_map/ppermute | solution.py:2044
  120.4 22.1 %collective-permute-start = (bf16[4,32,2048]{2,1,0:T(8,128)(2,1)}, bf16[4,32,2048]{2,1,0:T(8,128)(2,1)S(1)}, u32[]{:S(2)}, u32[]{:S(2)}) collective-permute-start(bf16[4,32,2048]{2,1,0:T(8,128)(2,1)} %get-tuple-element.40.line_a), channel_id=1, source_target_pairs={{0,16},{1,17},{2,18},{3,19},{4,20},{5,21},{6,22},{7,23},{8,24},{9,... | collective-permute-start | bytes 1572872 | tf_op jit(solution)/shard_map/ppermute | solution.py:2044
  120.4 24.6 %collective-permute-start.3 = (bf16[4,32,2048]{2,1,0:T(8,128)(2,1)}, bf16[4,32,2048]{2,1,0:T(8,128)(2,1)S(1)}, u32[]{:S(2)}, u32[]{:S(2)}) collective-permute-start(bf16[4,32,2048]{2,1,0:T(8,128)(2,1)} %get-tuple-element.41.line_b), channel_id=1, source_target_pairs={{0,8},{1,9},{2,10},{3,11},{4,12},{5,13},{6,14},{7,15},{8,0},{9,1},... | collective-permute-start | bytes 1572872 | tf_op jit(solution)/shard_map/ppermute | solution.py:2044
  121.1 25.0 %collective-permute-start.1 = (bf16[4,32,2048]{2,1,0:T(8,128)(2,1)}, bf16[4,32,2048]{2,1,0:T(8,128)(2,1)S(1)}, u32[]{:S(2)}, u32[]{:S(2)}) collective-permute-start(bf16[4,32,2048]{2,1,0:T(8,128)(2,1)} %get-tuple-element.41.line_b), channel_id=1, source_target_pairs={{0,16},{1,17},{2,18},{3,19},{4,20},{5,21},{6,22},{7,23},{8,24},{9,... | collective-permute-start | bytes 1572872 | tf_op jit(solution)/shard_map/ppermute | solution.py:2044
  123.1 1.6 copy-start
  124.7 0.7 copy-start.10
  141.7 0.8 copy-start.7
  142.5 3.6 %copy-start.13 = (bf16[4,32,2048]{2,1,0:T(8,128)(2,1)}, bf16[4,32,2048]{2,1,0:T(8,128)(2,1)S(1)}, u32[]{:S(2)}) copy-start(bf16[4,32,2048]{2,1,0:T(8,128)(2,1)S(1)} %collective-permute-done.2.xa) | copy-start | bytes 1572868
  142.5 3.6 %copy-start.14 = (bf16[4,32,2048]{2,1,0:T(8,128)(2,1)}, bf16[4,32,2048]{2,1,0:T(8,128)(2,1)S(1)}, u32[]{:S(2)}) copy-start(bf16[4,32,2048]{2,1,0:T(8,128)(2,1)S(1)} %collective-permute-done.ya) | copy-start | bytes 1572868
  145.0 1.1 copy-start.15
  146.1 0.8 copy-start.16
  146.9 51.3 %copy-start.1 = (bf16[22,3,64,256]{3,2,1,0:T(8,128)(2,1)S(1)}, bf16[22,3,64,256]{3,2,1,0:T(8,128)(2,1)}, u32[]{:S(2)}) copy-start(bf16[22,3,64,256]{3,2,1,0:T(8,128)(2,1)} %get-tuple-element.35.x_ref) | copy-start | bytes 6488068
  146.9 51.3 %copy-start.11 = (s32[8]{0:T(128)S(1)}, s32[8]{0:T(128)}, u32[]{:S(2)}) copy-start(s32[8]{0:T(128)} %lens_ref.9) | copy-start | bytes 100
  146.9 78.1 %copy-start.4 = (bf16[32,48,128]{2,1,0:T(8,128)(2,1)S(1)}, bf16[32,48,128]{2,1,0:T(8,128)(2,1)}, u32[]{:S(2)}) copy-start(bf16[32,48,128]{2,1,0:T(8,128)(2,1)} %get-tuple-element.38.ve) | copy-start | bytes 1179652
  146.9 78.1 %copy-start.9 = (bf16[3,256,128]{2,1,0:T(8,128)(2,1)S(1)}, bf16[3,256,128]{2,1,0:T(8,128)(2,1)}, u32[]{:S(2)}) copy-start(bf16[3,256,128]{2,1,0:T(8,128)(2,1)} %get-tuple-element.49.rank_ref) | copy-start | bytes 589828
  146.9 78.1 %copy-start.12 = (s32[8]{0:T(128)S(1)}, s32[8]{0:T(128)}, u32[]{:S(2)}) copy-start(s32[8]{0:T(128)} %choice_ref.5) | copy-start | bytes 100
  198.2 26.8 %copy-start.2 = (bf16[256,1024]{1,0:T(8,128)(2,1)S(1)}, bf16[256,1024]{1,0:T(8,128)(2,1)}, u32[]{:S(2)}) copy-start(bf16[256,1024]{1,0:T(8,128)(2,1)} %tok_ref.3) | copy-start | bytes 1572868
  198.2 26.8 %copy-start.3 = (bf16[32,384,128]{2,1,0:T(8,128)(2,1)S(1)}, bf16[32,384,128]{2,1,0:T(8,128)(2,1)}, u32[]{:S(2)}) copy-start(bf16[32,384,128]{2,1,0:T(8,128)(2,1)} %get-tuple-element.50.early_terms) | copy-start | bytes 9437188
  198.2 1.2 copy-start.8
  225.0 1.2 copy-start.5
  226.3 63.1 %copy-start.6 = (bf16[256,1024]{1,0:T(8,128)(2,1)S(1)}, bf16[256,1024]{1,0:T(8,128)(2,1)}, u32[]{:S(2)}) copy-start(bf16[256,1024]{1,0:T(8,128)(2,1)} %get-tuple-element.42.result_in) | copy-start | bytes 1572868

commit v6 on v5

--- a/solution.py
+++ b/solution.py
@@ -813,7 +813,7 @@
 
     steps = (gather.own, gather.inner, gather.outer, gather.first, gather.second, gather.third, gather.finish)
     for turn in range(DELAYS[0], len(chunks) + DELAYS[-1]):
-        if turn == len(chunks) - 2:
+        if turn == len(chunks) - 4:
             over = exchanged()
         for delay, step in zip(DELAYS, steps):
             index = turn - delay
@@ -1600,13 +1600,13 @@
     ranks_back(0)
     late[0].begin()
     project_back(0, (0, 4))
-    early.line()
     late[0].sides()
     gather_part(1)
     ranks_back(1)
     late[1].begin()
     project_back(1, (0, 4))
     late[0].corner()
+    early.line()
     late[1].sides()
     gather_part(2)
     ranks_back(2)

time: 290 us -> 286 us (0.986)
  Pallas kernels: 276 us -> 271 us
  transfers between devices with their start and end apart: 4 -> 4, of which waited for: 2 -> 2; matrix products, arithmetic and copies ran while one was open for 0% -> 0% of each run, Pallas kernels for 6% -> 5%
where the time goes in v6:
time: 286 us; the launch traced here: 287 us
  Pallas kernels  271 us (95%)
  local copies, waits for them, and re-layouts  6.28 us (2%)
  waiting for transfers between devices  4.83 us (2%)
  starting transfers between devices  4.12 us (1%)
    pallas_call x1, Pallas kernels, attention_in(): pl.pallas_call(functools.partial(attention_in_kernel, depth, halo, heads,...  118 us
    pallas_call x1, Pallas kernels, last_part(): pl.pallas_call(functools.partial(last_kernel, depth, heads, halo), out_sh...  61 us
    pallas_call x1, Pallas kernels, middle_part(): pl.pallas_call(functools.partial(middle_kernel, depth, heads), out_shape=...  51.3 us
    pallas_call x1, Pallas kernels, attention_backward(): pl.pallas_call(functools.partial(backward_kernel, own, halo, step), out_s...  23.8 us
    pallas_call x1, Pallas kernels, attention_forward(): pl.pallas_call(functools.partial(forward_kernel, own, halo, step), out_sh...  15.1 us
    unnamed x34, local copies, waits for them, and re-layouts  6.28 us
  transfers between devices with their start and end apart: 4, of which 2 were waited for; matrix products, arithmetic and copies ran while one was open for 0% of the time, Pallas kernels for 5%

profile of v6, /device:TPU:0, one launch (start us, length us, event | category | flops | bytes accessed | tf_op | source)
XLA Modules:
  0.0 286.8 jit_solution(15885883124972283184)
XLA Ops:
  0.6 118.3 %shard_map.224 = (bf16[32,32,5376]{2,1,0:T(8,128)(2,1)}, bf16[32,48,128]{2,1,0:T(8,128)(2,1)}, bf16[32,128,1280]{2,1,0:T(8,128)(2,1)}, bf16[4,32,2048]{2,1,0:T(8...) custom-call(s32[8]{0:T(128)} %lens_ref.9, s32[8]{0:T(128)} %choice_ref.5, ...), custom_call_target="tpu_custom_call" | custom-call | tf_op jit(solution)/shard_map/pallas_call | solution.py:870
  119.0 1.4 collective-permute-start.2
  120.4 0.0 collective-permute-start
  120.4 0.7 collective-permute-start.3
  121.1 2.0 collective-permute-start.1
  123.1 0.0 copy-start
  123.1 1.6 copy-done
  124.7 0.0 copy-start.10
  124.7 0.7 copy-done.10
  125.3 15.1 %shard_map.225 = (bf16[16,64,256]{2,1,0:T(8,128)(2,1)S(1)}, f32[16,8,256]{2,1,0:T(8,128)S(1)}, f32[16,64,256]{2,1,0:T(8,128)S(1)}) custom-call(s32[8]{0:T(128)S(1)} %copy-done.10, bf16[22,3,64,256]{3,2,1,0:T(8,128)(2,1)S(1)} %copy-done), custom_call_target="tpu_custom_call" | custom-call | tf_op jit(solution)/shard_map/pallas_call | solution.py:1848
  140.4 0.0 copy-start.7
  140.4 0.8 copy-done.7
  141.2 0.0 collective-permute-done.2.xa
  141.2 0.0 copy-start.13
  141.2 0.0 collective-permute-done.ya
  141.2 0.0 copy-start.14
  141.2 3.8 %collective-permute-done.3.xb = bf16[4,32,2048]{2,1,0:T(8,128)(2,1)S(1)} collective-permute-done((bf16[4,32,2048]{2,1,0:T(8,128)(2,1)}, bf16[4,32,2048]{2,1,0:T(8,128)(2,1)S(1)}, u32[]{:S(2)}, u32[]{:S(2)}) %collective-permute-start.3) | collective-permute-done | bytes 524320 | tf_op jit(solution)/shard_map/ppermute | solution.py:2044
  145.0 0.0 copy-start.15
  145.0 1.1 collective-permute-done.1.yb
  146.1 0.0 copy-start.16
  146.1 0.0 copy-done.13
  146.1 0.0 copy-done.14
  146.1 0.0 copy-done.15
  146.1 0.8 copy-done.16
  146.9 0.0 copy-start.1
  146.9 0.0 copy-start.11
  146.9 0.0 copy-start.4
  146.9 0.0 copy-start.9
  146.9 0.0 copy-start.12
  146.9 51.3 %shard_map.226 = (bf16[256,1024]{1,0:T(8,128)(2,1)}, f32[256,1024]{1,0:T(8,128)}, bf16[32,384,128]{2,1,0:T(8,128)(2,1)}, bf16[16,64,256]{2,1,0:T(8,128)(2,1)}) custom-call(s32[8]{0:T(128)} %lens_ref.9, s32[8]{0:T(128)} %choice_ref.5, bf16[16,64,256]{2,1,0:T(8,128)(2,1)} %copy-done.7, bf16[256,1024]{1,0:T(8,128)(2,1)} %tok_ref.3, bf16[256,1024]{1,0:T(8,128)(2,1)} %cot_ref.1, ...), custom_call_target="tpu_custom_call" | custom-call | tf_op jit(solution)/shard_map/pallas_call | solution.py:1278
  198.2 0.0 copy-start.2
  198.2 0.0 copy-start.3
  198.2 0.0 copy-done.1
  198.2 0.0 copy-done.11
  198.2 0.0 copy-start.8
  198.2 1.2 copy-done.8
  199.4 23.8 %shard_map.227 = (bf16[16,64,256]{2,1,0:T(8,128)(2,1)S(1)}, bf16[22,2,64,256]{3,2,1,0:T(8,128)(2,1)S(1)}) custom-call(s32[8]{0:T(128)S(1)} %copy-done.11, bf16[22,3,64,256]{3,2,1,0:T(8,128)(2,1)S(1)} %copy-done.1, bf16[16,64,256]{2,1,0:T(8,128)(2,1)S(1)} %copy-done.8, f32[16,8,256]{2,1,0:T(8,128)S(1)} %get-tuple-element.44.lse_ref, ...), custom_call_target="tpu_custom_call" | custom-call | tf_op jit(solution)/shard_map/pallas_call | solution.py:1969
  223.2 0.0 copy-done.4
  223.2 0.0 copy-done.9
  223.2 0.0 copy-done.12
  223.2 0.0 copy-done.2
  223.2 0.0 copy-done.3
  223.2 0.0 copy-start.5
  223.2 1.2 copy-done.5
  224.5 0.0 copy-start.6
  224.5 61.0 %shard_map.228 = (f32[256,1024]{1,0:T(8,128)S(1)}, f32[384,128]{1,0:T(8,128)S(1)}, f32[3,64,128]{2,1,0:T(8,128)S(1)}) custom-call(s32[8]{0:T(128)S(1)} %copy-done.11, s32[8]{0:T(128)S(1)} %copy-done.12, bf16[16,64,256]{2,1,0:T(8,128)(2,1)S(1)} %get-tuple-element.46.dq_ref, bf16[22,2,64,256]{3,2,1,0:T(8,128)(2,1)S(1)} %get-tuple-element.47.dkv_ref, ...), custom_call_target="tpu_custom_call" | custom-call | tf_op jit(solution)/shard_map/pallas_call | solution.py:1655
  285.5 0.0 copy-done.6
  285.5 1.3 shard_map.229
Async XLA Ops:
  119.0 22.3 %collective-permute-start.2 = (bf16[4,32,2048]{2,1,0:T(8,128)(2,1)}, bf16[4,32,2048]{2,1,0:T(8,128)(2,1)S(1)}, u32[]{:S(2)}, u32[]{:S(2)}) collective-permute-start(bf16[4,32,2048]{2,1,0:T(8,128)(2,1)} %get-tuple-element.40.line_a), channel_id=1, source_target_pairs={{0,8},{1,9},{2,10},{3,11},{4,12},{5,13},{6,14},{7,15},{8,0},{9,1},... | collective-permute-start | bytes 1572872 | tf_op jit(solution)/shard_map/ppermute | solution.py:2044
  120.4 20.9 %collective-permute-start = (bf16[4,32,2048]{2,1,0:T(8,128)(2,1)}, bf16[4,32,2048]{2,1,0:T(8,128)(2,1)S(1)}, u32[]{:S(2)}, u32[]{:S(2)}) collective-permute-start(bf16[4,32,2048]{2,1,0:T(8,128)(2,1)} %get-tuple-element.40.line_a), channel_id=1, source_target_pairs={{0,16},{1,17},{2,18},{3,19},{4,20},{5,21},{6,22},{7,23},{8,24},{9,... | collective-permute-start | bytes 1572872 | tf_op jit(solution)/shard_map/ppermute | solution.py:2044
  120.4 24.6 %collective-permute-start.3 = (bf16[4,32,2048]{2,1,0:T(8,128)(2,1)}, bf16[4,32,2048]{2,1,0:T(8,128)(2,1)S(1)}, u32[]{:S(2)}, u32[]{:S(2)}) collective-permute-start(bf16[4,32,2048]{2,1,0:T(8,128)(2,1)} %get-tuple-element.41.line_b), channel_id=1, source_target_pairs={{0,8},{1,9},{2,10},{3,11},{4,12},{5,13},{6,14},{7,15},{8,0},{9,1},... | collective-permute-start | bytes 1572872 | tf_op jit(solution)/shard_map/ppermute | solution.py:2044
  121.1 25.0 %collective-permute-start.1 = (bf16[4,32,2048]{2,1,0:T(8,128)(2,1)}, bf16[4,32,2048]{2,1,0:T(8,128)(2,1)S(1)}, u32[]{:S(2)}, u32[]{:S(2)}) collective-permute-start(bf16[4,32,2048]{2,1,0:T(8,128)(2,1)} %get-tuple-element.41.line_b), channel_id=1, source_target_pairs={{0,16},{1,17},{2,18},{3,19},{4,20},{5,21},{6,22},{7,23},{8,24},{9,... | collective-permute-start | bytes 1572872 | tf_op jit(solution)/shard_map/ppermute | solution.py:2044
  123.1 1.6 copy-start
  124.7 0.7 copy-start.10
  140.4 0.8 copy-start.7
  141.2 4.9 %copy-start.13 = (bf16[4,32,2048]{2,1,0:T(8,128)(2,1)}, bf16[4,32,2048]{2,1,0:T(8,128)(2,1)S(1)}, u32[]{:S(2)}) copy-start(bf16[4,32,2048]{2,1,0:T(8,128)(2,1)S(1)} %collective-permute-done.2.xa) | copy-start | bytes 1572868
  141.2 4.9 %copy-start.14 = (bf16[4,32,2048]{2,1,0:T(8,128)(2,1)}, bf16[4,32,2048]{2,1,0:T(8,128)(2,1)S(1)}, u32[]{:S(2)}) copy-start(bf16[4,32,2048]{2,1,0:T(8,128)(2,1)S(1)} %collective-permute-done.ya) | copy-start | bytes 1572868
  145.0 1.1 copy-start.15
  146.1 0.8 copy-start.16
  146.9 51.3 %copy-start.1 = (bf16[22,3,64,256]{3,2,1,0:T(8,128)(2,1)S(1)}, bf16[22,3,64,256]{3,2,1,0:T(8,128)(2,1)}, u32[]{:S(2)}) copy-start(bf16[22,3,64,256]{3,2,1,0:T(8,128)(2,1)} %get-tuple-element.35.x_ref) | copy-start | bytes 6488068
  146.9 51.3 %copy-start.11 = (s32[8]{0:T(128)S(1)}, s32[8]{0:T(128)}, u32[]{:S(2)}) copy-start(s32[8]{0:T(128)} %lens_ref.9) | copy-start | bytes 100
  146.9 76.3 %copy-start.4 = (bf16[32,48,128]{2,1,0:T(8,128)(2,1)S(1)}, bf16[32,48,128]{2,1,0:T(8,128)(2,1)}, u32[]{:S(2)}) copy-start(bf16[32,48,128]{2,1,0:T(8,128)(2,1)} %get-tuple-element.38.ve) | copy-start | bytes 1179652
  146.9 76.3 %copy-start.9 = (bf16[3,256,128]{2,1,0:T(8,128)(2,1)S(1)}, bf16[3,256,128]{2,1,0:T(8,128)(2,1)}, u32[]{:S(2)}) copy-start(bf16[3,256,128]{2,1,0:T(8,128)(2,1)} %get-tuple-element.49.rank_ref) | copy-start | bytes 589828
  146.9 76.3 %copy-start.12 = (s32[8]{0:T(128)S(1)}, s32[8]{0:T(128)}, u32[]{:S(2)}) copy-start(s32[8]{0:T(128)} %choice_ref.5) | copy-start | bytes 100
  198.2 25.0 %copy-start.2 = (bf16[256,1024]{1,0:T(8,128)(2,1)S(1)}, bf16[256,1024]{1,0:T(8,128)(2,1)}, u32[]{:S(2)}) copy-start(bf16[256,1024]{1,0:T(8,128)(2,1)} %tok_ref.3) | copy-start | bytes 1572868
  198.2 25.0 %copy-start.3 = (bf16[32,384,128]{2,1,0:T(8,128)(2,1)S(1)}, bf16[32,384,128]{2,1,0:T(8,128)(2,1)}, u32[]{:S(2)}) copy-start(bf16[32,384,128]{2,1,0:T(8,128)(2,1)} %get-tuple-element.50.early_terms) | copy-start | bytes 9437188
  198.2 1.2 copy-start.8
  223.2 1.2 copy-start.5
  224.5 61.1 %copy-start.6 = (bf16[256,1024]{1,0:T(8,128)(2,1)S(1)}, bf16[256,1024]{1,0:T(8,128)(2,1)}, u32[]{:S(2)}) copy-start(bf16[256,1024]{1,0:T(8,128)(2,1)} %get-tuple-element.42.result_in) | copy-start | bytes 1572868

commit v7 on v5

--- a/solution.py
+++ b/solution.py
@@ -908,7 +908,7 @@
     )(lengths, choice, tokens, *arrays)
 
 
-DELAYS = (-9, -6, -3, 0, 1, 2, 3)
+DELAYS = (-8, -4, -2, 0, 1, 2, 3)
 HIDDEN_TILE = 512
 
 

time: 290 us -> 289 us (level)
  Pallas kernels: 276 us -> 272 us
  transfers between devices with their start and end apart: 4 -> 4, of which waited for: 2 -> 2; matrix products, arithmetic and copies ran while one was open for 0% -> 0% of each run, Pallas kernels for 6% -> 5%
where the time goes in v7:
time: 289 us; the launch traced here: 288 us
  Pallas kernels  272 us (94%)
  local copies, waits for them, and re-layouts  6.28 us (2%)
  waiting for transfers between devices  4.85 us (2%)
  starting transfers between devices  4.12 us (1%)
    pallas_call x1, Pallas kernels, attention_in(): pl.pallas_call(functools.partial(attention_in_kernel, depth, halo, heads,...  118 us
    pallas_call x1, Pallas kernels, last_part(): pl.pallas_call(functools.partial(last_kernel, depth, heads, halo), out_sh...  63 us
    pallas_call x1, Pallas kernels, middle_part(): pl.pallas_call(functools.partial(middle_kernel, depth, heads), out_shape=...  51.4 us
    pallas_call x1, Pallas kernels, attention_backward(): pl.pallas_call(functools.partial(backward_kernel, own, halo, step), out_s...  23.3 us
    pallas_call x1, Pallas kernels, attention_forward(): pl.pallas_call(functools.partial(forward_kernel, own, halo, step), out_sh...  15.1 us
    unnamed x34, local copies, waits for them, and re-layouts  6.28 us
  transfers between devices with their start and end apart: 4, of which 2 were waited for; matrix products, arithmetic and copies ran while one was open for 0% of the time, Pallas kernels for 5%

profile of v7, /device:TPU:0, one launch (start us, length us, event | category | flops | bytes accessed | tf_op | source)
XLA Modules:
  0.0 288.4 jit_solution(4158610626292946248)
XLA Ops:
  0.6 118.3 %shard_map.224 = (bf16[32,32,5376]{2,1,0:T(8,128)(2,1)}, bf16[32,48,128]{2,1,0:T(8,128)(2,1)}, bf16[32,128,1280]{2,1,0:T(8,128)(2,1)}, bf16[4,32,2048]{2,1,0:T(8...) custom-call(s32[8]{0:T(128)} %lens_ref.9, s32[8]{0:T(128)} %choice_ref.5, ...), custom_call_target="tpu_custom_call" | custom-call | tf_op jit(solution)/shard_map/pallas_call | solution.py:870
  119.0 1.4 collective-permute-start.2
  120.4 0.0 collective-permute-start
  120.4 0.7 collective-permute-start.3
  121.1 2.0 collective-permute-start.1
  123.1 0.0 copy-start
  123.1 1.6 copy-done
  124.7 0.0 copy-start.10
  124.7 0.7 copy-done.10
  125.3 15.1 %shard_map.225 = (bf16[16,64,256]{2,1,0:T(8,128)(2,1)S(1)}, f32[16,8,256]{2,1,0:T(8,128)S(1)}, f32[16,64,256]{2,1,0:T(8,128)S(1)}) custom-call(s32[8]{0:T(128)S(1)} %copy-done.10, bf16[22,3,64,256]{3,2,1,0:T(8,128)(2,1)S(1)} %copy-done), custom_call_target="tpu_custom_call" | custom-call | tf_op jit(solution)/shard_map/pallas_call | solution.py:1848
  140.4 0.0 copy-start.7
  140.4 0.8 copy-done.7
  141.2 0.0 collective-permute-done.2.xa
  141.2 0.0 copy-start.13
  141.2 0.0 collective-permute-done.ya
  141.2 0.0 copy-start.14
  141.2 3.8 %collective-permute-done.3.xb = bf16[4,32,2048]{2,1,0:T(8,128)(2,1)S(1)} collective-permute-done((bf16[4,32,2048]{2,1,0:T(8,128)(2,1)}, bf16[4,32,2048]{2,1,0:T(8,128)(2,1)S(1)}, u32[]{:S(2)}, u32[]{:S(2)}) %collective-permute-start.3) | collective-permute-done | bytes 524320 | tf_op jit(solution)/shard_map/ppermute | solution.py:2044
  145.0 0.0 copy-start.15
  145.0 1.1 collective-permute-done.1.yb
  146.1 0.0 copy-start.16
  146.1 0.0 copy-done.13
  146.1 0.0 copy-done.14
  146.1 0.0 copy-done.15
  146.1 0.8 copy-done.16
  146.9 0.0 copy-start.1
  146.9 0.0 copy-start.11
  146.9 0.0 copy-start.4
  146.9 0.0 copy-start.9
  146.9 0.0 copy-start.12
  146.9 51.4 %shard_map.226 = (bf16[256,1024]{1,0:T(8,128)(2,1)}, f32[256,1024]{1,0:T(8,128)}, bf16[32,384,128]{2,1,0:T(8,128)(2,1)}, bf16[16,64,256]{2,1,0:T(8,128)(2,1)}) custom-call(s32[8]{0:T(128)} %lens_ref.9, s32[8]{0:T(128)} %choice_ref.5, bf16[16,64,256]{2,1,0:T(8,128)(2,1)} %copy-done.7, bf16[256,1024]{1,0:T(8,128)(2,1)} %tok_ref.3, bf16[256,1024]{1,0:T(8,128)(2,1)} %cot_ref.1, ...), custom_call_target="tpu_custom_call" | custom-call | tf_op jit(solution)/shard_map/pallas_call | solution.py:1278
  198.3 0.0 copy-start.2
  198.3 0.0 copy-start.3
  198.3 0.0 copy-done.1
  198.4 0.0 copy-done.11
  198.4 0.0 copy-start.8
  198.4 1.2 copy-done.8
  199.6 23.3 %shard_map.227 = (bf16[16,64,256]{2,1,0:T(8,128)(2,1)S(1)}, bf16[22,2,64,256]{3,2,1,0:T(8,128)(2,1)S(1)}) custom-call(s32[8]{0:T(128)S(1)} %copy-done.11, bf16[22,3,64,256]{3,2,1,0:T(8,128)(2,1)S(1)} %copy-done.1, bf16[16,64,256]{2,1,0:T(8,128)(2,1)S(1)} %copy-done.8, f32[16,8,256]{2,1,0:T(8,128)S(1)} %get-tuple-element.44.lse_ref, ...), custom_call_target="tpu_custom_call" | custom-call | tf_op jit(solution)/shard_map/pallas_call | solution.py:1969
  222.8 0.0 copy-done.4
  222.8 0.0 copy-done.9
  222.9 0.0 copy-done.12
  222.9 0.0 copy-done.2
  222.9 0.0 copy-done.3
  222.9 0.0 copy-start.5
  222.9 1.2 copy-done.5
  224.1 0.0 copy-start.6
  224.1 63.0 %shard_map.228 = (f32[256,1024]{1,0:T(8,128)S(1)}, f32[384,128]{1,0:T(8,128)S(1)}, f32[3,64,128]{2,1,0:T(8,128)S(1)}) custom-call(s32[8]{0:T(128)S(1)} %copy-done.11, s32[8]{0:T(128)S(1)} %copy-done.12, bf16[16,64,256]{2,1,0:T(8,128)(2,1)S(1)} %get-tuple-element.46.dq_ref, bf16[22,2,64,256]{3,2,1,0:T(8,128)(2,1)S(1)} %get-tuple-element.47.dkv_ref, ...), custom_call_target="tpu_custom_call" | custom-call | tf_op jit(solution)/shard_map/pallas_call | solution.py:1655
  287.1 0.0 copy-done.6
  287.2 1.3 shard_map.229
Async XLA Ops:
  119.0 22.2 %collective-permute-start.2 = (bf16[4,32,2048]{2,1,0:T(8,128)(2,1)}, bf16[4,32,2048]{2,1,0:T(8,128)(2,1)S(1)}, u32[]{:S(2)}, u32[]{:S(2)}) collective-permute-start(bf16[4,32,2048]{2,1,0:T(8,128)(2,1)} %get-tuple-element.40.line_a), channel_id=1, source_target_pairs={{0,8},{1,9},{2,10},{3,11},{4,12},{5,13},{6,14},{7,15},{8,0},{9,1},... | collective-permute-start | bytes 1572872 | tf_op jit(solution)/shard_map/ppermute | solution.py:2044
  120.4 20.8 %collective-permute-start = (bf16[4,32,2048]{2,1,0:T(8,128)(2,1)}, bf16[4,32,2048]{2,1,0:T(8,128)(2,1)S(1)}, u32[]{:S(2)}, u32[]{:S(2)}) collective-permute-start(bf16[4,32,2048]{2,1,0:T(8,128)(2,1)} %get-tuple-element.40.line_a), channel_id=1, source_target_pairs={{0,16},{1,17},{2,18},{3,19},{4,20},{5,21},{6,22},{7,23},{8,24},{9,... | collective-permute-start | bytes 1572872 | tf_op jit(solution)/shard_map/ppermute | solution.py:2044
  120.4 24.6 %collective-permute-start.3 = (bf16[4,32,2048]{2,1,0:T(8,128)(2,1)}, bf16[4,32,2048]{2,1,0:T(8,128)(2,1)S(1)}, u32[]{:S(2)}, u32[]{:S(2)}) collective-permute-start(bf16[4,32,2048]{2,1,0:T(8,128)(2,1)} %get-tuple-element.41.line_b), channel_id=1, source_target_pairs={{0,8},{1,9},{2,10},{3,11},{4,12},{5,13},{6,14},{7,15},{8,0},{9,1},... | collective-permute-start | bytes 1572872 | tf_op jit(solution)/shard_map/ppermute | solution.py:2044
  121.1 25.0 %collective-permute-start.1 = (bf16[4,32,2048]{2,1,0:T(8,128)(2,1)}, bf16[4,32,2048]{2,1,0:T(8,128)(2,1)S(1)}, u32[]{:S(2)}, u32[]{:S(2)}) collective-permute-start(bf16[4,32,2048]{2,1,0:T(8,128)(2,1)} %get-tuple-element.41.line_b), channel_id=1, source_target_pairs={{0,16},{1,17},{2,18},{3,19},{4,20},{5,21},{6,22},{7,23},{8,24},{9,... | collective-permute-start | bytes 1572872 | tf_op jit(solution)/shard_map/ppermute | solution.py:2044
  123.1 1.6 copy-start
  124.7 0.7 copy-start.10
  140.4 0.8 copy-start.7
  141.2 4.9 %copy-start.13 = (bf16[4,32,2048]{2,1,0:T(8,128)(2,1)}, bf16[4,32,2048]{2,1,0:T(8,128)(2,1)S(1)}, u32[]{:S(2)}) copy-start(bf16[4,32,2048]{2,1,0:T(8,128)(2,1)S(1)} %collective-permute-done.2.xa) | copy-start | bytes 1572868
  141.2 4.9 %copy-start.14 = (bf16[4,32,2048]{2,1,0:T(8,128)(2,1)}, bf16[4,32,2048]{2,1,0:T(8,128)(2,1)S(1)}, u32[]{:S(2)}) copy-start(bf16[4,32,2048]{2,1,0:T(8,128)(2,1)S(1)} %collective-permute-done.ya) | copy-start | bytes 1572868
  145.0 1.1 copy-start.15
  146.1 0.8 copy-start.16
  146.9 51.5 %copy-start.1 = (bf16[22,3,64,256]{3,2,1,0:T(8,128)(2,1)S(1)}, bf16[22,3,64,256]{3,2,1,0:T(8,128)(2,1)}, u32[]{:S(2)}) copy-start(bf16[22,3,64,256]{3,2,1,0:T(8,128)(2,1)} %get-tuple-element.35.x_ref) | copy-start | bytes 6488068
  146.9 51.5 %copy-start.11 = (s32[8]{0:T(128)S(1)}, s32[8]{0:T(128)}, u32[]{:S(2)}) copy-start(s32[8]{0:T(128)} %lens_ref.9) | copy-start | bytes 100
  146.9 76.0 %copy-start.4 = (bf16[32,48,128]{2,1,0:T(8,128)(2,1)S(1)}, bf16[32,48,128]{2,1,0:T(8,128)(2,1)}, u32[]{:S(2)}) copy-start(bf16[32,48,128]{2,1,0:T(8,128)(2,1)} %get-tuple-element.38.ve) | copy-start | bytes 1179652
  146.9 76.0 %copy-start.9 = (bf16[3,256,128]{2,1,0:T(8,128)(2,1)S(1)}, bf16[3,256,128]{2,1,0:T(8,128)(2,1)}, u32[]{:S(2)}) copy-start(bf16[3,256,128]{2,1,0:T(8,128)(2,1)} %get-tuple-element.49.rank_ref) | copy-start | bytes 589828
  146.9 76.0 %copy-start.12 = (s32[8]{0:T(128)S(1)}, s32[8]{0:T(128)}, u32[]{:S(2)}) copy-start(s32[8]{0:T(128)} %choice_ref.5) | copy-start | bytes 100
  198.3 24.5 %copy-start.2 = (bf16[256,1024]{1,0:T(8,128)(2,1)S(1)}, bf16[256,1024]{1,0:T(8,128)(2,1)}, u32[]{:S(2)}) copy-start(bf16[256,1024]{1,0:T(8,128)(2,1)} %tok_ref.3) | copy-start | bytes 1572868
  198.3 24.5 %copy-start.3 = (bf16[32,384,128]{2,1,0:T(8,128)(2,1)S(1)}, bf16[32,384,128]{2,1,0:T(8,128)(2,1)}, u32[]{:S(2)}) copy-start(bf16[32,384,128]{2,1,0:T(8,128)(2,1)} %get-tuple-element.50.early_terms) | copy-start | bytes 9437188
  198.4 1.2 copy-start.8
  222.9 1.2 copy-start.5
  224.1 63.0 %copy-start.6 = (bf16[256,1024]{1,0:T(8,128)(2,1)S(1)}, bf16[256,1024]{1,0:T(8,128)(2,1)}, u32[]{:S(2)}) copy-start(bf16[256,1024]{1,0:T(8,128)(2,1)} %get-tuple-element.42.result_in) | copy-start | bytes 1572868
